TPU v7x, 32 devices: a whole 2x2x4 slice. The times are simulated.
32 devices in a mesh: dp: 4 (over y, core), bank: 8 (over z, x).
Axes of the slice: x: 2, y: 2, z: 4, core: 2. Of those that a mesh axis runs over, the one named last changes fastest.
Arguments:
- features: bfloat16 [64, 512, 256], P('dp', 'bank'), may hold values from -6 to 6
- patch_index: int32 [64, 128], P('dp'), may hold values from 0 to 511, as said below
- positive_index: int32 [8192], P('dp'), may hold values from 0 to 32767
- bank: bfloat16 [32768, 256], P('bank'), may hold values from -0.4 to 0.4
Outputs:
- loss: float32 [8192], P(('dp', 'bank'))
- query_grad: float32 [8192, 256], P(('dp', 'bank'))
- mean_loss: float32 [], replicated
Inputs may be any that keep to these rules, and one draw needn't show every extreme that they name: `patch_index`: within one image the sampled positions are distinct.
All inputs are finite; a program needn't handle non-finite values.
Results may differ from a plain program's by a relative error of at most 0.00065.
Values may be sent and summed in bfloat16 or wider, within the bound.
No kernel may reach another device: no remote copies, remote signals or barrier semaphores. Data moves between devices by JAX's collectives and lax.ppermute only.
A program may use at most 64 MiB of HBM per device.

v0:
```python
import math

import jax
import jax.numpy as jnp
from jax import lax
from jax.sharding import PartitionSpec as P

SOFTMAX_TEMP = 0.07
EPSILON = 1e-05


def normalize(values):
    scale = lax.rsqrt(jnp.mean(values * values, axis=-1, keepdims=True) + EPSILON)
    return values * scale / math.sqrt(values.shape[-1])


def on_device(features, patch_index, positive_index, bank):
    groups = lax.axis_size("bank")
    place = lax.axis_index("bank")
    images, hw_dev, channels = features.shape
    queries_dp = images * patch_index.shape[1]
    owned_rows = queries_dp // groups
    local_pos = patch_index - place * hw_dev
    onehot = (local_pos[:, :, None] == jnp.arange(hw_dev, dtype=jnp.int32)[None, None, :]).astype(
        jnp.bfloat16
    )
    picked = jnp.einsum("iph,ihc->ipc", onehot, features, preferred_element_type=jnp.float32)
    term = picked.reshape(queries_dp, channels)
    raw_all = lax.psum(term, "bank")
    query_vector = normalize(raw_all).astype(jnp.bfloat16)
    raw_own = lax.dynamic_slice_in_dim(raw_all, place * owned_rows, owned_rows, 0)
    bank_dev = bank.shape[0]
    block_keys = math.gcd(bank_dev, 512)

    def visit(index, carry):
        exponent_sum, weighted_negatives = carry
        bank_block = lax.dynamic_slice_in_dim(bank, index * block_keys, block_keys, 0)
        logit_scores = (
            lax.dot_general(
                query_vector,
                bank_block,
                (((1,), (1,)), ((), ())),
                preferred_element_type=jnp.float32,
            )
            / SOFTMAX_TEMP
        )
        exponent_terms = jnp.exp(logit_scores - 1.0 / SOFTMAX_TEMP)
        exponent_sum = exponent_sum + jnp.sum(exponent_terms, axis=1)
        weighted_negatives = weighted_negatives + jnp.dot(
            exponent_terms.astype(jnp.bfloat16), bank_block, preferred_element_type=jnp.float32
        )
        return (exponent_sum, weighted_negatives)

    start = (jnp.zeros((queries_dp,), jnp.float32), jnp.zeros((queries_dp, channels), jnp.float32))
    exponent_sum, weighted_negatives = lax.fori_loop(0, bank_dev // block_keys, visit, start)
    key_pos = positive_index - place * bank_dev
    inside = (key_pos >= 0) & (key_pos < bank_dev)
    rows_pos = jnp.clip(key_pos, 0, bank_dev - 1)
    positive_key = bank[rows_pos].astype(jnp.float32) * inside[:, None].astype(jnp.float32)
    matched_logit = jnp.sum(query_vector.astype(jnp.float32) * positive_key, axis=1) / SOFTMAX_TEMP
    local_exponent_sum, local_logit, local_weighted, local_positive = (
        lax.psum_scatter(exponent_sum, "bank", scatter_dimension=0, tiled=True),
        lax.psum_scatter(matched_logit, "bank", scatter_dimension=0, tiled=True),
        lax.psum_scatter(weighted_negatives, "bank", scatter_dimension=0, tiled=True),
        lax.psum_scatter(positive_key, "bank", scatter_dimension=0, tiled=True),
    )
    query_update = (local_weighted / local_exponent_sum[:, None] - local_positive) / SOFTMAX_TEMP
    loss = jnp.log(local_exponent_sum) + 1.0 / SOFTMAX_TEMP - local_logit
    _, pullback = jax.vjp(normalize, raw_own)
    query_grad = pullback(query_update)[0]
    count_all = queries_dp * lax.axis_size("dp")
    mean_loss = lax.psum(jnp.sum(loss), ("dp", "bank")) / count_all
    return (loss, query_grad, mean_loss)


def solution(mesh):
    in_specs = (P("dp", "bank", None), P("dp", None), P("dp"), P("bank", None))
    out_specs = (P(("dp", "bank")), P(("dp", "bank"), None), P())
    return jax.shard_map(
        on_device, mesh=mesh, in_specs=in_specs, out_specs=out_specs, check_vma=False
    )
```

profile of v0, /device:TPU:0, one launch (start us, length us, event | category | flops | bytes accessed | tf_op | source)
XLA Modules:
  0.0 271.1 jit_solution(9167001712626896373)
XLA Ops:
  7.2 0.0 copy-start
  7.2 0.0 all-reduce.5.cloned.1.call-start
  7.2 0.7 broadcast_subtract_fusion
  8.0 0.2 copy-done
  8.2 0.0 copy-start.3
  8.2 1.8 fusion.12
  10.0 0.0 all-reduce.5.cloned.1.call-update
  10.0 0.0 reduce-scatter.5.cloned.1.call-start
  10.1 0.0 copy-done.3
  10.1 10.3 %gather_fusion = bf16[2048,256]{1,0:T(8,128)(2,1)} fusion(bf16[4096,256]{1,0:T(8,128)(2,1)} %param.9, s32[2048]{0:T(1024)S(1)} %fusion.14), kind=kCustom, calls=%fused_computation | custom fusion | bytes 2105344 | tf_op jit(solution)/shard_map/gather | solution.py:59
  20.5 95.7 %all-reduce.5.cloned.1.call-done = f32[2048,256]{1,0:T(8,128)} async-done(((f32[2048,256]{1,0:T(8,128)}), f32[2048,256]{1,0:T(8,128)}) %all-reduce.5.cloned.1.call-update) | async-done | bytes 2097168 | tf_op jit(solution)/shard_map/psum | solution.py:29
  116.2 0.0 copy-start.2
  116.2 2.1 multiply_reduce_fusion.1
  118.3 0.1 copy-done.2
  118.4 3.2 %multiply_reduce_fusion = (f32[2048]{0:T(1024)S(1)}, bf16[2048,256]{1,0:T(8,128)(2,1)}, f32[2048,256]{1,0:T(8,128)}) fusion(f32[2048]{0:T(1024)S(1)} %and_convert_fusion, bf16[2048,256]{1,0:T(8,128)(2,1)} %gather_fusion, f32[2048,256]{1,0:T(8,128)S(1)} %copy-done.2, f32[2048]{0:T(1024)S(1)} %add_rsqrt_fusion), kind=kLoop, calls=%fused_computation.15 | loop fusion | flops 4192256 | bytes 6316032 | tf_op jit(solution)/shard_map/reduce_sum | solution.py:60
  121.6 0.0 reduce-scatter.5.cloned.1.call-update
  121.6 0.0 reduce-scatter.3.cloned.1.call-start
  121.7 42.6 %while.18 = (s32[]{:T(128)}, f32[2048]{0:T(1024)S(1)}, f32[2048,256]{1,0:T(8,128)S(1)}, bf16[4096,256]{1,0:T(8,128)(2,1)}, bf16[2048,256]{1,0:T(8,128)(2,1)}, /*index=5*/s32[]{:T(128)}, s32[]{:T(128)}, s32[]{:T(128)}, s32[]{:T(128)}) while((s32[]{:T(128)}, f32[2048]{0:T(1024)S(1)}, f32[2048,256]{1,0:T(8,128)S(1)}, ...), condition=%wide.region_4.0_spmd.clone, body=%wide.region_2.0_spmd.clone.sunk | while | flops 1081083904 | bytes 14188710 | solution.py:55
  121.7 2.4 fusion.28
  124.1 2.8 %convolution_add_fusion.2 = f32[2048,256]{1,0:T(8,128)S(1)} fusion(f32[512,2048]{1,0:T(8,128)S(1)} %get-tuple-element.214, f32[2048,256]{1,0:T(8,128)S(1)} %get-tuple-element.226, pred[]{:T(512)S(6)} %compare.3, bf16[4096,256]{1,0:T(8,128)(2,1)} %get-tuple-element.236, s32[]{:T(128)S(6)} %select_n.23), kind=kOutput, calls=%fused_computation.4.clone.1 | convolution fusion | flops 541065216 | bytes 8650757 | tf_op jit(solution)/shard_map/while/body/eval_jaxpr/dot_general | solution.py:49
  127.0 2.4 fusion.28
  129.5 2.8 %convolution_add_fusion.2 = f32[2048,256]{1,0:T(8,128)S(1)} fusion(f32[512,2048]{1,0:T(8,128)S(1)} %get-tuple-element.214, f32[2048,256]{1,0:T(8,128)S(1)} %get-tuple-element.226, pred[]{:T(512)S(6)} %compare.3, bf16[4096,256]{1,0:T(8,128)(2,1)} %get-tuple-element.236, s32[]{:T(128)S(6)} %select_n.23), kind=kOutput, calls=%fused_computation.4.clone.1 | convolution fusion | flops 541065216 | bytes 8650757 | tf_op jit(solution)/shard_map/while/body/eval_jaxpr/dot_general | solution.py:49
  132.3 2.4 fusion.28
  134.8 2.8 %convolution_add_fusion.2 = f32[2048,256]{1,0:T(8,128)S(1)} fusion(f32[512,2048]{1,0:T(8,128)S(1)} %get-tuple-element.214, f32[2048,256]{1,0:T(8,128)S(1)} %get-tuple-element.226, pred[]{:T(512)S(6)} %compare.3, bf16[4096,256]{1,0:T(8,128)(2,1)} %get-tuple-element.236, s32[]{:T(128)S(6)} %select_n.23), kind=kOutput, calls=%fused_computation.4.clone.1 | convolution fusion | flops 541065216 | bytes 8650757 | tf_op jit(solution)/shard_map/while/body/eval_jaxpr/dot_general | solution.py:49
  137.6 2.5 fusion.28
  140.1 2.8 %convolution_add_fusion.2 = f32[2048,256]{1,0:T(8,128)S(1)} fusion(f32[512,2048]{1,0:T(8,128)S(1)} %get-tuple-element.214, f32[2048,256]{1,0:T(8,128)S(1)} %get-tuple-element.226, pred[]{:T(512)S(6)} %compare.3, bf16[4096,256]{1,0:T(8,128)(2,1)} %get-tuple-element.236, s32[]{:T(128)S(6)} %select_n.23), kind=kOutput, calls=%fused_computation.4.clone.1 | convolution fusion | flops 541065216 | bytes 8650757 | tf_op jit(solution)/shard_map/while/body/eval_jaxpr/dot_general | solution.py:49
  142.9 2.5 fusion.28
  145.4 2.8 %convolution_add_fusion.2 = f32[2048,256]{1,0:T(8,128)S(1)} fusion(f32[512,2048]{1,0:T(8,128)S(1)} %get-tuple-element.214, f32[2048,256]{1,0:T(8,128)S(1)} %get-tuple-element.226, pred[]{:T(512)S(6)} %compare.3, bf16[4096,256]{1,0:T(8,128)(2,1)} %get-tuple-element.236, s32[]{:T(128)S(6)} %select_n.23), kind=kOutput, calls=%fused_computation.4.clone.1 | convolution fusion | flops 541065216 | bytes 8650757 | tf_op jit(solution)/shard_map/while/body/eval_jaxpr/dot_general | solution.py:49
  148.3 2.4 fusion.28
  150.8 2.8 %convolution_add_fusion.2 = f32[2048,256]{1,0:T(8,128)S(1)} fusion(f32[512,2048]{1,0:T(8,128)S(1)} %get-tuple-element.214, f32[2048,256]{1,0:T(8,128)S(1)} %get-tuple-element.226, pred[]{:T(512)S(6)} %compare.3, bf16[4096,256]{1,0:T(8,128)(2,1)} %get-tuple-element.236, s32[]{:T(128)S(6)} %select_n.23), kind=kOutput, calls=%fused_computation.4.clone.1 | convolution fusion | flops 541065216 | bytes 8650757 | tf_op jit(solution)/shard_map/while/body/eval_jaxpr/dot_general | solution.py:49
  153.6 2.5 fusion.28
  156.1 2.8 %convolution_add_fusion.2 = f32[2048,256]{1,0:T(8,128)S(1)} fusion(f32[512,2048]{1,0:T(8,128)S(1)} %get-tuple-element.214, f32[2048,256]{1,0:T(8,128)S(1)} %get-tuple-element.226, pred[]{:T(512)S(6)} %compare.3, bf16[4096,256]{1,0:T(8,128)(2,1)} %get-tuple-element.236, s32[]{:T(128)S(6)} %select_n.23), kind=kOutput, calls=%fused_computation.4.clone.1 | convolution fusion | flops 541065216 | bytes 8650757 | tf_op jit(solution)/shard_map/while/body/eval_jaxpr/dot_general | solution.py:49
  159.0 2.4 fusion.28
  161.4 2.8 %convolution_add_fusion.2 = f32[2048,256]{1,0:T(8,128)S(1)} fusion(f32[512,2048]{1,0:T(8,128)S(1)} %get-tuple-element.214, f32[2048,256]{1,0:T(8,128)S(1)} %get-tuple-element.226, pred[]{:T(512)S(6)} %compare.3, bf16[4096,256]{1,0:T(8,128)(2,1)} %get-tuple-element.236, s32[]{:T(128)S(6)} %select_n.23), kind=kOutput, calls=%fused_computation.4.clone.1 | convolution fusion | flops 541065216 | bytes 8650757 | tf_op jit(solution)/shard_map/while/body/eval_jaxpr/dot_general | solution.py:49
  164.3 0.0 copy-start.1
  164.3 0.0 copy-start.4
  164.3 1.3 copy-done.1
  165.6 0.0 reduce-scatter.3.cloned.1.call-update
  165.7 0.0 copy-done.4
  165.7 0.6 dynamic-slice
  166.9 36.3 %all-reduce.2 = (f32[2048]{0:T(1024)S(1)}, f32[2048]{0:T(1024)S(1)}) all-reduce(f32[2048]{0:T(1024)S(1)} %broadcast_multiply_fusion, f32[2048]{0:T(1024)S(1)} %get-tuple-element.136), channel_id=3, replica_groups=mesh['dp'=4,'bank'=8] {'bank'}, use_global_device_ids=true, to_apply=%region_7.8.clone | all-reduce | flops 4096 | bytes 32768
  203.2 1.2 fusion.18
  204.5 37.3 %psum.15 = f32[]{:T(128)} all-reduce(f32[]{:T(128)} %get-tuple-element.170), channel_id=1, replica_groups=mesh['dp'=4,'bank'=8] {'dp','bank'}, use_global_device_ids=true, to_apply=%region_13.14 | all-reduce | flops 1 | bytes 8 | tf_op jit(solution)/shard_map/psum | solution.py:72
  242.4 0.0 reduce-scatter.5.cloned.1.call-done
  242.5 17.7 %reduce-scatter.3.cloned.1.call-done = f32[256,256]{1,0:T(8,128)} async-done(((f32[2048,256]{1,0:T(8,128)}), f32[256,256]{1,0:T(8,128)}) %reduce-scatter.3.cloned.1.call-update) | async-done | bytes 262160 | tf_op jit(solution)/shard_map/reduce_scatter | solution.py:64
  260.2 1.3 multiply_reduce_fusion.3
  261.5 2.0 add_add_fusion
  (15 shorter events, 0.1 us)
Async XLA Ops:
  7.2 1.1 copy-start
  7.2 109.0 %all-reduce.5.cloned.1.call-start = ((), (), s32[]{:S(2)}) async-start(), calls=%async_computation.2 | async-start | bytes 4194304 | tf_op jit(solution)/shard_map/psum | solution.py:29
  8.2 1.9 copy-start.3
  10.0 232.4 %reduce-scatter.5.cloned.1.call-start = ((), (), s32[]{:S(2)}) async-start(), calls=%async_computation.4 | async-start | bytes 2359296 | tf_op jit(solution)/shard_map/reduce_scatter | solution.py:65
  116.2 2.2 copy-start.2
  121.6 138.5 %reduce-scatter.3.cloned.1.call-start = ((), (), s32[]{:S(2)}) async-start(), calls=%async_computation.3 | async-start | bytes 2359296 | tf_op jit(solution)/shard_map/reduce_scatter | solution.py:64
  164.3 1.3 copy-start.1
  164.3 1.4 copy-start.4
Sparse Core Ops, SparseCore 0:
  11.6 104.5 all-reduce.4
  121.7 67.7 reduce-scatter.4
  193.1 66.9 reduce-scatter.2
where the time goes:
time: 272 us; the launch traced here: 271 us
  waiting for transfers between devices  114 us (42%)
  blocking collectives  73.6 us (27%)
  matrix products  44 us (16%)
  between operations  16.3 us (6%)
  local copies, waits for them, and re-layouts  12.6 us (5%)
  other arithmetic  10.6 us (4%)
    psum x1, waiting for transfers between devices, on_device(): raw_all = lax.psum(term, 'bank')  95.7 us
    psum x1, blocking collectives, on_device(): mean_loss = lax.psum(jnp.sum(loss), ('dp', 'bank')) / count_all  37.3 us
    unnamed x1, blocking collectives  36.3 us
    dot_general x8, matrix products, visit(): jnp.dot(exponent_terms.astype(jnp.bfloat16), bank_block, preferred_elemen...  22.7 us
    dot_general x8, matrix products, visit(): lax.dot_general(query_vector, bank_block, (((1,), (1,)), ((), ())), prefe...  19.6 us
    reduce_scatter x1, waiting for transfers between devices, on_device(): lax.psum_scatter(weighted_negatives, 'bank', scatter_dimension=0, tiled=T...  17.7 us
    gather x1, local copies, waits for them, and re-layouts, on_device(): bank[rows_pos].astype(jnp.float32) * inside[:, None].astype(jnp.float32)  10.3 us
  transfers between devices with their start and end apart: 3, of which 2 were waited for; matrix products, arithmetic and copies ran while one was open for 20% of the time, Pallas kernels for 0%

commit v1 on v0

v1 whole, which is shorter than its diff:
```python
import functools
import math

import jax
import jax.numpy as jnp
from jax import lax
from jax.experimental import pallas as pl
from jax.experimental.pallas import tpu as pltpu
from jax.sharding import PartitionSpec as P

SOFTMAX_TEMP = 0.07
EPSILON = 1e-05
INV_TEMP = 1.0 / SOFTMAX_TEMP
STEPS = 32767.0
F32 = jnp.float32
BF16 = jnp.bfloat16
NT = (((1,), (1,)), ((), ()))
ROOM = pltpu.CompilerParams(vmem_limit_bytes=48 << 20)


def normalize(values):
    scale = lax.rsqrt(jnp.mean(values * values, axis=-1, keepdims=True) + EPSILON)
    return values * scale / math.sqrt(values.shape[-1])


def plain(features, patch_index, positive_index, bank):
    groups = lax.axis_size("bank")
    place = lax.axis_index("bank")
    images, hw_dev, channels = features.shape
    queries_dp = images * patch_index.shape[1]
    owned_rows = queries_dp // groups
    local_pos = patch_index - place * hw_dev
    onehot = (local_pos[:, :, None] == jnp.arange(hw_dev, dtype=jnp.int32)[None, None, :]).astype(BF16)
    picked = jnp.einsum("iph,ihc->ipc", onehot, features, preferred_element_type=F32)
    raw_all = lax.psum(picked.reshape(queries_dp, channels), "bank")
    query_vector = normalize(raw_all).astype(BF16)
    raw_own = lax.dynamic_slice_in_dim(raw_all, place * owned_rows, owned_rows, 0)
    bank_dev = bank.shape[0]
    block_keys = math.gcd(bank_dev, 512)

    def visit(index, carry):
        exponent_sum, weighted = carry
        block = lax.dynamic_slice_in_dim(bank, index * block_keys, block_keys, 0)
        logit = lax.dot_general(query_vector, block, NT, preferred_element_type=F32) / SOFTMAX_TEMP
        terms = jnp.exp(logit - INV_TEMP)
        exponent_sum = exponent_sum + jnp.sum(terms, axis=1)
        weighted = weighted + jnp.dot(terms.astype(BF16), block, preferred_element_type=F32)
        return (exponent_sum, weighted)

    start = (jnp.zeros((queries_dp,), F32), jnp.zeros((queries_dp, channels), F32))
    exponent_sum, weighted = lax.fori_loop(0, bank_dev // block_keys, visit, start)
    key_pos = positive_index - place * bank_dev
    inside = (key_pos >= 0) & (key_pos < bank_dev)
    rows_pos = jnp.clip(key_pos, 0, bank_dev - 1)
    positive_key = bank[rows_pos].astype(F32) * inside[:, None].astype(F32)
    matched = jnp.sum(query_vector.astype(F32) * positive_key, axis=1) / SOFTMAX_TEMP
    own_sum, own_logit, own_weighted, own_positive = (
        lax.psum_scatter(v, "bank", scatter_dimension=0, tiled=True)
        for v in (exponent_sum, matched, weighted, positive_key)
    )
    step = (own_weighted / own_sum[:, None] - own_positive) / SOFTMAX_TEMP
    loss = jnp.log(own_sum) + INV_TEMP - own_logit
    _, pullback = jax.vjp(normalize, raw_own)
    query_grad = pullback(step)[0]
    count_all = queries_dp * lax.axis_size("dp")
    mean_loss = lax.psum(jnp.sum(loss), ("dp", "bank")) / count_all
    return (loss, query_grad, mean_loss)


def capacity(mean, least, sigmas):
    room = mean + sigmas * math.sqrt(mean)
    return min(least, -(-int(math.ceil(room)) // 16) * 16)


def pick_kernel(groups, owned, cap, place_ref, pos_ref, feat_ref, own_ref, other_ref, loc_ref, most_ref):
    place = place_ref[0]
    images, patches = pos_ref.shape
    hw = feat_ref.shape[1]
    pos = pos_ref[...]
    holder = pos // hw
    row = lax.broadcasted_iota(jnp.int32, pos.shape, 0) * patches + lax.broadcasted_iota(jnp.int32, pos.shape, 1)
    parity = (row // owned) % 2
    code = holder * 2 + parity
    up = lax.broadcasted_iota(jnp.int32, (patches, patches), 0) <= lax.broadcasted_iota(
        jnp.int32, (patches, patches), 1
    )
    up = up.astype(F32).astype(BF16)
    low = lax.broadcasted_iota(jnp.int32, (images, images), 0) > lax.broadcasted_iota(
        jnp.int32, (images, images), 1
    )
    low = low.astype(F32).astype(BF16)
    ones = jnp.ones((patches, patches), BF16)
    rank = jnp.full(pos.shape, -1.0, F32)
    most = jnp.zeros((1, patches), F32)
    for g in range(2 * groups):
        hit = (code == g).astype(F32)
        mask = hit.astype(BF16)
        prefix = jnp.dot(mask, up, preferred_element_type=F32)
        count = jnp.dot(mask, ones, preferred_element_type=F32)
        before = jnp.dot(low, count.astype(BF16), preferred_element_type=F32)
        rank = rank + hit * (prefix + before)
        most = jnp.maximum(most, jnp.sum(count, axis=0, keepdims=True))
    most_ref[...] = jnp.broadcast_to(most, most_ref.shape)
    inner = place % 2
    outer = place // 2
    turns = groups // 2
    away = (outer - holder // 2 + turns) % turns
    side = (holder % 2 + inner) % 2
    ranks = rank.astype(jnp.int32)
    loc_ref[...] = (away * 2 + side) * cap + ranks
    local = pos - place * hw
    mine = holder == place
    slot = ranks + jnp.where(parity == inner, 0, cap)
    slot = jnp.where(mine & (ranks < cap), slot, -1)
    total = jnp.zeros((2 * cap, feat_ref.shape[2]), F32)
    where_slot = lax.broadcasted_iota(jnp.int32, (2 * cap, patches), 0)
    where_pos = lax.broadcasted_iota(jnp.int32, (hw, patches), 0)
    for i in range(images):
        chosen = (where_slot == slot[i : i + 1, :]).astype(F32).astype(BF16)
        spots = (where_pos == local[i : i + 1, :]).astype(F32).astype(BF16)
        table = lax.dot_general(chosen, spots, NT, preferred_element_type=F32)
        total = total + jnp.dot(table.astype(BF16), feat_ref[i], preferred_element_type=F32)
    own_ref[...] = total[:cap].astype(BF16)
    other_ref[...] = total[cap:].astype(BF16)


def pick(features, patch_index, place, groups, owned, cap):
    images, patches = patch_index.shape
    channels = features.shape[2]
    return pl.pallas_call(
        functools.partial(pick_kernel, groups, owned, cap),
        in_specs=[
            pl.BlockSpec(memory_space=pltpu.SMEM),
            pl.BlockSpec(memory_space=pltpu.VMEM),
            pl.BlockSpec(memory_space=pltpu.VMEM),
        ],
        out_specs=[pl.BlockSpec(memory_space=pltpu.VMEM)] * 4,
        out_shape=[
            jax.ShapeDtypeStruct((cap, channels), BF16),
            jax.ShapeDtypeStruct((cap, channels), BF16),
            jax.ShapeDtypeStruct((images, patches), jnp.int32),
            jax.ShapeDtypeStruct((8, patches), F32),
        ],
        compiler_params=ROOM,
        cost_estimate=pl.CostEstimate(flops=10**9, bytes_accessed=10**6, transcendentals=0),
        name="pick",
    )(place.reshape(1), patch_index, features)


def arrange_kernel(cap, loc_ref, *refs):
    query_ref, raw_ref = refs[-2:]
    rows = loc_ref.shape[0]
    loc = loc_ref[...]
    lane = lax.broadcasted_iota(jnp.int32, (rows, cap), 1)
    raw = jnp.zeros(query_ref.shape, F32)
    for b, ref in enumerate(refs[:-2]):
        table = (lane + b * cap == loc).astype(F32).astype(BF16)
        raw = raw + jnp.dot(table, ref[...], preferred_element_type=F32)
    raw_ref[...] = raw.astype(BF16)
    query_ref[...] = normalize(raw).astype(BF16)


def arrange(loc, parts, cap):
    rows = loc.shape[0]
    channels = parts[0].shape[1]
    block = math.gcd(rows, 256)
    whole = pl.BlockSpec((cap, channels), lambda i: (0, 0))
    tall = pl.BlockSpec((block, channels), lambda i: (i, 0))
    return pl.pallas_call(
        functools.partial(arrange_kernel, cap),
        grid=(rows // block,),
        in_specs=[pl.BlockSpec((block, 1), lambda i: (i, 0))] + [whole] * len(parts),
        out_specs=[tall, tall],
        out_shape=[jax.ShapeDtypeStruct((rows, channels), BF16)] * 2,
        compiler_params=ROOM,
        cost_estimate=pl.CostEstimate(
            flops=2 * rows * cap * len(parts) * channels, bytes_accessed=3 * rows * channels, transcendentals=0
        ),
        name="arrange",
    )(loc, *parts)


def sweep(query, keys, sub, total, pushed):
    for at in range(0, keys.shape[0], sub):
        block = keys[at : at + sub, :]
        logit = lax.dot_general(query, block, NT, preferred_element_type=F32)
        terms = jnp.exp(logit * INV_TEMP - INV_TEMP)
        for c in range(0, sub, 128):
            total = total + terms[:, c : c + 128]
        pushed = pushed + jnp.dot(terms.astype(BF16), block, preferred_element_type=F32)
    return total, pushed


def first_kernel(sub, query_ref, keys_ref, total_ref, pushed_ref):
    total, pushed = sweep(
        query_ref[...], keys_ref, sub, jnp.zeros(total_ref.shape, F32), jnp.zeros(pushed_ref.shape, F32)
    )
    total_ref[...] = total
    pushed_ref[...] = pushed


def flash_cost(rows, keys, channels):
    return pl.CostEstimate(
        flops=4 * rows * keys * channels, bytes_accessed=2 * (rows + keys) * channels, transcendentals=rows * keys
    )


def first(query, keys):
    rows, channels = query.shape
    return pl.pallas_call(
        functools.partial(first_kernel, math.gcd(keys.shape[0], 256)),
        in_specs=[pl.BlockSpec(memory_space=pltpu.VMEM)] * 2,
        out_specs=[pl.BlockSpec(memory_space=pltpu.VMEM)] * 2,
        out_shape=[jax.ShapeDtypeStruct((rows, 128), F32), jax.ShapeDtypeStruct((rows, channels), F32)],
        compiler_params=ROOM,
        cost_estimate=flash_cost(rows, keys.shape[0], channels),
        name="first",
    )(query, keys)


def last_kernel(count, coded, query_ref, total_in, pushed_in, *refs):
    key_refs = refs[:count]
    pushed_ref, stats_ref = refs[count:]
    query = query_ref[...]
    total, pushed = total_in[...], pushed_in[...]
    for ref in key_refs:
        total, pushed = sweep(query, ref, math.gcd(ref.shape[0], 256), total, pushed)
    stats_ref[0:1, :] = jnp.sum(total.T, axis=0, keepdims=True)
    if not coded:
        pushed_ref[...] = pushed
        stats_ref[1:2, :] = jnp.zeros((1, stats_ref.shape[1]), F32)
        return
    size = jnp.abs(pushed)
    wide = size[:, :128]
    for c in range(128, size.shape[1], 128):
        wide = jnp.maximum(wide, size[:, c : c + 128])
    top = jnp.maximum(jnp.max(wide, axis=1, keepdims=True), 1e-30)
    stats_ref[1:2, :] = jnp.maximum(jnp.max(wide.T, axis=0, keepdims=True), 1e-30)
    pushed_ref[...] = jnp.round(pushed * (STEPS / top)).astype(jnp.int32).astype(jnp.int16)


def last(query, total, pushed, keys, start, rows, coded):
    channels = query.shape[1]
    at = start // rows
    part = lambda width: pl.BlockSpec((rows, width), lambda i: (at, 0))
    return pl.pallas_call(
        functools.partial(last_kernel, len(keys), coded),
        grid=(1,),
        in_specs=[part(channels), part(128), part(channels)]
        + [pl.BlockSpec(k.shape, lambda i: (0, 0)) for k in keys],
        out_specs=[pl.BlockSpec((rows, channels), lambda i: (0, 0)), pl.BlockSpec((2, rows), lambda i: (0, 0))],
        out_shape=[
            jax.ShapeDtypeStruct((rows, channels), jnp.int16 if coded else F32),
            jax.ShapeDtypeStruct((2, rows), F32),
        ],
        compiler_params=ROOM,
        cost_estimate=flash_cost(rows, sum(k.shape[0] for k in keys), channels),
        name="last",
    )(query, total, pushed, *keys)


def finish_kernel(count, raw_ref, positive_ref, own_ref, stats_ref, *refs):
    grad_ref = refs[-1]
    rows = raw_ref.shape[0]
    turned = jnp.concatenate(
        [stats_ref[...], jnp.zeros((128 - stats_ref.shape[0], rows), F32)], axis=0
    ).T
    pushed = own_ref[...]
    for j in range(count):
        pushed = pushed + refs[j][...].astype(jnp.int32).astype(F32) * (turned[:, j + 1 : j + 2] * (1.0 / STEPS))
    step = (pushed / turned[:, 0:1] - positive_ref[...].astype(F32)) * INV_TEMP
    raw = raw_ref[...].astype(F32)
    scale = lax.rsqrt(jnp.mean(raw * raw, axis=-1, keepdims=True) + EPSILON)
    inner = jnp.mean(step * raw, axis=-1, keepdims=True)
    grad_ref[...] = (step - raw * (scale * scale * inner)) * (scale / math.sqrt(raw.shape[1]))


def finish(raw, positive, own, stats, parts):
    return pl.pallas_call(
        functools.partial(finish_kernel, len(parts)),
        in_specs=[pl.BlockSpec(memory_space=pltpu.VMEM)] * (4 + len(parts)),
        out_specs=pl.BlockSpec(memory_space=pltpu.VMEM),
        out_shape=jax.ShapeDtypeStruct(own.shape, F32),
        compiler_params=ROOM,
        name="finish",
    )(raw, positive, own, stats, *parts)


def on_device(features, patch_index, positive_index, bank):
    groups, copies = lax.axis_size("bank"), lax.axis_size("dp")
    place = lax.axis_index("bank")
    core = lax.axis_index("dp") % 2
    images, hw_dev, channels = features.shape
    queries_dp = images * patch_index.shape[1]
    owned = queries_dp // groups
    turns = groups // 2
    inner, outer = place % 2, place // 2
    bank_dev = bank.shape[0]
    across = [(b, b ^ 1) for b in range(groups)]
    swap = [(c, c ^ 1) for c in range(copies)]

    def turn(value, k):
        pairs = [(b, ((b // 2 + k) % turns) * 2 + b % 2) for b in range(groups)]
        return lax.ppermute(value, "bank", pairs)

    half = bank_dev // 2
    part = math.gcd(half, 1024)
    far_keys = []
    for at in range(0, half, part):
        sent = lax.dynamic_slice_in_dim(bank, core * half + at, part, 0)
        got = lax.ppermute(sent, "bank", across)
        far_keys += [got, lax.ppermute(got, "dp", swap)]

    cap = capacity(queries_dp / groups / 2, queries_dp // 2, 4.0)
    own_set, other_set, loc, most = pick(features, patch_index, place, groups, owned, cap)
    from_side = lax.ppermute(other_set, "bank", across)
    parts = [own_set, from_side]
    for k in range(1, turns):
        parts += [turn(own_set, k), turn(from_side, k)]
    loc = lax.dynamic_index_in_dim(loc.reshape(turns, 2, owned), inner, 1, keepdims=False)
    loc = lax.dynamic_slice_in_dim(jnp.concatenate([loc, loc]), outer, turns, 0)
    query, raw = arrange(loc.reshape(turns * owned, 1), parts, cap)

    cap_pos = capacity(owned / groups, owned, 5.5)
    index = positive_index.reshape(groups, owned)
    holder = index // bank_dev
    mine = holder == place
    order = jnp.arange(owned, dtype=jnp.int32)
    earlier = order[None, :] < order[:, None]
    rank = jnp.sum((mine[:, None, :] & earlier).astype(jnp.int32), axis=2)
    slots = jnp.arange(cap_pos, dtype=jnp.int32)
    chosen = mine[:, None, :] & (rank[:, None, :] == slots[None, :, None])
    listed = jnp.sum(jnp.where(chosen, (index - place * bank_dev)[:, None, :], 0), axis=2)
    rows_out = bank[listed.reshape(-1)].reshape(turns, 2, cap_pos, channels)
    to_me = lax.dynamic_index_in_dim(rows_out, inner, 1, keepdims=False)
    to_side = lax.dynamic_index_in_dim(rows_out, 1 - inner, 1, keepdims=False)
    side_rows = lax.ppermute(to_side, "bank", across)
    both = jnp.stack([to_me, side_rows], axis=1)
    both = lax.dynamic_slice_in_dim(jnp.concatenate([both, both]), outer, turns, 0)
    landed = jnp.stack([both[0]] + [turn(both[k], k) for k in range(1, turns)])
    landed = landed.reshape(groups * cap_pos, channels)
    own_holder = lax.dynamic_index_in_dim(holder, place, 0, keepdims=False)
    same = own_holder[None, :] == own_holder[:, None]
    own_rank = jnp.sum((same & earlier).astype(jnp.int32), axis=1)
    away = (outer - own_holder // 2 + turns) % turns
    spot = (away * 2 + (own_holder + inner) % 2) * cap_pos + own_rank
    table = (spot[:, None] == jnp.arange(groups * cap_pos, dtype=jnp.int32)[None, :]).astype(BF16)
    positive = jnp.dot(table, landed, preferred_element_type=F32)
    matched = jnp.sum(query[:owned].astype(F32) * positive, axis=1) / SOFTMAX_TEMP

    held = jnp.sum((holder[:, None, :] == jnp.arange(groups, dtype=jnp.int32)[None, :, None]).astype(jnp.int32), axis=2)
    over = (jnp.max(most) > cap) | (jnp.max(held) > cap_pos)

    total, pushed = first(query, bank)
    sent, stats = [None] * turns, [None] * turns
    moved = []
    for k in list(range(1, turns)) + [0]:
        sent[k], stats[k] = last(query, total, pushed, far_keys, k * owned, owned, k > 0)
        if k:
            moved.append(turn(sent[k], k))
    note = jnp.concatenate(
        [s[0:1] for s in stats] + [s[1:2] for s in stats] + [jnp.full((1, owned), jnp.sum(matched))]
    )
    totals = note[:turns]
    matched_line = note[2 * turns, 0]
    sizes = []
    for k in range(1, turns):
        came = turn(note, k)
        totals = totals + jnp.roll(came[:turns], -k, axis=0)
        sizes.append(came[turns + k][None])
        matched_line = matched_line + came[2 * turns, 0]
    grad = finish(raw[:owned], positive, sent[0], jnp.concatenate([totals[:1]] + sizes), moved)
    loss = jnp.log(totals[0]) + INV_TEMP - matched

    line = jnp.sum(jnp.log(totals)) + INV_TEMP * totals.size - matched_line
    word = jnp.stack([jnp.full((128,), line), jnp.full((128,), over.astype(F32))])
    everyone = word
    for a in range(copies):
        for b in range(2):
            if a or b:
                pairs = [
                    (c * groups + p, ((c + a) % copies) * groups + (p ^ b))
                    for c in range(copies)
                    for p in range(groups)
                ]
                everyone = everyone + lax.ppermute(word, ("dp", "bank"), pairs)
    mean_loss = everyone[0, 0] / (queries_dp * copies)
    return lax.cond(
        everyone[1, 0] > 0.5,
        lambda *a: plain(*a[:4]),
        lambda *a: a[4:],
        features,
        patch_index,
        positive_index,
        bank,
        loss,
        grad,
        mean_loss,
    )


def solution(mesh):
    in_specs = (P("dp", "bank", None), P("dp", None), P("dp"), P("bank", None))
    out_specs = (P(("dp", "bank")), P(("dp", "bank"), None), P())
    paired = mesh.shape["bank"] % 2 == 0 and mesh.shape["dp"] % 2 == 0
    return jax.shard_map(
        on_device if paired else plain, mesh=mesh, in_specs=in_specs, out_specs=out_specs, check_vma=False
    )
```

time: 272 us -> 123 us (0.45)
  waiting for transfers between devices: 114 us -> 21.4 us
  blocking collectives: 73.6 us -> 0 us
  matrix products: 44 us -> 0.36 us
  starting transfers between devices: 0.12 us -> 31.9 us
  Pallas kernels: 0 us -> 20.7 us
  local copies, waits for them, and re-layouts: 12.6 us -> 19.4 us
  between operations: 16.3 us -> 20.8 us
  other arithmetic: 10.6 us -> 7.01 us
    psum x1 -> x0, waiting for transfers between devices: 95.7 us -> none  [on_device(): raw_all = lax.psum(term, 'bank')]
    dot_general x17 -> x1, matrix products: 44 us -> 0.36 us  [on_device(): positive = jnp.dot(table, landed, preferred_element_type=F32)]
    psum x1 -> x0, blocking collectives: 37.3 us -> none  [on_device(): mean_loss = lax.psum(jnp.sum(loss), ('dp', 'bank')) / count_all]
    unnamed x1 -> x0, blocking collectives: 36.3 us -> none
    ppermute x0 -> x28, starting transfers between devices: none -> 31.9 us  [the longest x15 20.3 us: turn(): return lax.ppermute(value, 'bank', pairs)]
    ppermute x0 -> x28, waiting for transfers between devices: none -> 21.4 us  [the longest x15 18.2 us: turn(): return lax.ppermute(value, 'bank', pairs)]
    pallas_call x0 -> x8, Pallas kernels: none -> 20.7 us  [the longest x4 7.77 us: last(): pl.pallas_call(functools.partial(last_kernel, len(keys), coded), grid=(1,...]
    reduce_scatter x2 -> x0, waiting for transfers between devices: 17.7 us -> none  [the longest x1 17.7 us: on_device(): lax.psum_scatter(weighted_negatives, 'bank', scatter_dimension=0, tiled=T...]
  transfers between devices with their start and end apart: 3 -> 28, of which waited for: 2 -> 7; matrix products, arithmetic and copies ran while one was open for 20% -> 12% of each run, Pallas kernels for 0% -> 7%
where the time goes in v1:
time: 123 us; the launch traced here: 122 us
  starting transfers between devices  31.9 us (26%)
  waiting for transfers between devices  21.4 us (17%)
  between operations  20.8 us (17%)
  Pallas kernels  20.7 us (17%)
  local copies, waits for them, and re-layouts  19.4 us (16%)
  other arithmetic  7.01 us (6%)
    ppermute x15, starting transfers between devices, turn(): return lax.ppermute(value, 'bank', pairs)  20.3 us
    ppermute x15, waiting for transfers between devices, turn(): return lax.ppermute(value, 'bank', pairs)  18.2 us
    pallas_call x4, Pallas kernels, last(): pl.pallas_call(functools.partial(last_kernel, len(keys), coded), grid=(1,...  7.77 us
    ppermute x7, starting transfers between devices, on_device(): everyone = everyone + lax.ppermute(word, ('dp', 'bank'), pairs)  6.87 us
    pallas_call x1, Pallas kernels, first(): pl.pallas_call(functools.partial(first_kernel, math.gcd(keys.shape[0], 25...  5.54 us
    pallas_call x1, Pallas kernels, pick(): pl.pallas_call(functools.partial(pick_kernel, groups, owned, cap), in_spe...  4.44 us
    slice x3, local copies, waits for them, and re-layouts, on_device(): matched_line = matched_line + came[2 * turns, 0]  2.91 us
    slice x3, local copies, waits for them, and re-layouts, on_device(): sizes.append(came[turns + k][None])  2.64 us
  transfers between devices with their start and end apart: 28, of which 7 were waited for; matrix products, arithmetic and copies ran while one was open for 12% of the time, Pallas kernels for 7%

profile of v1, /device:TPU:0, one launch (start us, length us, event | category | flops | bytes accessed | tf_op | source)
XLA Modules:
  0.0 122.2 jit_solution(4983994509864278891)
XLA Ops:
  7.2 4.4 %pick.1 = (bf16[176,256]{1,0:T(8,128)(2,1)S(1)}, bf16[176,256]{1,0:T(8,128)(2,1)S(1)}, s32[16,128]{1,0:T(8,128)S(1)}, f32[8,128]{1,0:T(8,128)S(1)}) custom-call(s32[1]{0:T(128)} %bitcast.3.place_ref, s32[16,128]{1,0:T(8,128)} %pos_ref.1, bf16[16,64,256]{2,1,0:T(8,128)(2,1)} %feat_ref.1), custom_call_target="tpu_custom_call" | custom-call | flops 1000000000 | bytes 1000000 | tf_op jit(solution)/shard_map/pick/pallas_call | solution.py:130
  11.6 3.1 %collective-permute-start.1 = (bf16[176,256]{1,0:T(8,128)(2,1)S(1)}, bf16[176,256]{1,0:T(8,128)(2,1)S(1)}, u32[]{:S(2)}, u32[]{:S(2)}) collective-permute-start(bf16[176,256]{1,0:T(8,128)(2,1)S(1)} %get-tuple-element.191.refs_0_), channel_id=1, source_target_pairs={{0,2},{1,3},{2,4},{3,5},{4,6},{5,7},{6,0},{7,1},{8,10},{9,11},{10,... | collective-permute-start | bytes 270344 | tf_op jit(solution)/shard_map/ppermute | solution.py:304
  14.7 2.6 %collective-permute-start.3 = (bf16[176,256]{1,0:T(8,128)(2,1)S(1)}, bf16[176,256]{1,0:T(8,128)(2,1)S(1)}, u32[]{:S(2)}, u32[]{:S(2)}) collective-permute-start(bf16[176,256]{1,0:T(8,128)(2,1)S(1)} %get-tuple-element.191.refs_0_), channel_id=1, source_target_pairs={{0,4},{1,5},{2,6},{3,7},{4,0},{5,1},{6,2},{7,3},{8,12},{9,13},{10,... | collective-permute-start | bytes 270344 | tf_op jit(solution)/shard_map/ppermute | solution.py:304
  17.3 1.3 %collective-permute-start.5 = (bf16[176,256]{1,0:T(8,128)(2,1)S(1)}, bf16[176,256]{1,0:T(8,128)(2,1)S(1)}, u32[]{:S(2)}, u32[]{:S(2)}) collective-permute-start(bf16[176,256]{1,0:T(8,128)(2,1)S(1)} %get-tuple-element.191.refs_0_), channel_id=1, source_target_pairs={{0,6},{1,7},{2,0},{3,1},{4,2},{5,3},{6,4},{7,5},{8,14},{9,15},{10,... | collective-permute-start | bytes 270344 | tf_op jit(solution)/shard_map/ppermute | solution.py:304
  18.7 1.5 %collective-permute-start = (bf16[176,256]{1,0:T(8,128)(2,1)S(1)}, bf16[176,256]{1,0:T(8,128)(2,1)S(1)}, u32[]{:S(2)}, u32[]{:S(2)}) collective-permute-start(bf16[176,256]{1,0:T(8,128)(2,1)S(1)} %get-tuple-element.192), channel_id=1, source_target_pairs={{0,1},{1,0},{2,3},{3,2},{4,5},{5,4},{6,7},{7,6},{8,9},{9,8},{10,11... | collective-permute-start | bytes 270344 | tf_op jit(solution)/shard_map/ppermute | solution.py:316
  20.9 2.0 %gather_fusion.1 = bf16[512,256]{1,0:T(8,128)(2,1)S(1)} fusion(bf16[4096,256]{1,0:T(8,128)(2,1)S(1)} %copy-done, s32[1024]{0:T(1024)S(1)} %pad_clamp_fusion), kind=kCustom, calls=%fused_computation.1 | custom fusion | bytes 526336 | tf_op jit(solution)/shard_map/gather | solution.py:334
  24.1 1.3 %constant_dynamic-slice_fusion.2 = (bf16[1024,256]{1,0:T(8,128)(2,1)S(1)}, bf16[1024,256]{1,0:T(8,128)(2,1)S(1)}) fusion(bf16[4096,256]{1,0:T(8,128)(2,1)} %keys_ref.1, s32[]{:T(128)S(6)} %select_n.113, s32[]{:T(128)S(6)} %select_n.112), kind=kLoop, calls=%fused_computation.88 | loop fusion | bytes 2097160 | tf_op jit(solution)/shard_map/dynamic_slice | solution.py:310
  25.4 2.6 %collective-permute-done.11 = bf16[4,64,256]{2,1,0:T(8,128)(2,1)S(1)} collective-permute-done((bf16[4,64,256]{2,1,0:T(8,128)(2,1)S(1)}, bf16[4,64,256]{2,1,0:T(8,128)(2,1)S(1)}, u32[]{:S(2)}, u32[]{:S(2)}) %collective-permute-start.11) | collective-permute-done | bytes 131104 | tf_op jit(solution)/shard_map/ppermute | solution.py:337
  28.6 1.6 %collective-permute-start.9 = (bf16[1024,256]{1,0:T(8,128)(2,1)S(1)}, bf16[1024,256]{1,0:T(8,128)(2,1)S(1)}, u32[]{:S(2)}, u32[]{:S(2)}) collective-permute-start(bf16[1024,256]{1,0:T(8,128)(2,1)S(1)} %get-tuple-element.254), channel_id=1, source_target_pairs={{0,1},{1,0},{2,3},{3,2},{4,5},{5,4},{6,7},{7,6},{8,9},{9,8},{10,11... | collective-permute-start | bytes 1572872 | tf_op jit(solution)/shard_map/ppermute | solution.py:311
  30.2 0.7 collective-permute-start.2
  31.2 2.9 %collective-permute-start.6 = (bf16[176,256]{1,0:T(8,128)(2,1)S(1)}, bf16[176,256]{1,0:T(8,128)(2,1)S(1)}, u32[]{:S(2)}, u32[]{:S(2)}) collective-permute-start(bf16[176,256]{1,0:T(8,128)(2,1)S(1)} %collective-permute-done.refs_1_), channel_id=1, source_target_pairs={{0,6},{1,7},{2,0},{3,1},{4,2},{5,3},{6,4},{7,5},{8,14},{9,15},{10,... | collective-permute-start | bytes 270344 | tf_op jit(solution)/shard_map/ppermute | solution.py:304
  34.1 2.6 %collective-permute-done.2.refs_3_ = bf16[176,256]{1,0:T(8,128)(2,1)S(1)} collective-permute-done((bf16[176,256]{1,0:T(8,128)(2,1)S(1)}, bf16[176,256]{1,0:T(8,128)(2,1)S(1)}, u32[]{:S(2)}, u32[]{:S(2)}) %collective-permute-start.2) | collective-permute-done | bytes 90144 | tf_op jit(solution)/shard_map/ppermute | solution.py:304
  37.1 3.6 %collective-permute-done.4.refs_5_ = bf16[176,256]{1,0:T(8,128)(2,1)S(1)} collective-permute-done((bf16[176,256]{1,0:T(8,128)(2,1)S(1)}, bf16[176,256]{1,0:T(8,128)(2,1)S(1)}, u32[]{:S(2)}, u32[]{:S(2)}) %collective-permute-start.4) | collective-permute-done | bytes 90144 | tf_op jit(solution)/shard_map/ppermute | solution.py:304
  40.7 2.2 %collective-permute-start.12 = (bf16[2,64,256]{2,1,0:T(8,128)(2,1)S(1)}, bf16[2,64,256]{2,1,0:T(8,128)(2,1)S(1)}, u32[]{:S(2)}, u32[]{:S(2)}) collective-permute-start(bf16[2,64,256]{2,1,0:T(8,128)(2,1)S(1)} %get-tuple-element.258), channel_id=1, source_target_pairs={{0,2},{1,3},{2,4},{3,5},{4,6},{5,7},{6,0},{7,1},{8,10},{9,11},{10,... | collective-permute-start | bytes 196616 | tf_op jit(solution)/shard_map/ppermute | solution.py:304
  43.0 2.4 %arrange.1 = (bf16[1024,256]{1,0:T(8,128)(2,1)S(1)}, bf16[1024,256]{1,0:T(8,128)(2,1)S(1)}) custom-call(s32[1024,1]{1,0:T(8,128)S(1)} %bitcast.39, bf16[176,256]{1,0:T(8,128)(2,1)S(1)} %get-tuple-element.191.refs_0_, bf16[176,256]{1,0:T(8,128)(2,1)S(1)} %collective-permute-done.refs_1_, bf16[176,256]{1,0:T(8,128)(2,1)S(1)} %collective-permute-done.1.refs_2_, ...), custom_call_target="tpu_custom_call" | custom-call | flops 738197504 | bytes 786432 | tf_op jit(solution)/shard_map/arrange/pallas_call | solution.py:169
  45.4 5.5 %first.1 = (f32[1024,128]{1,0:T(8,128)S(1)}, f32[1024,256]{1,0:T(8,128)S(1)}) custom-call(bf16[1024,256]{1,0:T(8,128)(2,1)S(1)} %get-tuple-element.193.query_ref, bf16[4096,256]{1,0:T(8,128)(2,1)S(1)} %copy-done.1), custom_call_target="tpu_custom_call" | custom-call | flops 4294967296 | bytes 2621440 | tf_op jit(solution)/shard_map/first/pallas_call | solution.py:210
  52.0 1.1 broadcast_multiply_fusion.1
  53.7 1.8 %last.4 = (f32[256,256]{1,0:T(8,128)S(1)}, f32[2,256]{1,0:T(2,128)S(1)}) custom-call(bf16[1024,256]{1,0:T(8,128)(2,1)S(1)} %get-tuple-element.193.query_ref, f32[1024,128]{1,0:T(8,128)S(1)} %get-tuple-element.194.total_in, f32[1024,256]{1,0:T(8,128)S(1)} %get-tuple-element.195.pushed_in, bf16[1024,256]{1,0:T(8,128)(2,1)S(1)} %collective-permute-done.7.refs_0_, ...), custom_call_target="tpu_custom_call" | custom-call | flops 1073741824 | bytes 2228224 | tf_op jit(solution)/shard_map/last/pallas_call | solution.py:246
  56.1 1.9 %last.5 = (s16[256,256]{1,0:T(8,128)(2,1)S(1)}, f32[2,256]{1,0:T(2,128)S(1)}) custom-call(bf16[1024,256]{1,0:T(8,128)(2,1)S(1)} %get-tuple-element.193.query_ref, f32[1024,128]{1,0:T(8,128)S(1)} %get-tuple-element.194.total_in, f32[1024,256]{1,0:T(8,128)S(1)} %get-tuple-element.195.pushed_in, bf16[1024,256]{1,0:T(8,128)(2,1)S(1)} %collective-permute-done.7.refs_0_, ...), custom_call_target="tpu_custom_call" | custom-call | flops 1073741824 | bytes 2228224 | tf_op jit(solution)/shard_map/last/pallas_call | solution.py:246
  58.0 0.6 fusion.43
  58.6 1.9 %last.6 = (s16[256,256]{1,0:T(8,128)(2,1)S(1)}, f32[2,256]{1,0:T(2,128)S(1)}) custom-call(bf16[1024,256]{1,0:T(8,128)(2,1)S(1)} %get-tuple-element.193.query_ref, f32[1024,128]{1,0:T(8,128)S(1)} %get-tuple-element.194.total_in, f32[1024,256]{1,0:T(8,128)S(1)} %get-tuple-element.195.pushed_in, bf16[1024,256]{1,0:T(8,128)(2,1)S(1)} %collective-permute-done.7.refs_0_, ...), custom_call_target="tpu_custom_call" | custom-call | flops 1073741824 | bytes 2228224 | tf_op jit(solution)/shard_map/last/pallas_call | solution.py:246
  61.1 2.1 %last.7 = (s16[256,256]{1,0:T(8,128)(2,1)S(1)}, f32[2,256]{1,0:T(2,128)S(1)}) custom-call(bf16[1024,256]{1,0:T(8,128)(2,1)S(1)} %get-tuple-element.193.query_ref, f32[1024,128]{1,0:T(8,128)S(1)} %get-tuple-element.194.total_in, f32[1024,256]{1,0:T(8,128)S(1)} %get-tuple-element.195.pushed_in, bf16[1024,256]{1,0:T(8,128)(2,1)S(1)} %collective-permute-done.7.refs_0_, ...), custom_call_target="tpu_custom_call" | custom-call | flops 1073741824 | bytes 2228224 | tf_op jit(solution)/shard_map/last/pallas_call | solution.py:246
  63.9 1.2 %broadcast_in_dim.20 = f32[1,256]{1,0:T(1,128)} broadcast(f32[]{:T(128)} %get-tuple-element.277), dimensions={} | broadcast | bytes 1028 | tf_op jit(solution)/shard_map/broadcast_in_dim | solution.py:362
  65.1 2.6 %concatenate.30 = f32[9,256]{1,0:T(8,128)} concatenate(f32[1,256]{1,0:T(1,128)S(1)} %get-tuple-element.275, f32[1,256]{1,0:T(1,128)} %get-tuple-element.273, f32[1,256]{1,0:T(1,128)} %get-tuple-element.271, f32[1,256]{1,0:T(1,128)} %get-tuple-element.269, f32[1,256]{1,0:T(1,128)} %get-tuple-element.274, f32[1,256]{1,0:T(1,128)} %get-tuple-element.272, ...), dimensions={0} | concatenate | bytes 18432 | tf_op jit(solution)/shard_map/concatenate | solution.py:361
  67.7 1.6 %collective-permute-start.17 = (f32[9,256]{1,0:T(8,128)}, f32[9,256]{1,0:T(8,128)}, u32[]{:S(2)}, u32[]{:S(2)}) collective-permute-start(f32[9,256]{1,0:T(8,128)} %concatenate.30), channel_id=1, source_target_pairs={{0,6},{1,7},{2,0},{3,1},{4,2},{5,3},{6,4},{7,5},{8,14},{9,15},{10,... | collective-permute-start | bytes 27656 | tf_op jit(solution)/shard_map/ppermute | solution.py:304
  69.3 0.9 convert_reduce_fusion.2
  71.5 0.6 reduce_max.19
  72.8 1.2 collective-permute-start.16
  74.0 1.3 %fusion.39 = (f32[1,256]{1,0:T(1,128)}, f32[1,256]{1,0:T(1,128)S(1)}) fusion(f32[9,256]{1,0:T(8,128)} %collective-permute-done.17), kind=kLoop, calls=%fused_computation.112 | loop fusion | bytes 4096 | tf_op jit(solution)/shard_map/slice | solution.py:370
  75.3 4.4 %collective-permute-done.15 = f32[9,256]{1,0:T(8,128)S(1)} collective-permute-done((f32[9,256]{1,0:T(8,128)}, f32[9,256]{1,0:T(8,128)S(1)}, u32[]{:S(2)}, u32[]{:S(2)}) %collective-permute-start.15) | collective-permute-done | bytes 9248 | tf_op jit(solution)/shard_map/ppermute | solution.py:304
  82.1 0.7 slice.148
  82.8 0.7 slice.143
  83.5 0.8 fusion.40
  84.3 1.3 %log_reduce_fusion = (f32[]{:T(128)}, f32[4,256]{1,0:T(4,128)S(1)}) fusion(f32[3,256]{1,0:T(4,128)S(1)} %slice.148, f32[1,256]{1,0:T(1,128)S(1)} %get-tuple-element.265, f32[2,256]{1,0:T(2,128)S(1)} %get-tuple-element.267, f32[2,256]{1,0:T(2,128)S(1)} %get-tuple-element.266, f32[1,256]{1,0:T(1,128)} %get-tuple-element.263, f32[3,256]{1,0:T(4,128)S(1)} %slice.143, ...), kind=kLoop, calls=%fused_computation.83 | loop fusion | flops 10239 | bytes 20484 | tf_op jit(solution)/shard_map/reduce_sum | solution.py:375
  86.3 1.2 slice.150
  88.1 1.2 slice.151
  90.1 1.8 %collective-permute-start.23 = (f32[2,128]{1,0:T(2,128)S(1)}, f32[2,128]{1,0:T(2,128)S(1)}, u32[]{:S(2)}, u32[]{:S(2)}) collective-permute-start(f32[2,128]{1,0:T(2,128)S(1)} %stack.31), channel_id=1, source_target_pairs={{0,24},{1,25},{2,26},{3,27},{4,28},{5,29},{6,30},{7,31},{8,0},{9,1... | collective-permute-start | bytes 3080 | tf_op jit(solution)/shard_map/ppermute | solution.py:386
  91.9 1.5 %collective-permute-start.22 = (f32[2,128]{1,0:T(2,128)S(1)}, f32[2,128]{1,0:T(2,128)S(1)}, u32[]{:S(2)}, u32[]{:S(2)}) collective-permute-start(f32[2,128]{1,0:T(2,128)S(1)} %stack.31), channel_id=1, source_target_pairs={{0,17},{1,16},{2,19},{3,18},{4,21},{5,20},{6,23},{7,22},{8,25},{9,... | collective-permute-start | bytes 3080 | tf_op jit(solution)/shard_map/ppermute | solution.py:386
  93.4 1.5 %collective-permute-start.21 = (f32[2,128]{1,0:T(2,128)S(1)}, f32[2,128]{1,0:T(2,128)S(1)}, u32[]{:S(2)}, u32[]{:S(2)}) collective-permute-start(f32[2,128]{1,0:T(2,128)S(1)} %stack.31), channel_id=1, source_target_pairs={{0,16},{1,17},{2,18},{3,19},{4,20},{5,21},{6,22},{7,23},{8,24},{9,... | collective-permute-start | bytes 3080 | tf_op jit(solution)/shard_map/ppermute | solution.py:386
  94.9 0.7 slice.154
  96.2 1.5 %collective-permute-start.18 = (f32[2,128]{1,0:T(2,128)S(1)}, f32[2,128]{1,0:T(2,128)S(1)}, u32[]{:S(2)}, u32[]{:S(2)}) collective-permute-start(f32[2,128]{1,0:T(2,128)S(1)} %stack.31), channel_id=1, source_target_pairs={{0,1},{1,0},{2,3},{3,2},{4,5},{5,4},{6,7},{7,6},{8,9},{9,8},{10,11... | collective-permute-start | bytes 3080 | tf_op jit(solution)/shard_map/ppermute | solution.py:386
  97.7 0.7 pad_maximum_fusion.1.stats_ref
  98.9 3.4 %collective-permute-start.27 = (s16[256,256]{1,0:T(8,128)(2,1)S(1)}, s16[256,256]{1,0:T(8,128)(2,1)S(1)}, u32[]{:S(2)}, u32[]{:S(2)}) collective-permute-start(s16[256,256]{1,0:T(8,128)(2,1)S(1)} %get-tuple-element.205), channel_id=1, source_target_pairs={{0,6},{1,7},{2,0},{3,1},{4,2},{5,3},{6,4},{7,5},{8,14},{9,15},{10,... | collective-permute-start | bytes 393224 | tf_op jit(solution)/shard_map/ppermute | solution.py:304
  103.6 3.1 %collective-permute-done.25.refs_0_ = s16[256,256]{1,0:T(8,128)(2,1)S(1)} collective-permute-done((s16[256,256]{1,0:T(8,128)(2,1)S(1)}, s16[256,256]{1,0:T(8,128)(2,1)S(1)}, u32[]{:S(2)}, u32[]{:S(2)}) %collective-permute-start.25) | collective-permute-done | bytes 131104 | tf_op jit(solution)/shard_map/ppermute | solution.py:304
  106.7 4.5 %collective-permute-done.26.refs_1_ = s16[256,256]{1,0:T(8,128)(2,1)S(1)} collective-permute-done((s16[256,256]{1,0:T(8,128)(2,1)S(1)}, s16[256,256]{1,0:T(8,128)(2,1)S(1)}, u32[]{:S(2)}, u32[]{:S(2)}) %collective-permute-start.26) | collective-permute-done | bytes 131104 | tf_op jit(solution)/shard_map/ppermute | solution.py:304
  111.7 1.8 %conditional.1 = (f32[256,256]{1,0:T(8,128)S(1)}, f32[256]{0:T(256)S(1)}, f32[]{:T(128)}) conditional(s32[]{:T(128)} %bitcast.20, (f32[1,256]{1,0:T(1,128)S(1)}, f32[256]{0:T(256)S(1)}, f32[256]{0:T(256)}, f32[2,128]{1,0:T(2,128)S(1)}, f32[256,256]{1,0:T(8,128)S(1)}) %tuple.42, (s32[16,128]{1,0:T(8,128)}, bf16[16,64,256]{2,1,0:T(8,128)(2,1)}, ...), branch_computations={%region_9.10_spmd, %region_10.25_spmd} | conditional | flops 1154975744 | bytes 68631688 | solution.py:388
  111.7 0.6 add_subtract_fusion
  113.6 0.7 copy-done.5
  (91 shorter events, 11.2 us)
Async XLA Ops:
  7.2 13.0 %copy-start.6 = (s32[2048]{0:T(1024)S(1)}, s32[2048]{0:T(1024)}, u32[]{:S(2)}) copy-start(s32[2048]{0:T(1024)} %param.10) | copy-start | bytes 24580
  7.2 13.8 %copy-start = (bf16[4096,256]{1,0:T(8,128)(2,1)S(1)}, bf16[4096,256]{1,0:T(8,128)(2,1)}, u32[]{:S(2)}) copy-start(bf16[4096,256]{1,0:T(8,128)(2,1)} %keys_ref.1) | copy-start | bytes 6291460
  11.6 18.6 %collective-permute-start.1 = (bf16[176,256]{1,0:T(8,128)(2,1)S(1)}, bf16[176,256]{1,0:T(8,128)(2,1)S(1)}, u32[]{:S(2)}, u32[]{:S(2)}) collective-permute-start(bf16[176,256]{1,0:T(8,128)(2,1)S(1)} %get-tuple-element.191.refs_0_), channel_id=1, source_target_pairs={{0,2},{1,3},{2,4},{3,5},{4,6},{5,7},{6,0},{7,1},{8,10},{9,11},{10,... | collective-permute-start | bytes 270344 | tf_op jit(solution)/shard_map/ppermute | solution.py:304
  14.7 16.2 %collective-permute-start.3 = (bf16[176,256]{1,0:T(8,128)(2,1)S(1)}, bf16[176,256]{1,0:T(8,128)(2,1)S(1)}, u32[]{:S(2)}, u32[]{:S(2)}) collective-permute-start(bf16[176,256]{1,0:T(8,128)(2,1)S(1)} %get-tuple-element.191.refs_0_), channel_id=1, source_target_pairs={{0,4},{1,5},{2,6},{3,7},{4,0},{5,1},{6,2},{7,3},{8,12},{9,13},{10,... | collective-permute-start | bytes 270344 | tf_op jit(solution)/shard_map/ppermute | solution.py:304
  17.3 13.9 %collective-permute-start.5 = (bf16[176,256]{1,0:T(8,128)(2,1)S(1)}, bf16[176,256]{1,0:T(8,128)(2,1)S(1)}, u32[]{:S(2)}, u32[]{:S(2)}) collective-permute-start(bf16[176,256]{1,0:T(8,128)(2,1)S(1)} %get-tuple-element.191.refs_0_), channel_id=1, source_target_pairs={{0,6},{1,7},{2,0},{3,1},{4,2},{5,3},{6,4},{7,5},{8,14},{9,15},{10,... | collective-permute-start | bytes 270344 | tf_op jit(solution)/shard_map/ppermute | solution.py:304
  18.7 10.0 %collective-permute-start = (bf16[176,256]{1,0:T(8,128)(2,1)S(1)}, bf16[176,256]{1,0:T(8,128)(2,1)S(1)}, u32[]{:S(2)}, u32[]{:S(2)}) collective-permute-start(bf16[176,256]{1,0:T(8,128)(2,1)S(1)} %get-tuple-element.192), channel_id=1, source_target_pairs={{0,1},{1,0},{2,3},{3,2},{4,5},{5,4},{6,7},{7,6},{8,9},{9,8},{10,11... | collective-permute-start | bytes 270344 | tf_op jit(solution)/shard_map/ppermute | solution.py:316
  20.2 5.2 %copy-start.7 = (s32[8,256]{1,0:T(8,128)}, s32[8,256]{1,0:T(8,128)S(1)}, u32[]{:S(2)}) copy-start(s32[8,256]{1,0:T(8,128)S(1)} %get-tuple-element.247) | copy-start | bytes 24580
  22.9 5.0 %collective-permute-start.11 = (bf16[4,64,256]{2,1,0:T(8,128)(2,1)S(1)}, bf16[4,64,256]{2,1,0:T(8,128)(2,1)S(1)}, u32[]{:S(2)}, u32[]{:S(2)}) collective-permute-start(bf16[4,64,256]{2,1,0:T(8,128)(2,1)S(1)} %get-tuple-element.260), channel_id=1, source_target_pairs={{0,1},{1,0},{2,3},{3,2},{4,5},{5,4},{6,7},{7,6},{8,9},{9,8},{10,11... | collective-permute-start | bytes 393224 | tf_op jit(solution)/shard_map/ppermute | solution.py:337
  25.4 20.0 %copy-start.1 = (bf16[4096,256]{1,0:T(8,128)(2,1)S(1)}, bf16[4096,256]{1,0:T(8,128)(2,1)}, u32[]{:S(2)}) copy-start(bf16[4096,256]{1,0:T(8,128)(2,1)} %keys_ref.1) | copy-start | bytes 6291460
  28.0 23.0 %collective-permute-start.7 = (bf16[1024,256]{1,0:T(8,128)(2,1)S(1)}, bf16[1024,256]{1,0:T(8,128)(2,1)S(1)}, u32[]{:S(2)}, u32[]{:S(2)}) collective-permute-start(bf16[1024,256]{1,0:T(8,128)(2,1)S(1)} %get-tuple-element.255), channel_id=1, source_target_pairs={{0,1},{1,0},{2,3},{3,2},{4,5},{5,4},{6,7},{7,6},{8,9},{9,8},{10,11... | collective-permute-start | bytes 1572872 | tf_op jit(solution)/shard_map/ppermute | solution.py:311
  28.6 22.4 %collective-permute-start.9 = (bf16[1024,256]{1,0:T(8,128)(2,1)S(1)}, bf16[1024,256]{1,0:T(8,128)(2,1)S(1)}, u32[]{:S(2)}, u32[]{:S(2)}) collective-permute-start(bf16[1024,256]{1,0:T(8,128)(2,1)S(1)} %get-tuple-element.254), channel_id=1, source_target_pairs={{0,1},{1,0},{2,3},{3,2},{4,5},{5,4},{6,7},{7,6},{8,9},{9,8},{10,11... | collective-permute-start | bytes 1572872 | tf_op jit(solution)/shard_map/ppermute | solution.py:311
  30.2 6.5 %collective-permute-start.2 = (bf16[176,256]{1,0:T(8,128)(2,1)S(1)}, bf16[176,256]{1,0:T(8,128)(2,1)S(1)}, u32[]{:S(2)}, u32[]{:S(2)}) collective-permute-start(bf16[176,256]{1,0:T(8,128)(2,1)S(1)} %collective-permute-done.refs_1_), channel_id=1, source_target_pairs={{0,2},{1,3},{2,4},{3,5},{4,6},{5,7},{6,0},{7,1},{8,10},{9,11},{10,... | collective-permute-start | bytes 270344 | tf_op jit(solution)/shard_map/ppermute | solution.py:304
  30.9 9.8 %collective-permute-start.4 = (bf16[176,256]{1,0:T(8,128)(2,1)S(1)}, bf16[176,256]{1,0:T(8,128)(2,1)S(1)}, u32[]{:S(2)}, u32[]{:S(2)}) collective-permute-start(bf16[176,256]{1,0:T(8,128)(2,1)S(1)} %collective-permute-done.refs_1_), channel_id=1, source_target_pairs={{0,4},{1,5},{2,6},{3,7},{4,0},{5,1},{6,2},{7,3},{8,12},{9,13},{10,... | collective-permute-start | bytes 270344 | tf_op jit(solution)/shard_map/ppermute | solution.py:304
  31.2 9.5 %collective-permute-start.6 = (bf16[176,256]{1,0:T(8,128)(2,1)S(1)}, bf16[176,256]{1,0:T(8,128)(2,1)S(1)}, u32[]{:S(2)}, u32[]{:S(2)}) collective-permute-start(bf16[176,256]{1,0:T(8,128)(2,1)S(1)} %collective-permute-done.refs_1_), channel_id=1, source_target_pairs={{0,6},{1,7},{2,0},{3,1},{4,2},{5,3},{6,4},{7,5},{8,14},{9,15},{10,... | collective-permute-start | bytes 270344 | tf_op jit(solution)/shard_map/ppermute | solution.py:304
  36.7 14.9 %collective-permute-start.14 = (bf16[2,64,256]{2,1,0:T(8,128)(2,1)S(1)}, bf16[2,64,256]{2,1,0:T(8,128)(2,1)S(1)}, u32[]{:S(2)}, u32[]{:S(2)}) collective-permute-start(bf16[2,64,256]{2,1,0:T(8,128)(2,1)S(1)} %get-tuple-element.259), channel_id=1, source_target_pairs={{0,6},{1,7},{2,0},{3,1},{4,2},{5,3},{6,4},{7,5},{8,14},{9,15},{10,... | collective-permute-start | bytes 196616 | tf_op jit(solution)/shard_map/ppermute | solution.py:304
  40.7 10.8 %collective-permute-start.13 = (bf16[2,64,256]{2,1,0:T(8,128)(2,1)S(1)}, bf16[2,64,256]{2,1,0:T(8,128)(2,1)S(1)}, u32[]{:S(2)}, u32[]{:S(2)}) collective-permute-start(bf16[2,64,256]{2,1,0:T(8,128)(2,1)S(1)} %get-tuple-element.257), channel_id=1, source_target_pairs={{0,4},{1,5},{2,6},{3,7},{4,0},{5,1},{6,2},{7,3},{8,12},{9,13},{10,... | collective-permute-start | bytes 196616 | tf_op jit(solution)/shard_map/ppermute | solution.py:304
  40.7 10.8 %collective-permute-start.12 = (bf16[2,64,256]{2,1,0:T(8,128)(2,1)S(1)}, bf16[2,64,256]{2,1,0:T(8,128)(2,1)S(1)}, u32[]{:S(2)}, u32[]{:S(2)}) collective-permute-start(bf16[2,64,256]{2,1,0:T(8,128)(2,1)S(1)} %get-tuple-element.258), channel_id=1, source_target_pairs={{0,2},{1,3},{2,4},{3,5},{4,6},{5,7},{6,0},{7,1},{8,10},{9,11},{10,... | collective-permute-start | bytes 196616 | tf_op jit(solution)/shard_map/ppermute | solution.py:304
  51.0 2.1 %collective-permute-start.8 = (bf16[1024,256]{1,0:T(8,128)(2,1)S(1)}, bf16[1024,256]{1,0:T(8,128)(2,1)S(1)}, u32[]{:S(2)}, u32[]{:S(2)}) collective-permute-start(bf16[1024,256]{1,0:T(8,128)(2,1)S(1)} %collective-permute-done.7.refs_0_), channel_id=1, source_target_pairs={{0,8},{8,0},{16,24},{24,16},{1,9},{9,1},{17,25},{25,17},{2,10},{10... | collective-permute-start | bytes 1572872 | tf_op jit(solution)/shard_map/ppermute | solution.py:312
  51.1 2.6 %collective-permute-start.10 = (bf16[1024,256]{1,0:T(8,128)(2,1)S(1)}, bf16[1024,256]{1,0:T(8,128)(2,1)S(1)}, u32[]{:S(2)}, u32[]{:S(2)}) collective-permute-start(bf16[1024,256]{1,0:T(8,128)(2,1)S(1)} %collective-permute-done.9.refs_2_), channel_id=1, source_target_pairs={{0,8},{8,0},{16,24},{24,16},{1,9},{9,1},{17,25},{25,17},{2,10},{10... | collective-permute-start | bytes 1572872 | tf_op jit(solution)/shard_map/ppermute | solution.py:312
  56.1 9.1 %copy-start.8 = (f32[1,256]{1,0:T(1,128)}, f32[1,256]{1,0:T(1,128)S(1)}, u32[]{:S(2)}) copy-start(f32[1,256]{1,0:T(1,128)S(1)} %get-tuple-element.275) | copy-start | bytes 3076
  61.1 50.6 %copy-start.2 = (bf16[4096,256]{1,0:T(8,128)(2,1)S(1)}, bf16[4096,256]{1,0:T(8,128)(2,1)}, u32[]{:S(2)}) copy-start(bf16[4096,256]{1,0:T(8,128)(2,1)} %keys_ref.1) | copy-start | bytes 6291460
  67.7 6.2 %collective-permute-start.17 = (f32[9,256]{1,0:T(8,128)}, f32[9,256]{1,0:T(8,128)}, u32[]{:S(2)}, u32[]{:S(2)}) collective-permute-start(f32[9,256]{1,0:T(8,128)} %concatenate.30), channel_id=1, source_target_pairs={{0,6},{1,7},{2,0},{3,1},{4,2},{5,3},{6,4},{7,5},{8,14},{9,15},{10,... | collective-permute-start | bytes 27656 | tf_op jit(solution)/shard_map/ppermute | solution.py:304
  72.8 10.8 %collective-permute-start.16 = (f32[9,256]{1,0:T(8,128)}, f32[9,256]{1,0:T(8,128)}, u32[]{:S(2)}, u32[]{:S(2)}) collective-permute-start(f32[9,256]{1,0:T(8,128)} %concatenate.30), channel_id=1, source_target_pairs={{0,4},{1,5},{2,6},{3,7},{4,0},{5,1},{6,2},{7,3},{8,12},{9,13},{10,... | collective-permute-start | bytes 27656 | tf_op jit(solution)/shard_map/ppermute | solution.py:304
  74.0 5.7 %collective-permute-start.15 = (f32[9,256]{1,0:T(8,128)}, f32[9,256]{1,0:T(8,128)S(1)}, u32[]{:S(2)}, u32[]{:S(2)}) collective-permute-start(f32[9,256]{1,0:T(8,128)} %concatenate.30), channel_id=1, source_target_pairs={{0,2},{1,3},{2,4},{3,5},{4,6},{5,7},{6,0},{7,1},{8,10},{9,11},{10,... | collective-permute-start | bytes 27656 | tf_op jit(solution)/shard_map/ppermute | solution.py:304
  79.7 0.6 copy-start.9
  90.1 5.5 %collective-permute-start.24 = (f32[2,128]{1,0:T(2,128)S(1)}, f32[2,128]{1,0:T(2,128)S(1)}, u32[]{:S(2)}, u32[]{:S(2)}) collective-permute-start(f32[2,128]{1,0:T(2,128)S(1)} %stack.31), channel_id=1, source_target_pairs={{0,25},{1,24},{2,27},{3,26},{4,29},{5,28},{6,31},{7,30},{8,1},{9,0... | collective-permute-start | bytes 3080 | tf_op jit(solution)/shard_map/ppermute | solution.py:386
  90.1 6.1 %collective-permute-start.23 = (f32[2,128]{1,0:T(2,128)S(1)}, f32[2,128]{1,0:T(2,128)S(1)}, u32[]{:S(2)}, u32[]{:S(2)}) collective-permute-start(f32[2,128]{1,0:T(2,128)S(1)} %stack.31), channel_id=1, source_target_pairs={{0,24},{1,25},{2,26},{3,27},{4,28},{5,29},{6,30},{7,31},{8,0},{9,1... | collective-permute-start | bytes 3080 | tf_op jit(solution)/shard_map/ppermute | solution.py:386
  91.9 6.5 %collective-permute-start.22 = (f32[2,128]{1,0:T(2,128)S(1)}, f32[2,128]{1,0:T(2,128)S(1)}, u32[]{:S(2)}, u32[]{:S(2)}) collective-permute-start(f32[2,128]{1,0:T(2,128)S(1)} %stack.31), channel_id=1, source_target_pairs={{0,17},{1,16},{2,19},{3,18},{4,21},{5,20},{6,23},{7,22},{8,25},{9,... | collective-permute-start | bytes 3080 | tf_op jit(solution)/shard_map/ppermute | solution.py:386
  93.4 5.1 %collective-permute-start.21 = (f32[2,128]{1,0:T(2,128)S(1)}, f32[2,128]{1,0:T(2,128)S(1)}, u32[]{:S(2)}, u32[]{:S(2)}) collective-permute-start(f32[2,128]{1,0:T(2,128)S(1)} %stack.31), channel_id=1, source_target_pairs={{0,16},{1,17},{2,18},{3,19},{4,20},{5,21},{6,22},{7,23},{8,24},{9,... | collective-permute-start | bytes 3080 | tf_op jit(solution)/shard_map/ppermute | solution.py:386
  94.9 4.0 %collective-permute-start.20 = (f32[2,128]{1,0:T(2,128)S(1)}, f32[2,128]{1,0:T(2,128)S(1)}, u32[]{:S(2)}, u32[]{:S(2)}) collective-permute-start(f32[2,128]{1,0:T(2,128)S(1)} %stack.31), channel_id=1, source_target_pairs={{0,9},{1,8},{2,11},{3,10},{4,13},{5,12},{6,15},{7,14},{8,17},{9,16... | collective-permute-start | bytes 3080 | tf_op jit(solution)/shard_map/ppermute | solution.py:386
  95.6 6.7 %collective-permute-start.19 = (f32[2,128]{1,0:T(2,128)S(1)}, f32[2,128]{1,0:T(2,128)S(1)}, u32[]{:S(2)}, u32[]{:S(2)}) collective-permute-start(f32[2,128]{1,0:T(2,128)S(1)} %stack.31), channel_id=1, source_target_pairs={{0,8},{1,9},{2,10},{3,11},{4,12},{5,13},{6,14},{7,15},{8,16},{9,17... | collective-permute-start | bytes 3080 | tf_op jit(solution)/shard_map/ppermute | solution.py:386
  96.2 6.1 %collective-permute-start.18 = (f32[2,128]{1,0:T(2,128)S(1)}, f32[2,128]{1,0:T(2,128)S(1)}, u32[]{:S(2)}, u32[]{:S(2)}) collective-permute-start(f32[2,128]{1,0:T(2,128)S(1)} %stack.31), channel_id=1, source_target_pairs={{0,1},{1,0},{2,3},{3,2},{4,5},{5,4},{6,7},{7,6},{8,9},{9,8},{10,11... | collective-permute-start | bytes 3080 | tf_op jit(solution)/shard_map/ppermute | solution.py:386
  98.4 8.3 %collective-permute-start.25 = (s16[256,256]{1,0:T(8,128)(2,1)S(1)}, s16[256,256]{1,0:T(8,128)(2,1)S(1)}, u32[]{:S(2)}, u32[]{:S(2)}) collective-permute-start(s16[256,256]{1,0:T(8,128)(2,1)S(1)} %get-tuple-element.203), channel_id=1, source_target_pairs={{0,2},{1,3},{2,4},{3,5},{4,6},{5,7},{6,0},{7,1},{8,10},{9,11},{10,... | collective-permute-start | bytes 393224 | tf_op jit(solution)/shard_map/ppermute | solution.py:304
  98.5 12.7 %collective-permute-start.26 = (s16[256,256]{1,0:T(8,128)(2,1)S(1)}, s16[256,256]{1,0:T(8,128)(2,1)S(1)}, u32[]{:S(2)}, u32[]{:S(2)}) collective-permute-start(s16[256,256]{1,0:T(8,128)(2,1)S(1)} %get-tuple-element.204), channel_id=1, source_target_pairs={{0,4},{1,5},{2,6},{3,7},{4,0},{5,1},{6,2},{7,3},{8,12},{9,13},{10,... | collective-permute-start | bytes 393224 | tf_op jit(solution)/shard_map/ppermute | solution.py:304
  98.9 12.3 %collective-permute-start.27 = (s16[256,256]{1,0:T(8,128)(2,1)S(1)}, s16[256,256]{1,0:T(8,128)(2,1)S(1)}, u32[]{:S(2)}, u32[]{:S(2)}) collective-permute-start(s16[256,256]{1,0:T(8,128)(2,1)S(1)} %get-tuple-element.205), channel_id=1, source_target_pairs={{0,6},{1,7},{2,0},{3,1},{4,2},{5,3},{6,4},{7,5},{8,14},{9,15},{10,... | collective-permute-start | bytes 393224 | tf_op jit(solution)/shard_map/ppermute | solution.py:304
  113.5 0.7 copy-start.5
  113.5 0.7 copy-start.10

commit v2 on v0

v2 whole, which is shorter than its diff:
```python
import functools
import math

import jax
import jax.numpy as jnp
from jax import lax
from jax.experimental import pallas as pl
from jax.experimental.pallas import tpu as pltpu
from jax.sharding import PartitionSpec as P

SOFTMAX_TEMP = 0.07
EPSILON = 1e-05
INV_TEMP = 1.0 / SOFTMAX_TEMP
STEPS = 32700.0
F32 = jnp.float32
BF16 = jnp.bfloat16
NT = (((1,), (1,)), ((), ()))


def normalize(values):
    scale = lax.rsqrt(jnp.mean(values * values, axis=-1, keepdims=True) + EPSILON)
    return values * scale / math.sqrt(values.shape[-1])


def ring_sum(value, axis):
    size = lax.axis_size(axis)
    pairs = [(i, (i + 1) % size) for i in range(size)]

    def step(_, carry):
        moving, total = carry
        moving = lax.ppermute(moving, axis, pairs)
        return (moving, total + moving)

    return lax.fori_loop(0, size - 1, step, (value, value))[1]


def plain(features, patch_index, positive_index, bank):
    groups = lax.axis_size("bank")
    place = lax.axis_index("bank")
    images, hw_dev, channels = features.shape
    queries_dp = images * patch_index.shape[1]
    owned_rows = queries_dp // groups
    local_pos = patch_index - place * hw_dev
    onehot = (local_pos[:, :, None] == jnp.arange(hw_dev, dtype=jnp.int32)[None, None, :]).astype(BF16)
    picked = jnp.einsum("iph,ihc->ipc", onehot, features, preferred_element_type=F32)
    raw_all = ring_sum(picked.reshape(queries_dp, channels), "bank")
    query_vector = normalize(raw_all).astype(BF16)
    raw_own = lax.dynamic_slice_in_dim(raw_all, place * owned_rows, owned_rows, 0)
    bank_dev = bank.shape[0]
    block_keys = math.gcd(bank_dev, 512)

    def visit(index, carry):
        exponent_sum, weighted = carry
        block = lax.dynamic_slice_in_dim(bank, index * block_keys, block_keys, 0)
        logit = lax.dot_general(query_vector, block, NT, preferred_element_type=F32) / SOFTMAX_TEMP
        terms = jnp.exp(logit - INV_TEMP)
        exponent_sum = exponent_sum + jnp.sum(terms, axis=1)
        weighted = weighted + jnp.dot(terms.astype(BF16), block, preferred_element_type=F32)
        return (exponent_sum, weighted)

    start = (jnp.zeros((queries_dp,), F32), jnp.zeros((queries_dp, channels), F32))
    exponent_sum, weighted = lax.fori_loop(0, bank_dev // block_keys, visit, start)
    key_pos = positive_index - place * bank_dev
    inside = (key_pos >= 0) & (key_pos < bank_dev)
    rows_pos = jnp.clip(key_pos, 0, bank_dev - 1)
    positive_key = bank[rows_pos].astype(F32) * inside[:, None].astype(F32)
    matched = jnp.sum(query_vector.astype(F32) * positive_key, axis=1) / SOFTMAX_TEMP
    own_sum, own_logit, own_weighted, own_positive = (
        lax.dynamic_slice_in_dim(ring_sum(v, "bank"), place * owned_rows, owned_rows, 0)
        for v in (exponent_sum, matched, weighted, positive_key)
    )
    step = (own_weighted / own_sum[:, None] - own_positive) / SOFTMAX_TEMP
    loss = jnp.log(own_sum) + INV_TEMP - own_logit
    _, pullback = jax.vjp(normalize, raw_own)
    query_grad = pullback(step)[0]
    count_all = queries_dp * lax.axis_size("dp")
    mean_loss = ring_sum(ring_sum(jnp.full((8, 128), jnp.sum(loss)), "bank"), "dp")[0, 0] / count_all
    return (loss, query_grad, mean_loss)


def cost(flops):
    return pl.CostEstimate(flops=int(flops), bytes_accessed=1 << 20, transcendentals=0)


def capacity(mean, least, sigmas):
    room = mean + sigmas * math.sqrt(mean)
    return min(least, -(-int(math.ceil(room)) // 16) * 16)


def call(kernel, name, out_shape, flops, room=16, **more):
    params = pltpu.CompilerParams(vmem_limit_bytes=room << 20)
    return pl.pallas_call(
        kernel, out_shape=out_shape, compiler_params=params, cost_estimate=cost(flops), name=name, **more
    )


ANYWHERE = pl.BlockSpec(memory_space=pl.ANY)


def after(value, *others):
    return call(
        lambda *refs: None,
        "after",
        jax.ShapeDtypeStruct(value.shape, value.dtype),
        0,
        in_specs=[ANYWHERE] * (1 + len(others)),
        out_specs=ANYWHERE,
        input_output_aliases={0: 0},
    )(value, *others)


def in_lanes(column_parts, reduce):
    return reduce(column_parts.T, axis=0, keepdims=True)


def pick_kernel(
    groups, owned, cap, place_ref, pos_ref, feat_ref, bank_ref, own_ref, other_ref, loc_ref, most_ref, half_ref, sem
):
    half = half_ref.shape[0]
    rows = pl.ds(pl.multiple_of(place_ref[1] * half, half), half)
    fetch = pltpu.make_async_copy(bank_ref.at[rows], half_ref, sem)
    fetch.start()
    place = place_ref[0]
    images, patches = pos_ref.shape
    hw = feat_ref.shape[1]
    pos = pos_ref[...]
    holder = pos // hw
    row = lax.broadcasted_iota(jnp.int32, pos.shape, 0) * patches + lax.broadcasted_iota(jnp.int32, pos.shape, 1)
    parity = (row // owned) % 2
    code = holder * 2 + parity
    batch = math.gcd(2 * groups, 16)
    tall = batch * images
    up = lax.broadcasted_iota(jnp.int32, (patches, 2 * patches), 0) <= lax.broadcasted_iota(
        jnp.int32, (patches, 2 * patches), 1
    )
    up = up.astype(F32).astype(BF16)
    above = lax.broadcasted_iota(jnp.int32, (tall, tall), 0)
    under = lax.broadcasted_iota(jnp.int32, (tall, tall), 1)
    low = (above > under) & (above // images == under // images)
    low = low.astype(F32).astype(BF16)
    ranks = jnp.full(pos.shape, -1.0, F32)
    most = jnp.zeros((1, patches), F32)
    for g in range(0, 2 * groups, batch):
        hits = [(code == g + b).astype(F32) for b in range(batch)]
        mask = jnp.concatenate(hits, axis=0)
        sums = jnp.dot(mask.astype(BF16), up, preferred_element_type=F32)
        count = sums[:, patches:]
        rank = sums[:, :patches] + jnp.dot(low, count.astype(BF16), preferred_element_type=F32)
        rank = rank * mask
        for b in range(batch):
            ranks = ranks + rank[b * images : (b + 1) * images]
            most = jnp.maximum(most, jnp.sum(count[b * images : (b + 1) * images], axis=0, keepdims=True))
    most_ref[...] = jnp.broadcast_to(most, most_ref.shape)
    inner = place % 2
    outer = place // 2
    away = outer ^ (holder // 2)
    side = (holder % 2 + inner) % 2
    ranks = ranks.astype(jnp.int32)
    loc_ref[...] = (away * 2 + side) * cap + ranks
    local = pos - place * hw
    mine = holder == place
    slot = ranks + jnp.where(parity == inner, 0, cap)
    slot = jnp.where(mine & (ranks < cap), slot, -1)
    total = jnp.zeros((2 * cap, feat_ref.shape[2]), F32)
    where_slot = lax.broadcasted_iota(jnp.int32, (2 * cap, patches), 0)
    where_pos = lax.broadcasted_iota(jnp.int32, (hw, patches), 0)
    for i in range(images):
        chosen = (where_slot == slot[i : i + 1, :]).astype(F32).astype(BF16)
        spots = (where_pos == local[i : i + 1, :]).astype(F32).astype(BF16)
        table = lax.dot_general(chosen, spots, NT, preferred_element_type=F32)
        total = total + jnp.dot(table.astype(BF16), feat_ref[i], preferred_element_type=F32)
    own_ref[...] = total[:cap].astype(BF16)
    other_ref[...] = total[cap:].astype(BF16)
    fetch.wait()


def pick(features, patch_index, bank, place, core, groups, owned, cap):
    images, patches = patch_index.shape
    channels = features.shape[2]
    return call(
        functools.partial(pick_kernel, groups, owned, cap),
        "pick",
        [
            jax.ShapeDtypeStruct((cap, channels), BF16),
            jax.ShapeDtypeStruct((cap, channels), BF16),
            jax.ShapeDtypeStruct((images, patches), jnp.int32),
            jax.ShapeDtypeStruct((8, patches), F32),
            jax.ShapeDtypeStruct((bank.shape[0] // 2, channels), BF16),
        ],
        3e9,
        in_specs=[
            pl.BlockSpec(memory_space=pltpu.SMEM),
            pl.BlockSpec(memory_space=pltpu.VMEM),
            pl.BlockSpec(memory_space=pltpu.VMEM),
            pl.BlockSpec(memory_space=pl.ANY),
        ],
        scratch_shapes=[pltpu.SemaphoreType.DMA],
    )(jnp.stack([place, core]), patch_index, features, bank)


def pack_kernel(turns, place_ref, mine_ref, side_ref, *refs):
    cap = mine_ref.shape[2]
    outs = refs[-turns:]
    for k in range(turns):
        outer = (place_ref[0] // 2) ^ k
        outs[k][:cap, :] = mine_ref[outer, place_ref[0] % 2]
        outs[k][cap:, :] = side_ref[outer]


def pack(place, mine, side, gates):
    turns, _, cap, channels = mine.shape
    return call(
        functools.partial(pack_kernel, turns),
        "pack",
        [jax.ShapeDtypeStruct((2 * cap, channels), BF16)] * turns,
        1e8,
        in_specs=[pl.BlockSpec(memory_space=pltpu.SMEM)]
        + [pl.BlockSpec(memory_space=pltpu.VMEM)] * 2
        + [ANYWHERE] * len(gates),
    )(place.reshape(1), mine, side, *gates)


def arrange_kernel(turns, loc_ref, gate_ref, *refs):
    parts, (query_ref, raw_ref), blocks = refs[: -2 - turns], refs[-2 - turns : -turns], refs[-turns:]
    rows = loc_ref.shape[0]
    loc = loc_ref[...]
    raw = jnp.zeros(query_ref.shape, F32)
    at = 0
    for ref in parts:
        lane = lax.broadcasted_iota(jnp.int32, (rows, ref.shape[0]), 1)
        table = (lane + at == loc).astype(F32).astype(BF16)
        raw = raw + jnp.dot(table, ref[...], preferred_element_type=F32)
        at += ref.shape[0]
    query = normalize(raw).astype(BF16)
    query_ref[...] = query
    owned = raw_ref.shape[0]

    @pl.when(pl.program_id(0) == 0)
    def _():
        raw_ref[...] = raw[:owned].astype(BF16)

    each = rows // owned
    for k in range(turns):

        @pl.when(pl.program_id(0) == k // each)
        def _():
            blocks[k][...] = query[k % each * owned : (k % each + 1) * owned]


def arrange(loc, parts, owned, gate):
    rows = loc.shape[0]
    turns = rows // owned
    channels = parts[0].shape[1]
    block = max(math.gcd(rows, 256), owned)
    all_of = lambda shape: pl.BlockSpec(shape, lambda i: (0, 0))
    out = call(
        functools.partial(arrange_kernel, turns),
        "arrange",
        [jax.ShapeDtypeStruct((rows, channels), BF16)] + [jax.ShapeDtypeStruct((owned, channels), BF16)] * (turns + 1),
        2e6 * rows,
        grid=(rows // block,),
        in_specs=[pl.BlockSpec((block, 1), lambda i: (i, 0)), ANYWHERE] + [all_of(v.shape) for v in parts],
        out_specs=[pl.BlockSpec((block, channels), lambda i: (i, 0))] + [all_of((owned, channels))] * (turns + 1),
    )(loc, gate, *parts)
    return out[0], out[1], out[2:]


def match_kernel(turns, spot_ref, note_in, query_ref, *refs):
    positive_ref, matched_ref, note_ref = refs[-3:]
    rows = spot_ref.shape[0]
    landed = jnp.concatenate([ref[...] for ref in refs[:-3]], axis=0)
    table = lax.broadcasted_iota(jnp.int32, (rows, landed.shape[0]), 1) == spot_ref[...]
    positive = jnp.dot(table.astype(F32).astype(BF16), landed, preferred_element_type=F32)
    positive_ref[...] = positive.astype(BF16)
    matched = in_lanes(query_ref[...].astype(F32) * positive, jnp.sum) / SOFTMAX_TEMP
    matched_ref[...] = matched
    note_ref[...] = note_in[...]
    note_ref[turns : turns + 1, :] = matched


def match(spot, landed, query, note, turns):
    rows, channels = query.shape
    return call(
        functools.partial(match_kernel, turns),
        "match",
        [
            jax.ShapeDtypeStruct((rows, channels), BF16),
            jax.ShapeDtypeStruct((1, rows), F32),
            jax.ShapeDtypeStruct(note.shape, F32),
        ],
        3e8,
    )(spot, note, query, *landed)


def sweep(query, keys, total, pushed):
    sub = math.gcd(keys.shape[0], 512)
    for at in range(0, keys.shape[0], sub):
        block = keys[at : at + sub, :]
        logit = lax.dot_general(query, block, NT, preferred_element_type=F32)
        terms = jnp.exp(logit * INV_TEMP - INV_TEMP)
        if total is not None:
            for c in range(0, sub, 128):
                total = total + terms[:, c : c + 128]
        pushed = pushed + jnp.dot(terms.astype(BF16), block, preferred_element_type=F32)
    return total, pushed


def first_kernel(turns, gates, query_ref, keys_ref, *refs):
    total_ref, blocks = refs[gates], refs[gates + 1 :]
    query = query_ref[...]
    total, pushed = sweep(query, keys_ref, jnp.zeros(total_ref.shape, F32), jnp.zeros(query.shape, F32))
    total_ref[...] = total
    rows = query.shape[0] // turns
    for k in range(turns):
        blocks[k][...] = pushed[k * rows : (k + 1) * rows]


def first(query, keys, turns, gates):
    rows, channels = query.shape
    out = call(
        functools.partial(first_kernel, turns, len(gates)),
        "first",
        [jax.ShapeDtypeStruct((rows, 128), F32)] + [jax.ShapeDtypeStruct((rows // turns, channels), F32)] * turns,
        4 * rows * keys.shape[0] * channels,
        room=24,
        in_specs=[pl.BlockSpec(memory_space=pltpu.VMEM)] * 2 + [ANYWHERE] * len(gates),
    )(query, keys, *gates)
    return out[0], out[1:]


def lane_sums(query, keys, total):
    sub = math.gcd(keys.shape[0], 256)
    for at in range(0, keys.shape[0], sub):
        logit = lax.dot_general(query, keys[at : at + sub, :], NT, preferred_element_type=F32)
        terms = jnp.exp(logit * INV_TEMP - INV_TEMP)
        for c in range(0, sub, 128):
            total = total + terms[:, c : c + 128]
    return total


def far_kernel(count, turns, query_ref, total_in, *refs):
    note_ref = refs[-1]
    rows = note_ref.shape[1]
    total = total_in[...]
    for ref in refs[:count]:
        total = lane_sums(query_ref[...], ref, total)
    note_ref[...] = jnp.zeros(note_ref.shape, F32)
    for t in range(turns):
        note_ref[t : t + 1, :] = in_lanes(total[t * rows : (t + 1) * rows], jnp.sum)


def far_totals(query, total, keys, turns):
    lines = -(-(turns + 1) // 8) * 8
    return call(
        functools.partial(far_kernel, len(keys), turns),
        "far",
        jax.ShapeDtypeStruct((lines, query.shape[0] // turns), F32),
        2 * query.shape[0] * sum(k.shape[0] for k in keys) * query.shape[1],
        room=24,
    )(query, total, *keys)


def exponent(size):
    return jnp.ceil(jnp.log2(jnp.maximum(size, 1e-30)))


def last_kernel(k, query_ref, pushed_in, gate_ref, *refs):
    sent_ref = refs[-1]
    pushed = pushed_in[...]
    for ref in refs[:-1]:
        _, pushed = sweep(query_ref[...], ref, None, pushed)
    if k == 0:
        sent_ref[...] = pushed
        return
    size = jnp.abs(pushed)
    wide = size[:, :128]
    for c in range(128, size.shape[1], 128):
        wide = jnp.maximum(wide, size[:, c : c + 128])
    rows = pushed.shape[0]
    scale = jnp.exp2(-exponent(jnp.max(wide, axis=1, keepdims=True))) * STEPS
    sent_ref[:rows, :] = jnp.round(pushed * scale).astype(jnp.int32).astype(jnp.int16)
    power = exponent(in_lanes(wide, jnp.max)).astype(jnp.int32)
    rest = sent_ref.shape[1] - rows
    if rest:
        power = jnp.concatenate([power, jnp.zeros((1, rest), jnp.int32)], axis=1)
    sent_ref[rows:, :] = jnp.broadcast_to(power, (sent_ref.shape[0] - rows, sent_ref.shape[1])).astype(jnp.int16)


def last(query, pushed, keys, k, gate):
    rows, channels = query.shape
    sent = jax.ShapeDtypeStruct((rows + 16, channels), jnp.int16) if k else jax.ShapeDtypeStruct((rows, channels), F32)
    return call(
        functools.partial(last_kernel, k),
        "last",
        sent,
        4 * rows * sum(v.shape[0] for v in keys) * channels,
        in_specs=[pl.BlockSpec(memory_space=pltpu.VMEM)] * 2 + [ANYWHERE] + [pl.BlockSpec(memory_space=pltpu.VMEM)] * len(keys),
    )(query, pushed, gate, *keys)


def settle_kernel(turns, caps, note_ref, matched_ref, most_ref, held_ref, *refs):
    came = refs[: turns - 1]
    loss_ref, total_ref, word_ref = refs[turns - 1 :]
    totals = [note_ref[t : t + 1, :] for t in range(turns)]
    matched = note_ref[turns : turns + 1, :]
    for k in range(1, turns):
        ref = came[k - 1]
        for t in range(turns):
            totals[t] = totals[t] + ref[t ^ k : (t ^ k) + 1, :]
        matched = matched + ref[turns : turns + 1, :]
    total_ref[...] = totals[0]
    loss_ref[...] = jnp.log(totals[0]) + INV_TEMP - matched_ref[...]
    line = INV_TEMP * turns - matched
    for t in range(turns):
        line = line + jnp.log(totals[t])
    over = (jnp.max(most_ref[...]) > caps[0]) | (jnp.max(held_ref[...]) > caps[1])
    word_ref[...] = jnp.zeros(word_ref.shape, F32)
    word_ref[0:1, 0:1] = jnp.sum(line, axis=1, keepdims=True)
    word_ref[1:2, :] = jnp.full((1, word_ref.shape[1]), jnp.where(over, 1.0, 0.0))


def settle(note, matched, most, held, came, turns, caps):
    row = jax.ShapeDtypeStruct((1, note.shape[1]), F32)
    return call(
        functools.partial(settle_kernel, turns, caps),
        "settle",
        [row, row, jax.ShapeDtypeStruct((8, 128), F32)],
        1e8,
    )(note, matched, most, held, *came)


def finish_kernel(count, raw_ref, positive_ref, own_ref, total_ref, *refs):
    grad_ref = refs[-1]
    rows = raw_ref.shape[0]
    scales = [ref[rows : rows + 16, :rows].astype(jnp.int32).astype(F32)[0:1, :] for ref in refs[:count]]
    scales = [jnp.exp2(v) * (1.0 / STEPS) for v in scales]
    fill = -(1 + count) % 128
    turned = jnp.concatenate([total_ref[...]] + scales + [jnp.zeros((fill, rows), F32)], axis=0).T
    pushed = own_ref[...]
    for j in range(count):
        pushed = pushed + refs[j][:rows, :].astype(jnp.int32).astype(F32) * turned[:, j + 1 : j + 2]
    step = (pushed / turned[:, 0:1] - positive_ref[...].astype(F32)) * INV_TEMP
    raw = raw_ref[...].astype(F32)
    scale = lax.rsqrt(jnp.mean(raw * raw, axis=-1, keepdims=True) + EPSILON)
    inner = jnp.mean(step * raw, axis=-1, keepdims=True)
    grad_ref[...] = (step - raw * (scale * scale * inner)) * (scale / math.sqrt(raw.shape[1]))


def finish(raw, positive, own, total, parts):
    rows, channels = own.shape
    all_of = lambda v: pl.BlockSpec(v.shape, lambda i: (0, 0))
    return call(
        functools.partial(finish_kernel, len(parts)),
        "finish",
        jax.ShapeDtypeStruct(own.shape, F32),
        5e8,
        grid=(1,),
        in_specs=[pl.BlockSpec((rows, channels), lambda i: (0, 0))]
        + [all_of(v) for v in (positive, own, total, *parts)],
        out_specs=all_of(own),
    )(raw, positive, own, total, *parts)


def on_device(features, patch_index, positive_index, bank):
    groups, copies = lax.axis_size("bank"), lax.axis_size("dp")
    place = lax.axis_index("bank")
    core = lax.axis_index("dp") % 2
    images, hw_dev, channels = features.shape
    queries_dp = images * patch_index.shape[1]
    owned = queries_dp // groups
    turns = groups // 2
    inner, outer = place % 2, place // 2
    bank_dev = bank.shape[0]
    across = [(b, b ^ 1) for b in range(groups)]
    swap = [(c, c ^ 1) for c in range(copies)]

    def turn(value, k):
        pairs = [(b, b ^ (2 * k)) for b in range(groups)]
        return lax.ppermute(value, "bank", pairs)

    def in_turns(value):
        return [lax.dynamic_index_in_dim(value, outer ^ k, 0, keepdims=False) for k in range(turns)]

    cap = capacity(queries_dp / groups / 2, queries_dp // 2, 4.0)
    own_set, other_set, loc, most, half = pick(features, patch_index, bank, place, core, groups, owned, cap)
    from_side = lax.ppermute(other_set, "bank", across)
    fetched = lax.ppermute(half, "bank", across)
    held_rows = jnp.concatenate([own_set, from_side])
    parts = [held_rows] + [turn(held_rows, k) for k in range(1, turns)]

    cap_pos = capacity(owned / groups, owned, 5.5)
    index = positive_index.reshape(groups, owned)
    holder = index // bank_dev
    mine = holder == place
    order = jnp.arange(owned, dtype=jnp.int32)
    earlier = order[None, :] < order[:, None]
    rank = jnp.sum((mine[:, None, :] & earlier).astype(jnp.int32), axis=2)
    slots = jnp.arange(cap_pos, dtype=jnp.int32)
    chosen = mine[:, None, :] & (rank[:, None, :] == slots[None, :, None])
    listed = jnp.sum(jnp.where(chosen, (index - place * bank_dev)[:, None, :], 0), axis=2)
    rows_out = bank[after(listed, from_side).reshape(-1)].reshape(turns, 2, cap_pos, channels)
    to_side = lax.dynamic_index_in_dim(rows_out, 1 - inner, 1, keepdims=False)
    side_rows = lax.ppermute(to_side, "bank", across)

    loc = lax.dynamic_index_in_dim(loc.reshape(turns, 2, owned), inner, 1, keepdims=False)
    loc = jnp.stack(in_turns(loc)).reshape(turns * owned, 1)
    query, raw, blocks = arrange(loc, parts, owned, to_side)
    fetched = after(fetched, query)
    far_keys = [fetched, lax.ppermute(fetched, "dp", swap)]
    total, pushed = first(query, bank, turns, [])
    packed = pack(place, rows_out, side_rows, [total])
    landed = [packed[0]] + [turn(packed[k], k) for k in range(1, turns)]

    own_holder = lax.dynamic_index_in_dim(holder, place, 0, keepdims=False)
    same = own_holder[None, :] == own_holder[:, None]
    own_rank = jnp.sum((same & earlier).astype(jnp.int32), axis=1)
    away = outer ^ (own_holder // 2)
    spot = (away * 2 + (own_holder + inner) % 2) * cap_pos + own_rank
    counts = jnp.sum((holder[:, None, :] == jnp.arange(groups, dtype=jnp.int32)[None, :, None]).astype(F32), axis=2)

    note = far_totals(query, total, far_keys, turns)
    positive, matched, note = match(spot[:, None], landed, blocks[0], note, turns)

    came = [turn(note, k) for k in range(1, turns)]

    def over(word, a, b):
        pairs = [(c * groups + p, (c ^ a) * groups + (p ^ b)) for c in range(copies) for p in range(groups)]
        return lax.ppermute(word, ("dp", "bank"), pairs)

    moved = [None] * turns
    order = list(range(2, turns)) + [1]

    def send_next(gate):
        if order:
            k = order.pop(0)
            sent = last(blocks[k], pushed[k], far_keys, k, gate)
            moved[k] = turn(sent, k)

    send_next(note)
    loss, total, word = settle(note, matched, most, counts, came, turns, (cap, cap_pos))
    send_next(word)
    word = word + over(word, 1, 0)
    send_next(word)
    far_words = [over(word, a, b) for a in range(0, copies, 2) for b in range(2) if a or b]
    while order:
        send_next(word)
    own = last(blocks[0], pushed[0], far_keys, 0, word)
    moved = moved[1:]
    for far_word in far_words:
        word = word + far_word
    grad = finish(raw, positive, own, total, moved)
    mean_loss = word[0, 0] * (1.0 / (queries_dp * copies))
    return lax.cond(
        word[1, 0] > 0.5,
        lambda *a: plain(*a[:4]),
        lambda *a: a[4:],
        features,
        patch_index,
        positive_index,
        bank,
        loss.reshape(owned),
        grad,
        mean_loss,
    )


def solution(mesh):
    in_specs = (P("dp", "bank", None), P("dp", None), P("dp"), P("bank", None))
    out_specs = (P(("dp", "bank")), P(("dp", "bank"), None), P())
    turns = mesh.shape["bank"] // 2
    paired = turns > 1 and turns & (turns - 1) == 0 and mesh.shape["bank"] % 2 == 0
    copies = mesh.shape["dp"]
    paired = paired and copies > 1 and copies & (copies - 1) == 0
    return jax.shard_map(
        on_device if paired else plain, mesh=mesh, in_specs=in_specs, out_specs=out_specs, check_vma=False
    )
```

time: 272 us -> 82 us (0.30)
  waiting for transfers between devices: 114 us -> 20.2 us
  blocking collectives: 73.6 us -> 0 us
  matrix products: 44 us -> 0 us
  Pallas kernels: 0 us -> 25.6 us
  starting transfers between devices: 0.12 us -> 25.3 us
  between operations: 16.3 us -> 2.94 us
  other arithmetic: 10.6 us -> 1.15 us
  local copies, waits for them, and re-layouts: 12.6 us -> 5.86 us
    psum x1 -> x0, waiting for transfers between devices: 95.7 us -> none  [on_device(): raw_all = lax.psum(term, 'bank')]
    dot_general x17 -> x0, matrix products: 44 us -> none  [the longest x8 22.7 us: visit(): jnp.dot(exponent_terms.astype(jnp.bfloat16), bank_block, preferred_elemen...]
    psum x1 -> x0, blocking collectives: 37.3 us -> none  [on_device(): mean_loss = lax.psum(jnp.sum(loss), ('dp', 'bank')) / count_all]
    unnamed x1 -> x0, blocking collectives: 36.3 us -> none
    pallas_call x0 -> x14, Pallas kernels: none -> 25.6 us  [the longest x1 7.7 us: first(): call(functools.partial(first_kernel, turns, len(gates)), 'first', [jax.Sh...]
    ppermute x0 -> x20, starting transfers between devices: none -> 25.3 us  [the longest x12 16.6 us: turn(): return lax.ppermute(value, 'bank', pairs)]
    ppermute x0 -> x20, waiting for transfers between devices: none -> 20.2 us  [the longest x12 16 us: turn(): return lax.ppermute(value, 'bank', pairs)]
    reduce_scatter x2 -> x0, waiting for transfers between devices: 17.7 us -> none  [the longest x1 17.7 us: on_device(): lax.psum_scatter(weighted_negatives, 'bank', scatter_dimension=0, tiled=T...]
  transfers between devices with their start and end apart: 3 -> 20, of which waited for: 2 -> 7; matrix products, arithmetic and copies ran while one was open for 20% -> 7% of each run, Pallas kernels for 0% -> 25%
where the time goes in v2:
time: 82 us; the launch traced here: 81.8 us
  Pallas kernels  25.6 us (31%)
  starting transfers between devices  25.3 us (31%)
  waiting for transfers between devices  20.2 us (25%)
  local copies, waits for them, and re-layouts  5.86 us (7%)
  between operations  2.94 us (4%)
  other arithmetic  1.15 us (1%)
    ppermute x12, starting transfers between devices, turn(): return lax.ppermute(value, 'bank', pairs)  16.6 us
    ppermute x12, waiting for transfers between devices, turn(): return lax.ppermute(value, 'bank', pairs)  16 us
    pallas_call x1, Pallas kernels, first(): call(functools.partial(first_kernel, turns, len(gates)), 'first', [jax.Sh...  7.7 us
    pallas_call x4, Pallas kernels, last(): call(functools.partial(last_kernel, k), 'last', sent, 4 * rows * sum((v.s...  6.05 us
    pallas_call x1, Pallas kernels, pick(): call(functools.partial(pick_kernel, groups, owned, cap), 'pick', [jax.Sha...  4.58 us
    ppermute x4, starting transfers between devices, over(): return lax.ppermute(word, ('dp', 'bank'), pairs)  3.78 us
    pallas_call x1, Pallas kernels, far_totals(): call(functools.partial(far_kernel, len(keys), turns), 'far', jax.ShapeDty...  3.65 us
    gather x1, local copies, waits for them, and re-layouts, on_device(): bank[after(listed, from_side).reshape(-1)]  3.42 us
  transfers between devices with their start and end apart: 20, of which 7 were waited for; matrix products, arithmetic and copies ran while one was open for 7% of the time, Pallas kernels for 25%

profile of v2, /device:TPU:0, one launch (start us, length us, event | category | flops | bytes accessed | tf_op | source)
XLA Modules:
  0.0 81.8 jit_solution(8233246397288897463)
XLA Ops:
  0.7 4.6 %pick.1 = (bf16[176,256]{1,0:T(8,128)(2,1)S(1)}, bf16[176,256]{1,0:T(8,128)(2,1)S(1)}, s32[16,128]{1,0:T(8,128)S(1)}, f32[8,128]{1,0:T(8,128)S(1)}, bf16[2048,256]{1,0:T(8,128)(2,1)}) custom-call(s32[2]{0:T(128)S(1)} %pad_add_fusion.place_ref, s32[16,128]{1,0:T(8,128)} %pos_ref.1, bf16[16,64,256]{2,1,0:T(8,128)(2,1)} %feat_ref.1, bf16[4096,256]{1,0:T(8,128)(2,1)} %keys_ref.1), custom_call_target="tpu_custom_call" | custom-call | flops 3000000000 | bytes 1048576 | tf_op jit(solution)/shard_map/pick/pallas_call | solution.py:180
  5.3 3.0 %collective-permute-start.7 = (bf16[176,256]{1,0:T(8,128)(2,1)S(1)}, bf16[176,256]{1,0:T(8,128)(2,1)S(1)}, u32[]{:S(2)}, u32[]{:S(2)}) collective-permute-start(bf16[176,256]{1,0:T(8,128)(2,1)S(1)} %get-tuple-element.311), channel_id=1, source_target_pairs={{0,1},{1,0},{2,3},{3,2},{4,5},{5,4},{6,7},{7,6},{8,9},{9,8},{10,11... | collective-permute-start | bytes 270344 | tf_op jit(solution)/shard_map/ppermute | solution.py:486
  8.3 0.1 collective-permute-start.11
  8.5 0.3 convert_reduce_fusion
  8.9 0.2 copy.42
  9.2 0.2 select_reduce_fusion.refs_0_
  9.4 1.9 %collective-permute-done.7.refs_1_ = bf16[176,256]{1,0:T(8,128)(2,1)S(1)} collective-permute-done((bf16[176,256]{1,0:T(8,128)(2,1)S(1)}, bf16[176,256]{1,0:T(8,128)(2,1)S(1)}, u32[]{:S(2)}, u32[]{:S(2)}) %collective-permute-start.7) | collective-permute-done | bytes 90144 | tf_op jit(solution)/shard_map/ppermute | solution.py:486
  11.3 2.3 %collective-permute-start.8 = (bf16[352,256]{1,0:T(8,128)(2,1)S(1)}, bf16[352,256]{1,0:T(8,128)(2,1)S(1)}, u32[]{:S(2)}, u32[]{:S(2)}) collective-permute-start(bf16[352,256]{1,0:T(8,128)(2,1)S(1)} %constant_dynamic-update-slice_fusion.refs_0_), channel_id=1, source_target_pairs={{0,2},{1,3},{2,0},{3,1},{4,6},{5,7},{6,4},{7,5},{8,10},{9,11},{10,... | collective-permute-start | bytes 540680 | tf_op jit(solution)/shard_map/ppermute | solution.py:479
  13.7 2.6 %collective-permute-start.9 = (bf16[352,256]{1,0:T(8,128)(2,1)S(1)}, bf16[352,256]{1,0:T(8,128)(2,1)S(1)}, u32[]{:S(2)}, u32[]{:S(2)}) collective-permute-start(bf16[352,256]{1,0:T(8,128)(2,1)S(1)} %constant_dynamic-update-slice_fusion.refs_0_), channel_id=1, source_target_pairs={{0,4},{1,5},{2,6},{3,7},{4,0},{5,1},{6,2},{7,3},{8,12},{9,13},{10,... | collective-permute-start | bytes 540680 | tf_op jit(solution)/shard_map/ppermute | solution.py:479
  16.4 3.4 %gather_fusion.1 = bf16[512,256]{1,0:T(8,128)(2,1)S(1)} fusion(bf16[4096,256]{1,0:T(8,128)(2,1)} %keys_ref.1, s32[1024]{0:T(1024)S(1)} %pad_clamp_fusion), kind=kCustom, calls=%fused_computation.1 | custom fusion | bytes 526336 | tf_op jit(solution)/shard_map/gather | solution.py:501
  19.8 8.6 %collective-permute-done.9.refs_2_ = bf16[352,256]{1,0:T(8,128)(2,1)S(1)} collective-permute-done((bf16[352,256]{1,0:T(8,128)(2,1)S(1)}, bf16[352,256]{1,0:T(8,128)(2,1)S(1)}, u32[]{:S(2)}, u32[]{:S(2)}) %collective-permute-start.9) | collective-permute-done | bytes 180256 | tf_op jit(solution)/shard_map/ppermute | solution.py:479
  28.4 2.6 %arrange.1 = (bf16[1024,256]{1,0:T(8,128)(2,1)S(1)}, bf16[256,256]{1,0:T(8,128)(2,1)S(1)}, bf16[256,256]{1,0:T(8,128)(2,1)S(1)}, bf16[256,256]{1,0:T(8,128)(2,1)...) custom-call(s32[1024,1]{1,0:T(8,128)S(1)} %bitcast.34, ...), custom_call_target="tpu_custom_call" | custom-call | flops 2048000000 | bytes 1048576 | tf_op jit(solution)/shard_map/arrange/pallas_call | solution.py:256
  31.1 2.3 %collective-permute-done.11.refs_0_ = bf16[2048,256]{1,0:T(8,128)(2,1)S(1)} collective-permute-done((bf16[2048,256]{1,0:T(8,128)(2,1)}, bf16[2048,256]{1,0:T(8,128)(2,1)S(1)}, u32[]{:S(2)}, u32[]{:S(2)}) %collective-permute-start.11) | collective-permute-done | bytes 1048608 | tf_op jit(solution)/shard_map/ppermute | solution.py:487
  33.5 0.2 convert_reduce_fusion.1
  33.6 0.1 copy.33
  33.8 0.1 copy.27
  33.9 0.1 convert_reduce_fusion.2.held_ref
  34.0 0.2 fusion.24.spot_ref
  34.2 1.8 %collective-permute-start.13 = (bf16[4,64,256]{2,1,0:T(8,128)(2,1)S(1)}, bf16[4,64,256]{2,1,0:T(8,128)(2,1)S(1)}, u32[]{:S(2)}, u32[]{:S(2)}) collective-permute-start(bf16[4,64,256]{2,1,0:T(8,128)(2,1)S(1)} %dynamic-slice_bitcast_fusion.gate_ref), channel_id=1, source_target_pairs={{0,1},{1,0},{2,3},{3,2},{4,5},{5,4},{6,7},{7,6},{8,9},{9,8},{10,11... | collective-permute-start | bytes 393224 | tf_op jit(solution)/shard_map/ppermute | solution.py:503
  36.0 7.7 %first.1 = (f32[1024,128]{1,0:T(8,128)S(1)}, f32[256,256]{1,0:T(8,128)S(1)}, f32[256,256]{1,0:T(8,128)S(1)}, f32[256,256]{1,0:T(8,128)S(1)}, f32[256,256]{1,0:T(8,128)S(1)}) custom-call(bf16[1024,256]{1,0:T(8,128)(2,1)S(1)} %get-tuple-element.313.query_ref.refs_1_, bf16[4096,256]{1,0:T(8,128)(2,1)} %keys_ref.1), custom_call_target="tpu_custom_call" | custom-call | flops 4294967296 | bytes 1048576 | tf_op jit(solution)/shard_map/first/pallas_call | solution.py:320
  43.7 1.6 %collective-permute-start.14 = (bf16[128,256]{1,0:T(8,128)(2,1)S(1)}, bf16[128,256]{1,0:T(8,128)(2,1)S(1)}, u32[]{:S(2)}, u32[]{:S(2)}) collective-permute-start(bf16[128,256]{1,0:T(8,128)(2,1)S(1)} %get-tuple-element.318), channel_id=1, source_target_pairs={{0,2},{1,3},{2,0},{3,1},{4,6},{5,7},{6,4},{7,5},{8,10},{9,11},{10,... | collective-permute-start | bytes 196616 | tf_op jit(solution)/shard_map/ppermute | solution.py:479
  45.4 2.6 %collective-permute-start.15 = (bf16[128,256]{1,0:T(8,128)(2,1)S(1)}, bf16[128,256]{1,0:T(8,128)(2,1)S(1)}, u32[]{:S(2)}, u32[]{:S(2)}) collective-permute-start(bf16[128,256]{1,0:T(8,128)(2,1)S(1)} %get-tuple-element.319), channel_id=1, source_target_pairs={{0,4},{1,5},{2,6},{3,7},{4,0},{5,1},{6,2},{7,3},{8,12},{9,13},{10,... | collective-permute-start | bytes 196616 | tf_op jit(solution)/shard_map/ppermute | solution.py:479
  48.0 0.2 collective-permute-start.16
  48.2 3.6 %far.1.note_in = f32[8,256]{1,0:T(8,128)S(1)} custom-call(bf16[1024,256]{1,0:T(8,128)(2,1)S(1)} %get-tuple-element.313.query_ref.refs_1_, f32[1024,128]{1,0:T(8,128)S(1)} %get-tuple-element.314.total_in.refs_0_, bf16[2048,256]{1,0:T(8,128)(2,1)S(1)} %after.3.refs_0_, bf16[2048,256]{1,0:T(8,128)(2,1)S(1)} %collective-permute-done.12.refs_1_), custom_call_target="tpu_custom_call" | custom-call | flops 2147483648 | bytes 1048576 | tf_op jit(solution)/shard_map/far/pallas_call | solution.py:354
  51.9 1.1 %collective-permute-done.15.refs_2_ = bf16[128,256]{1,0:T(8,128)(2,1)S(1)} collective-permute-done((bf16[128,256]{1,0:T(8,128)(2,1)S(1)}, bf16[128,256]{1,0:T(8,128)(2,1)S(1)}, u32[]{:S(2)}, u32[]{:S(2)}) %collective-permute-start.15) | collective-permute-done | bytes 65568 | tf_op jit(solution)/shard_map/ppermute | solution.py:479
  53.0 1.2 %collective-permute-done.16.refs_3_ = bf16[128,256]{1,0:T(8,128)(2,1)S(1)} collective-permute-done((bf16[128,256]{1,0:T(8,128)(2,1)S(1)}, bf16[128,256]{1,0:T(8,128)(2,1)S(1)}, u32[]{:S(2)}, u32[]{:S(2)}) %collective-permute-start.16) | collective-permute-done | bytes 65568 | tf_op jit(solution)/shard_map/ppermute | solution.py:479
  54.2 0.4 match.1
  54.5 1.0 %collective-permute-start.17 = (f32[8,256]{1,0:T(8,128)S(1)}, f32[8,256]{1,0:T(8,128)S(1)}, u32[]{:S(2)}, u32[]{:S(2)}) collective-permute-start(f32[8,256]{1,0:T(8,128)S(1)} %get-tuple-element.321.note_ref.gate_ref), channel_id=1, source_target_pairs={{0,2},{1,3},{2,0},{3,1},{4,6},{5,7},{6,4},{7,5},{8,10},{9,11},{10,... | collective-permute-start | bytes 24584 | tf_op jit(solution)/shard_map/ppermute | solution.py:479
  55.5 1.7 %collective-permute-start.18 = (f32[8,256]{1,0:T(8,128)S(1)}, f32[8,256]{1,0:T(8,128)S(1)}, u32[]{:S(2)}, u32[]{:S(2)}) collective-permute-start(f32[8,256]{1,0:T(8,128)S(1)} %get-tuple-element.321.note_ref.gate_ref), channel_id=1, source_target_pairs={{0,4},{1,5},{2,6},{3,7},{4,0},{5,1},{6,2},{7,3},{8,12},{9,13},{10,... | collective-permute-start | bytes 24584 | tf_op jit(solution)/shard_map/ppermute | solution.py:479
  57.2 1.8 %collective-permute-start.19 = (f32[8,256]{1,0:T(8,128)S(1)}, f32[8,256]{1,0:T(8,128)S(1)}, u32[]{:S(2)}, u32[]{:S(2)}) collective-permute-start(f32[8,256]{1,0:T(8,128)S(1)} %get-tuple-element.321.note_ref.gate_ref), channel_id=1, source_target_pairs={{0,6},{1,7},{2,4},{3,5},{4,2},{5,3},{6,0},{7,1},{8,14},{9,15},{10,... | collective-permute-start | bytes 24584 | tf_op jit(solution)/shard_map/ppermute | solution.py:479
  59.0 1.5 %last.6 = s16[272,256]{1,0:T(8,128)(2,1)S(1)} custom-call(bf16[256,256]{1,0:T(8,128)(2,1)S(1)} %copy-done.5, f32[256,256]{1,0:T(8,128)S(1)} %get-tuple-element.333.pushed_in, f32[8,256]{1,0:T(8,128)S(1)} %get-tuple-element.321.note_ref.gate_ref, bf16[2048,256]{1,0:T(8,128)(2,1)S(1)} %after.3.refs_0_, bf16[2048,256]{1,0:T(8,128)(2,1)S(1)} %collective-permute-done.12.refs_1_), custom_call_target="tpu_custom_call" | custom-call | flops 1073741824 | bytes 1048576 | tf_op jit(solution)/shard_map/last/pallas_call | solution.py:392
  60.6 1.0 %collective-permute-start.25 = (s16[272,256]{1,0:T(8,128)(2,1)S(1)}, s16[272,256]{1,0:T(8,128)(2,1)S(1)}, u32[]{:S(2)}, u32[]{:S(2)}) collective-permute-start(s16[272,256]{1,0:T(8,128)(2,1)S(1)} %last.6), channel_id=1, source_target_pairs={{0,4},{1,5},{2,6},{3,7},{4,0},{5,1},{6,2},{7,3},{8,12},{9,13},{10,... | collective-permute-start | bytes 417800 | tf_op jit(solution)/shard_map/ppermute | solution.py:479
  61.6 1.3 %collective-permute-done.19.refs_2_ = f32[8,256]{1,0:T(8,128)S(1)} collective-permute-done((f32[8,256]{1,0:T(8,128)S(1)}, f32[8,256]{1,0:T(8,128)S(1)}, u32[]{:S(2)}, u32[]{:S(2)}) %collective-permute-start.19) | collective-permute-done | bytes 8224 | tf_op jit(solution)/shard_map/ppermute | solution.py:479
  62.9 0.1 settle.1
  63.0 0.3 collective-permute-start.20
  63.3 1.6 %last.7 = s16[272,256]{1,0:T(8,128)(2,1)S(1)} custom-call(bf16[256,256]{1,0:T(8,128)(2,1)S(1)} %copy-done.9, f32[256,256]{1,0:T(8,128)S(1)} %get-tuple-element.335.pushed_in, f32[8,128]{1,0:T(8,128)S(1)} %get-tuple-element.324.gate_ref, bf16[2048,256]{1,0:T(8,128)(2,1)S(1)} %after.3.refs_0_, bf16[2048,256]{1,0:T(8,128)(2,1)S(1)} %collective-permute-done.12.refs_1_), custom_call_target="tpu_custom_call" | custom-call | flops 1073741824 | bytes 1048576 | tf_op jit(solution)/shard_map/last/pallas_call | solution.py:392
  64.9 1.7 %collective-permute-start.26 = (s16[272,256]{1,0:T(8,128)(2,1)S(1)}, s16[272,256]{1,0:T(8,128)(2,1)S(1)}, u32[]{:S(2)}, u32[]{:S(2)}) collective-permute-start(s16[272,256]{1,0:T(8,128)(2,1)S(1)} %last.7), channel_id=1, source_target_pairs={{0,6},{1,7},{2,4},{3,5},{4,2},{5,3},{6,0},{7,1},{8,14},{9,15},{10,... | collective-permute-start | bytes 417800 | tf_op jit(solution)/shard_map/ppermute | solution.py:479
  66.6 1.7 %collective-permute-start.23 = (f32[8,128]{1,0:T(8,128)S(1)}, f32[8,128]{1,0:T(8,128)S(1)}, u32[]{:S(2)}, u32[]{:S(2)}) collective-permute-start(f32[8,128]{1,0:T(8,128)S(1)} %add.279.gate_ref), channel_id=1, source_target_pairs={{0,17},{1,16},{2,19},{3,18},{4,21},{5,20},{6,23},{7,22},{8,25},{9,... | collective-permute-start | bytes 12296 | tf_op jit(solution)/shard_map/ppermute | solution.py:528
  68.2 0.5 collective-permute-start.22
  68.7 1.3 %collective-permute-start.21 = (f32[8,128]{1,0:T(8,128)S(1)}, f32[8,128]{1,0:T(8,128)S(1)}, u32[]{:S(2)}, u32[]{:S(2)}) collective-permute-start(f32[8,128]{1,0:T(8,128)S(1)} %add.279.gate_ref), channel_id=1, source_target_pairs={{0,1},{1,0},{2,3},{3,2},{4,5},{5,4},{6,7},{7,6},{8,9},{9,8},{10,11... | collective-permute-start | bytes 12296 | tf_op jit(solution)/shard_map/ppermute | solution.py:528
  70.1 1.4 %last.4.own_ref = f32[256,256]{1,0:T(8,128)S(1)} custom-call(bf16[256,256]{1,0:T(8,128)(2,1)S(1)} %copy-done.1, f32[256,256]{1,0:T(8,128)S(1)} %get-tuple-element.328.pushed_in, f32[8,128]{1,0:T(8,128)S(1)} %add.279.gate_ref, bf16[2048,256]{1,0:T(8,128)(2,1)S(1)} %after.3.refs_0_, bf16[2048,256]{1,0:T(8,128)(2,1)S(1)} %collective-permute-done.12.refs_1_), custom_call_target="tpu_custom_call" | custom-call | flops 1073741824 | bytes 1048576 | tf_op jit(solution)/shard_map/last/pallas_call | solution.py:392
  71.5 1.6 %last.5 = s16[272,256]{1,0:T(8,128)(2,1)S(1)} custom-call(bf16[256,256]{1,0:T(8,128)(2,1)S(1)} %copy-done.7, f32[256,256]{1,0:T(8,128)S(1)} %get-tuple-element.331.pushed_in, f32[8,128]{1,0:T(8,128)S(1)} %add.279.gate_ref, bf16[2048,256]{1,0:T(8,128)(2,1)S(1)} %after.3.refs_0_, bf16[2048,256]{1,0:T(8,128)(2,1)S(1)} %collective-permute-done.12.refs_1_), custom_call_target="tpu_custom_call" | custom-call | flops 1073741824 | bytes 1048576 | tf_op jit(solution)/shard_map/last/pallas_call | solution.py:392
  73.2 0.5 slice.10
  74.4 3.8 %collective-permute-done.24.refs_0_ = s16[272,256]{1,0:T(8,128)(2,1)S(1)} collective-permute-done((s16[272,256]{1,0:T(8,128)(2,1)S(1)}, s16[272,256]{1,0:T(8,128)(2,1)S(1)}, u32[]{:S(2)}, u32[]{:S(2)}) %collective-permute-start.24) | collective-permute-done | bytes 139296 | tf_op jit(solution)/shard_map/ppermute | solution.py:479
  78.2 0.5 finish.1
  78.7 1.2 %conditional.1 = (f32[256,256]{1,0:T(8,128)S(1)}, f32[256]{0:T(256)S(1)}, f32[]{:T(128)}) conditional(s32[]{:T(128)} %bitcast.16, (f32[1,256]{1,0:T(1,128)S(1)}, f32[8,128]{1,0:T(8,128)S(1)}, f32[256,256]{1,0:T(8,128)S(1)}) %tuple.181, (s32[16,128]{1,0:T(8,128)S(1)}, bf16[16,64,256]{2,1,0:T(8,128)(2,1)S(1)}, bf16[4096,256]{1,0:T(8,128)(2,1)}, ...), branch_computations={%region_4.5_spmd, %region_5.28_spmd} | conditional | flops 1156026368 | bytes 178445888 | solution.py:553
  78.8 0.5 slice.7
  80.0 0.7 copy-done.23
  (67 shorter events, 0.5 us)
Async XLA Ops:
  0.7 7.7 %copy-start.21 = (s32[2048]{0:T(1024)S(1)}, s32[2048]{0:T(1024)}, u32[]{:S(2)}) copy-start(s32[2048]{0:T(1024)} %param.24) | copy-start | bytes 24580
  5.3 6.0 %collective-permute-start.7 = (bf16[176,256]{1,0:T(8,128)(2,1)S(1)}, bf16[176,256]{1,0:T(8,128)(2,1)S(1)}, u32[]{:S(2)}, u32[]{:S(2)}) collective-permute-start(bf16[176,256]{1,0:T(8,128)(2,1)S(1)} %get-tuple-element.311), channel_id=1, source_target_pairs={{0,1},{1,0},{2,3},{3,2},{4,5},{5,4},{6,7},{7,6},{8,9},{9,8},{10,11... | collective-permute-start | bytes 270344 | tf_op jit(solution)/shard_map/ppermute | solution.py:486
  8.3 25.1 %collective-permute-start.11 = (bf16[2048,256]{1,0:T(8,128)(2,1)}, bf16[2048,256]{1,0:T(8,128)(2,1)S(1)}, u32[]{:S(2)}, u32[]{:S(2)}) collective-permute-start(bf16[2048,256]{1,0:T(8,128)(2,1)} %get-tuple-element.315), channel_id=1, source_target_pairs={{0,1},{1,0},{2,3},{3,2},{4,5},{5,4},{6,7},{7,6},{8,9},{9,8},{10,11... | collective-permute-start | bytes 3145736 | tf_op jit(solution)/shard_map/ppermute | solution.py:487
  11.3 8.5 %collective-permute-start.8 = (bf16[352,256]{1,0:T(8,128)(2,1)S(1)}, bf16[352,256]{1,0:T(8,128)(2,1)S(1)}, u32[]{:S(2)}, u32[]{:S(2)}) collective-permute-start(bf16[352,256]{1,0:T(8,128)(2,1)S(1)} %constant_dynamic-update-slice_fusion.refs_0_), channel_id=1, source_target_pairs={{0,2},{1,3},{2,0},{3,1},{4,6},{5,7},{6,4},{7,5},{8,10},{9,11},{10,... | collective-permute-start | bytes 540680 | tf_op jit(solution)/shard_map/ppermute | solution.py:479
  13.7 14.7 %collective-permute-start.9 = (bf16[352,256]{1,0:T(8,128)(2,1)S(1)}, bf16[352,256]{1,0:T(8,128)(2,1)S(1)}, u32[]{:S(2)}, u32[]{:S(2)}) collective-permute-start(bf16[352,256]{1,0:T(8,128)(2,1)S(1)} %constant_dynamic-update-slice_fusion.refs_0_), channel_id=1, source_target_pairs={{0,4},{1,5},{2,6},{3,7},{4,0},{5,1},{6,2},{7,3},{8,12},{9,13},{10,... | collective-permute-start | bytes 540680 | tf_op jit(solution)/shard_map/ppermute | solution.py:479
  16.3 12.2 %collective-permute-start.10 = (bf16[352,256]{1,0:T(8,128)(2,1)S(1)}, bf16[352,256]{1,0:T(8,128)(2,1)S(1)}, u32[]{:S(2)}, u32[]{:S(2)}) collective-permute-start(bf16[352,256]{1,0:T(8,128)(2,1)S(1)} %constant_dynamic-update-slice_fusion.refs_0_), channel_id=1, source_target_pairs={{0,6},{1,7},{2,4},{3,5},{4,2},{5,3},{6,0},{7,1},{8,14},{9,15},{10,... | collective-permute-start | bytes 540680 | tf_op jit(solution)/shard_map/ppermute | solution.py:479
  31.0 2.4 %copy-start = (bf16[256,256]{1,0:T(8,128)(2,1)}, bf16[256,256]{1,0:T(8,128)(2,1)S(1)}, u32[]{:S(2)}) copy-start(bf16[256,256]{1,0:T(8,128)(2,1)S(1)} %get-tuple-element.316.query_ref) | copy-start | bytes 393220
  31.1 2.4 %copy-start.2 = (bf16[256,256]{1,0:T(8,128)(2,1)}, bf16[256,256]{1,0:T(8,128)(2,1)S(1)}, u32[]{:S(2)}) copy-start(bf16[256,256]{1,0:T(8,128)(2,1)S(1)} %get-tuple-element.326.raw_ref) | copy-start | bytes 393220
  31.1 2.4 %copy-start.4 = (bf16[256,256]{1,0:T(8,128)(2,1)}, bf16[256,256]{1,0:T(8,128)(2,1)S(1)}, u32[]{:S(2)}) copy-start(bf16[256,256]{1,0:T(8,128)(2,1)S(1)} %get-tuple-element.332.query_ref) | copy-start | bytes 393220
  31.1 2.4 %copy-start.6 = (bf16[256,256]{1,0:T(8,128)(2,1)}, bf16[256,256]{1,0:T(8,128)(2,1)S(1)}, u32[]{:S(2)}) copy-start(bf16[256,256]{1,0:T(8,128)(2,1)S(1)} %get-tuple-element.330.query_ref) | copy-start | bytes 393220
  31.1 2.4 %copy-start.8 = (bf16[256,256]{1,0:T(8,128)(2,1)}, bf16[256,256]{1,0:T(8,128)(2,1)S(1)}, u32[]{:S(2)}) copy-start(bf16[256,256]{1,0:T(8,128)(2,1)S(1)} %get-tuple-element.334.query_ref) | copy-start | bytes 393220
  33.4 14.8 %collective-permute-start.12 = (bf16[2048,256]{1,0:T(8,128)(2,1)S(1)}, bf16[2048,256]{1,0:T(8,128)(2,1)S(1)}, u32[]{:S(2)}, u32[]{:S(2)}) collective-permute-start(bf16[2048,256]{1,0:T(8,128)(2,1)S(1)} %after.3.refs_0_), channel_id=1, source_target_pairs={{0,8},{8,0},{16,24},{24,16},{1,9},{9,1},{17,25},{25,17},{2,10},{10... | collective-permute-start | bytes 3145736 | tf_op jit(solution)/shard_map/ppermute | solution.py:509
  34.2 9.5 %collective-permute-start.13 = (bf16[4,64,256]{2,1,0:T(8,128)(2,1)S(1)}, bf16[4,64,256]{2,1,0:T(8,128)(2,1)S(1)}, u32[]{:S(2)}, u32[]{:S(2)}) collective-permute-start(bf16[4,64,256]{2,1,0:T(8,128)(2,1)S(1)} %dynamic-slice_bitcast_fusion.gate_ref), channel_id=1, source_target_pairs={{0,1},{1,0},{2,3},{3,2},{4,5},{5,4},{6,7},{7,6},{8,9},{9,8},{10,11... | collective-permute-start | bytes 393224 | tf_op jit(solution)/shard_map/ppermute | solution.py:503
  43.7 8.1 %collective-permute-start.14 = (bf16[128,256]{1,0:T(8,128)(2,1)S(1)}, bf16[128,256]{1,0:T(8,128)(2,1)S(1)}, u32[]{:S(2)}, u32[]{:S(2)}) collective-permute-start(bf16[128,256]{1,0:T(8,128)(2,1)S(1)} %get-tuple-element.318), channel_id=1, source_target_pairs={{0,2},{1,3},{2,0},{3,1},{4,6},{5,7},{6,4},{7,5},{8,10},{9,11},{10,... | collective-permute-start | bytes 196616 | tf_op jit(solution)/shard_map/ppermute | solution.py:479
  45.4 7.6 %collective-permute-start.15 = (bf16[128,256]{1,0:T(8,128)(2,1)S(1)}, bf16[128,256]{1,0:T(8,128)(2,1)S(1)}, u32[]{:S(2)}, u32[]{:S(2)}) collective-permute-start(bf16[128,256]{1,0:T(8,128)(2,1)S(1)} %get-tuple-element.319), channel_id=1, source_target_pairs={{0,4},{1,5},{2,6},{3,7},{4,0},{5,1},{6,2},{7,3},{8,12},{9,13},{10,... | collective-permute-start | bytes 196616 | tf_op jit(solution)/shard_map/ppermute | solution.py:479
  48.0 6.2 %copy-start.1 = (bf16[256,256]{1,0:T(8,128)(2,1)S(1)}, bf16[256,256]{1,0:T(8,128)(2,1)}, u32[]{:S(2)}) copy-start(bf16[256,256]{1,0:T(8,128)(2,1)} %copy-done) | copy-start | bytes 393220
  48.0 11.0 %copy-start.5 = (bf16[256,256]{1,0:T(8,128)(2,1)S(1)}, bf16[256,256]{1,0:T(8,128)(2,1)}, u32[]{:S(2)}) copy-start(bf16[256,256]{1,0:T(8,128)(2,1)} %copy-done.4) | copy-start | bytes 393220
  48.0 6.2 %collective-permute-start.16 = (bf16[128,256]{1,0:T(8,128)(2,1)S(1)}, bf16[128,256]{1,0:T(8,128)(2,1)S(1)}, u32[]{:S(2)}, u32[]{:S(2)}) collective-permute-start(bf16[128,256]{1,0:T(8,128)(2,1)S(1)} %get-tuple-element.320), channel_id=1, source_target_pairs={{0,6},{1,7},{2,4},{3,5},{4,2},{5,3},{6,0},{7,1},{8,14},{9,15},{10,... | collective-permute-start | bytes 196616 | tf_op jit(solution)/shard_map/ppermute | solution.py:479
  54.5 7.0 %collective-permute-start.17 = (f32[8,256]{1,0:T(8,128)S(1)}, f32[8,256]{1,0:T(8,128)S(1)}, u32[]{:S(2)}, u32[]{:S(2)}) collective-permute-start(f32[8,256]{1,0:T(8,128)S(1)} %get-tuple-element.321.note_ref.gate_ref), channel_id=1, source_target_pairs={{0,2},{1,3},{2,0},{3,1},{4,6},{5,7},{6,4},{7,5},{8,10},{9,11},{10,... | collective-permute-start | bytes 24584 | tf_op jit(solution)/shard_map/ppermute | solution.py:479
  55.5 6.1 %collective-permute-start.18 = (f32[8,256]{1,0:T(8,128)S(1)}, f32[8,256]{1,0:T(8,128)S(1)}, u32[]{:S(2)}, u32[]{:S(2)}) collective-permute-start(f32[8,256]{1,0:T(8,128)S(1)} %get-tuple-element.321.note_ref.gate_ref), channel_id=1, source_target_pairs={{0,4},{1,5},{2,6},{3,7},{4,0},{5,1},{6,2},{7,3},{8,12},{9,13},{10,... | collective-permute-start | bytes 24584 | tf_op jit(solution)/shard_map/ppermute | solution.py:479
  57.2 5.6 %collective-permute-start.19 = (f32[8,256]{1,0:T(8,128)S(1)}, f32[8,256]{1,0:T(8,128)S(1)}, u32[]{:S(2)}, u32[]{:S(2)}) collective-permute-start(f32[8,256]{1,0:T(8,128)S(1)} %get-tuple-element.321.note_ref.gate_ref), channel_id=1, source_target_pairs={{0,6},{1,7},{2,4},{3,5},{4,2},{5,3},{6,0},{7,1},{8,14},{9,15},{10,... | collective-permute-start | bytes 24584 | tf_op jit(solution)/shard_map/ppermute | solution.py:479
  59.0 4.3 %copy-start.9 = (bf16[256,256]{1,0:T(8,128)(2,1)S(1)}, bf16[256,256]{1,0:T(8,128)(2,1)}, u32[]{:S(2)}) copy-start(bf16[256,256]{1,0:T(8,128)(2,1)} %copy-done.8) | copy-start | bytes 393220
  60.6 13.8 %collective-permute-start.25 = (s16[272,256]{1,0:T(8,128)(2,1)S(1)}, s16[272,256]{1,0:T(8,128)(2,1)S(1)}, u32[]{:S(2)}, u32[]{:S(2)}) collective-permute-start(s16[272,256]{1,0:T(8,128)(2,1)S(1)} %last.6), channel_id=1, source_target_pairs={{0,4},{1,5},{2,6},{3,7},{4,0},{5,1},{6,2},{7,3},{8,12},{9,13},{10,... | collective-permute-start | bytes 417800 | tf_op jit(solution)/shard_map/ppermute | solution.py:479
  63.0 3.6 %collective-permute-start.20 = (f32[8,128]{1,0:T(8,128)S(1)}, f32[8,128]{1,0:T(8,128)S(1)}, u32[]{:S(2)}, u32[]{:S(2)}) collective-permute-start(f32[8,128]{1,0:T(8,128)S(1)} %get-tuple-element.324.gate_ref), channel_id=1, source_target_pairs={{0,8},{1,9},{2,10},{3,11},{4,12},{5,13},{6,14},{7,15},{8,0},{9,1},... | collective-permute-start | bytes 12296 | tf_op jit(solution)/shard_map/ppermute | solution.py:528
  64.8 6.6 %copy-start.7 = (bf16[256,256]{1,0:T(8,128)(2,1)S(1)}, bf16[256,256]{1,0:T(8,128)(2,1)}, u32[]{:S(2)}) copy-start(bf16[256,256]{1,0:T(8,128)(2,1)} %copy-done.6) | copy-start | bytes 393220
  64.9 9.5 %collective-permute-start.26 = (s16[272,256]{1,0:T(8,128)(2,1)S(1)}, s16[272,256]{1,0:T(8,128)(2,1)S(1)}, u32[]{:S(2)}, u32[]{:S(2)}) collective-permute-start(s16[272,256]{1,0:T(8,128)(2,1)S(1)} %last.7), channel_id=1, source_target_pairs={{0,6},{1,7},{2,4},{3,5},{4,2},{5,3},{6,0},{7,1},{8,14},{9,15},{10,... | collective-permute-start | bytes 417800 | tf_op jit(solution)/shard_map/ppermute | solution.py:479
  66.6 6.5 %collective-permute-start.23 = (f32[8,128]{1,0:T(8,128)S(1)}, f32[8,128]{1,0:T(8,128)S(1)}, u32[]{:S(2)}, u32[]{:S(2)}) collective-permute-start(f32[8,128]{1,0:T(8,128)S(1)} %add.279.gate_ref), channel_id=1, source_target_pairs={{0,17},{1,16},{2,19},{3,18},{4,21},{5,20},{6,23},{7,22},{8,25},{9,... | collective-permute-start | bytes 12296 | tf_op jit(solution)/shard_map/ppermute | solution.py:528
  68.2 4.9 %collective-permute-start.22 = (f32[8,128]{1,0:T(8,128)S(1)}, f32[8,128]{1,0:T(8,128)S(1)}, u32[]{:S(2)}, u32[]{:S(2)}) collective-permute-start(f32[8,128]{1,0:T(8,128)S(1)} %add.279.gate_ref), channel_id=1, source_target_pairs={{0,16},{1,17},{2,18},{3,19},{4,20},{5,21},{6,22},{7,23},{8,24},{9,... | collective-permute-start | bytes 12296 | tf_op jit(solution)/shard_map/ppermute | solution.py:528
  68.7 4.4 %collective-permute-start.21 = (f32[8,128]{1,0:T(8,128)S(1)}, f32[8,128]{1,0:T(8,128)S(1)}, u32[]{:S(2)}, u32[]{:S(2)}) collective-permute-start(f32[8,128]{1,0:T(8,128)S(1)} %add.279.gate_ref), channel_id=1, source_target_pairs={{0,1},{1,0},{2,3},{3,2},{4,5},{5,4},{6,7},{7,6},{8,9},{9,8},{10,11... | collective-permute-start | bytes 12296 | tf_op jit(solution)/shard_map/ppermute | solution.py:528
  71.5 6.7 %copy-start.3 = (bf16[256,256]{1,0:T(8,128)(2,1)S(1)}, bf16[256,256]{1,0:T(8,128)(2,1)}, u32[]{:S(2)}) copy-start(bf16[256,256]{1,0:T(8,128)(2,1)} %copy-done.2) | copy-start | bytes 393220
  71.5 7.2 %copy-start.20 = (bf16[16,64,256]{2,1,0:T(8,128)(2,1)S(1)}, bf16[16,64,256]{2,1,0:T(8,128)(2,1)}, u32[]{:S(2)}) copy-start(bf16[16,64,256]{2,1,0:T(8,128)(2,1)} %feat_ref.1) | copy-start | bytes 1572868
  71.5 7.2 %copy-start.22 = (s32[16,128]{1,0:T(8,128)S(1)}, s32[16,128]{1,0:T(8,128)}, u32[]{:S(2)}) copy-start(s32[16,128]{1,0:T(8,128)} %pos_ref.1) | copy-start | bytes 24580
  73.1 5.1 %collective-permute-start.24 = (s16[272,256]{1,0:T(8,128)(2,1)S(1)}, s16[272,256]{1,0:T(8,128)(2,1)S(1)}, u32[]{:S(2)}, u32[]{:S(2)}) collective-permute-start(s16[272,256]{1,0:T(8,128)(2,1)S(1)} %last.5), channel_id=1, source_target_pairs={{0,2},{1,3},{2,0},{3,1},{4,6},{5,7},{6,4},{7,5},{8,10},{9,11},{10,... | collective-permute-start | bytes 417800 | tf_op jit(solution)/shard_map/ppermute | solution.py:479
  79.9 0.7 copy-start.23
  79.9 0.7 copy-start.24

commit v3 on v2

v3 whole, which is shorter than its diff:
```python
import functools
import math

import jax
import jax.numpy as jnp
from jax import lax
from jax.experimental import pallas as pl
from jax.experimental.pallas import tpu as pltpu
from jax.sharding import PartitionSpec as P

SOFTMAX_TEMP = 0.07
EPSILON = 1e-05
INV_TEMP = 1.0 / SOFTMAX_TEMP
RATE = INV_TEMP * math.log2(math.e)
STEPS = 32700.0
F32 = jnp.float32
BF16 = jnp.bfloat16
NT = (((1,), (1,)), ((), ()))


def normalize(values):
    scale = lax.rsqrt(jnp.mean(values * values, axis=-1, keepdims=True) + EPSILON)
    return values * scale / math.sqrt(values.shape[-1])


def ring_sum(value, axis):
    size = lax.axis_size(axis)
    pairs = [(i, (i + 1) % size) for i in range(size)]

    def step(_, carry):
        moving, total = carry
        moving = lax.ppermute(moving, axis, pairs)
        return (moving, total + moving)

    return lax.fori_loop(0, size - 1, step, (value, value))[1]


def plain(features, patch_index, positive_index, bank):
    groups = lax.axis_size("bank")
    place = lax.axis_index("bank")
    images, hw_dev, channels = features.shape
    queries_dp = images * patch_index.shape[1]
    owned_rows = queries_dp // groups
    local_pos = patch_index - place * hw_dev
    onehot = (local_pos[:, :, None] == jnp.arange(hw_dev, dtype=jnp.int32)[None, None, :]).astype(BF16)
    picked = jnp.einsum("iph,ihc->ipc", onehot, features, preferred_element_type=F32)
    raw_all = ring_sum(picked.reshape(queries_dp, channels), "bank")
    query_vector = normalize(raw_all).astype(BF16)
    raw_own = lax.dynamic_slice_in_dim(raw_all, place * owned_rows, owned_rows, 0)
    bank_dev = bank.shape[0]
    block_keys = math.gcd(bank_dev, 512)

    def visit(index, carry):
        exponent_sum, weighted = carry
        block = lax.dynamic_slice_in_dim(bank, index * block_keys, block_keys, 0)
        logit = lax.dot_general(query_vector, block, NT, preferred_element_type=F32) / SOFTMAX_TEMP
        terms = jnp.exp(logit - INV_TEMP)
        exponent_sum = exponent_sum + jnp.sum(terms, axis=1)
        weighted = weighted + jnp.dot(terms.astype(BF16), block, preferred_element_type=F32)
        return (exponent_sum, weighted)

    start = (jnp.zeros((queries_dp,), F32), jnp.zeros((queries_dp, channels), F32))
    exponent_sum, weighted = lax.fori_loop(0, bank_dev // block_keys, visit, start)
    key_pos = positive_index - place * bank_dev
    inside = (key_pos >= 0) & (key_pos < bank_dev)
    rows_pos = jnp.clip(key_pos, 0, bank_dev - 1)
    positive_key = bank[rows_pos].astype(F32) * inside[:, None].astype(F32)
    matched = jnp.sum(query_vector.astype(F32) * positive_key, axis=1) / SOFTMAX_TEMP
    own_sum, own_logit, own_weighted, own_positive = (
        lax.dynamic_slice_in_dim(ring_sum(v, "bank"), place * owned_rows, owned_rows, 0)
        for v in (exponent_sum, matched, weighted, positive_key)
    )
    step = (own_weighted / own_sum[:, None] - own_positive) / SOFTMAX_TEMP
    loss = jnp.log(own_sum) + INV_TEMP - own_logit
    _, pullback = jax.vjp(normalize, raw_own)
    query_grad = pullback(step)[0]
    count_all = queries_dp * lax.axis_size("dp")
    mean_loss = ring_sum(ring_sum(jnp.full((8, 128), jnp.sum(loss)), "bank"), "dp")[0, 0] / count_all
    return (loss, query_grad, mean_loss)


def cost(flops):
    return pl.CostEstimate(flops=int(flops), bytes_accessed=1 << 20, transcendentals=0)


def capacity(mean, least, sigmas):
    room = mean + sigmas * math.sqrt(mean)
    return min(least, -(-int(math.ceil(room)) // 16) * 16)


def call(kernel, name, out_shape, flops, room=16, **more):
    params = pltpu.CompilerParams(vmem_limit_bytes=room << 20)
    return pl.pallas_call(
        kernel, out_shape=out_shape, compiler_params=params, cost_estimate=cost(flops), name=name, **more
    )


ANYWHERE = pl.BlockSpec(memory_space=pl.ANY)


def after(value, *others):
    return call(
        lambda *refs: None,
        "after",
        jax.ShapeDtypeStruct(value.shape, value.dtype),
        0,
        in_specs=[ANYWHERE] * (1 + len(others)),
        out_specs=ANYWHERE,
        input_output_aliases={0: 0},
    )(value, *others)


def in_lanes(column_parts, reduce):
    return reduce(column_parts.T, axis=0, keepdims=True)


def ranks_of(code, codes):
    rows, lanes = code.shape
    batch = math.gcd(codes, 16)
    tall = batch * rows
    up = lax.broadcasted_iota(jnp.int32, (lanes, 2 * lanes), 0) <= lax.broadcasted_iota(
        jnp.int32, (lanes, 2 * lanes), 1
    )
    up = up.astype(F32).astype(BF16)
    above = lax.broadcasted_iota(jnp.int32, (tall, tall), 0)
    under = lax.broadcasted_iota(jnp.int32, (tall, tall), 1)
    low = ((above > under) & (above // rows == under // rows)).astype(F32).astype(BF16)
    ranks = jnp.full(code.shape, -1.0, F32)
    most = jnp.zeros((1, lanes), F32)
    for g in range(0, codes, batch):
        mask = jnp.concatenate([(code == g + b).astype(F32) for b in range(batch)], axis=0)
        sums = jnp.dot(mask.astype(BF16), up, preferred_element_type=F32)
        count = sums[:, lanes:]
        rank = sums[:, :lanes] + jnp.dot(low, count.astype(BF16), preferred_element_type=F32)
        rank = rank * mask
        for b in range(batch):
            part = slice(b * rows, (b + 1) * rows)
            ranks = ranks + rank[part]
            most = jnp.maximum(most, jnp.sum(count[part], axis=0, keepdims=True))
    return ranks.astype(jnp.int32), most


def parity_of(shape, owned):
    row = lax.broadcasted_iota(jnp.int32, shape, 0) * shape[1] + lax.broadcasted_iota(jnp.int32, shape, 1)
    return (row // owned) % 2


def by_owner(value, owned):
    rows, lanes = value.shape
    out = []
    for start in range(0, rows * lanes, owned):
        row, lane = divmod(start, lanes)
        if owned <= lanes:
            out.append(value[row : row + 1, lane : lane + owned])
        else:
            out.append(jnp.concatenate([value[row + i : row + i + 1] for i in range(owned // lanes)], axis=1))
    return jnp.concatenate(out, axis=0)


def row_at(ref, place_ref, k):
    return ref[pl.ds(((place_ref[0] // 2) ^ k) * 2 + place_ref[0] % 2, 1), :]


SCALARS = pl.BlockSpec(memory_space=pltpu.SMEM)
NEAR = pl.BlockSpec(memory_space=pltpu.VMEM)


def pick_kernel(
    groups, owned, cap, place_ref, pos_ref, feat_ref, bank_ref, own_ref, other_ref, loc_ref, most_ref, half_ref, sem
):
    half = half_ref.shape[0]
    rows = pl.ds(pl.multiple_of(place_ref[1] * half, half), half)
    fetch = pltpu.make_async_copy(bank_ref.at[rows], half_ref, sem)
    fetch.start()
    place = place_ref[0]
    images, patches = pos_ref.shape
    hw = feat_ref.shape[1]
    pos = pos_ref[...]
    holder = pos // hw
    parity = parity_of(pos.shape, owned)
    ranks, most = ranks_of(holder * 2 + parity, 2 * groups)
    most_ref[...] = jnp.broadcast_to(most, most_ref.shape)
    inner = place % 2
    outer = place // 2
    away = outer ^ (holder // 2)
    side = (holder % 2 + inner) % 2
    stand = jnp.where(away == 1, groups // 2 - 1, jnp.maximum(away - 1, 0))
    loc_ref[...] = by_owner((stand * 2 + side) * cap + ranks, owned)
    local = pos - place * hw
    mine = holder == place
    slot = ranks + jnp.where(parity == inner, 0, cap)
    slot = jnp.where(mine & (ranks < cap), slot, -1)
    total = jnp.zeros((2 * cap, feat_ref.shape[2]), F32)
    where_slot = lax.broadcasted_iota(jnp.int32, (2 * cap, patches), 0)
    where_pos = lax.broadcasted_iota(jnp.int32, (hw, patches), 0)
    for i in range(images):
        chosen = (where_slot == slot[i : i + 1, :]).astype(F32).astype(BF16)
        spots = (where_pos == local[i : i + 1, :]).astype(F32).astype(BF16)
        table = lax.dot_general(chosen, spots, NT, preferred_element_type=F32)
        total = total + jnp.dot(table.astype(BF16), feat_ref[i], preferred_element_type=F32)
    own_ref[...] = total[:cap].astype(BF16)
    other_ref[...] = total[cap:].astype(BF16)
    fetch.wait()


def pick(features, patch_index, bank, place, core, groups, owned, cap):
    images, patches = patch_index.shape
    channels = features.shape[2]
    return call(
        functools.partial(pick_kernel, groups, owned, cap),
        "pick",
        [
            jax.ShapeDtypeStruct((cap, channels), BF16),
            jax.ShapeDtypeStruct((cap, channels), BF16),
            jax.ShapeDtypeStruct((groups, owned), jnp.int32),
            jax.ShapeDtypeStruct((8, patches), F32),
            jax.ShapeDtypeStruct((bank.shape[0] // 2, channels), BF16),
        ],
        3e9,
        in_specs=[
            pl.BlockSpec(memory_space=pltpu.SMEM),
            pl.BlockSpec(memory_space=pltpu.VMEM),
            pl.BlockSpec(memory_space=pltpu.VMEM),
            pl.BlockSpec(memory_space=pl.ANY),
        ],
        scratch_shapes=[pltpu.SemaphoreType.DMA],
    )(jnp.stack([place, core]), patch_index, features, bank)


def keys_kernel(groups, owned, cap, gates, place_ref, index_ref, bank_ref, *refs):
    near_ref, own_ref, other_ref, loc_ref, most_ref, sem = refs[gates:]
    fetch = pltpu.make_async_copy(bank_ref, near_ref, sem)
    fetch.start()
    place = place_ref[0]
    inner = place % 2
    index = index_ref[...]
    keys = near_ref.shape[0]
    holder = index // keys
    parity = parity_of(index.shape, owned)
    ranks, most = ranks_of(holder * 2 + parity, 2 * groups)
    most_ref[...] = jnp.broadcast_to(most, most_ref.shape)
    mine = holder == place
    loc_ref[...] = by_owner(jnp.where(mine, ranks, jnp.where(holder == (place ^ 1), ranks + cap, -1)), owned)
    slot = ranks + jnp.where(parity == inner, 0, cap)
    slot = jnp.where(mine & (ranks < cap), slot, -1)
    local = (index - place * keys + 1).astype(F32)
    rows, lanes = index.shape
    where_slot = lax.broadcasted_iota(jnp.int32, (2 * cap, lanes), 0)
    listed = jnp.zeros((2 * cap, lanes), F32)
    for i in range(rows):
        listed = listed + jnp.where(where_slot == slot[i : i + 1, :], local[i : i + 1, :], 0.0)
    listed = jnp.sum(listed, axis=1, keepdims=True).astype(jnp.int32) - 1
    fetch.wait()
    sub = math.gcd(keys, 256)
    lane = lax.broadcasted_iota(jnp.int32, (2 * cap, sub), 1)
    total = jnp.zeros((2 * cap, near_ref.shape[1]), F32)
    for at in range(0, keys, sub):
        table = (lane + at == listed).astype(F32).astype(BF16)
        total = total + jnp.dot(table, near_ref[at : at + sub, :], preferred_element_type=F32)
    own_ref[...] = total[:cap].astype(BF16)
    other_ref[...] = total[cap:].astype(BF16)


def bring_keys(index, bank, place, groups, owned, cap, gates):
    channels = bank.shape[1]
    return call(
        functools.partial(keys_kernel, groups, owned, cap, len(gates)),
        "keys",
        [
            jax.ShapeDtypeStruct(bank.shape, BF16),
            jax.ShapeDtypeStruct((cap, channels), BF16),
            jax.ShapeDtypeStruct((cap, channels), BF16),
            jax.ShapeDtypeStruct((groups, owned), jnp.int32),
            jax.ShapeDtypeStruct((8, index.shape[1]), F32),
        ],
        2e9,
        in_specs=[pl.BlockSpec(memory_space=pltpu.SMEM), pl.BlockSpec(memory_space=pltpu.VMEM)]
        + [ANYWHERE] * (1 + len(gates)),
        scratch_shapes=[pltpu.SemaphoreType.DMA],
    )(place.reshape(1), index, bank, *gates)


def column_of(row):
    return jnp.broadcast_to(row, (128, row.shape[1])).T[:, 0:1]


def chosen_rows(loc, parts, at):
    column = column_of(loc.astype(F32)).astype(jnp.int32)
    total = jnp.zeros((loc.shape[1], parts[0].shape[1]), F32)
    for ref in parts:
        lane = lax.broadcasted_iota(jnp.int32, (loc.shape[1], ref.shape[0]), 1)
        table = (lane + at == column).astype(F32).astype(BF16)
        total = total + jnp.dot(table, ref[...], preferred_element_type=F32)
        at += ref.shape[0]
    return total


def early_kernel(turns, place_ref, loc_ref, *refs):
    rows = loc_ref.shape[1]
    for k in range(turns):
        chosen = chosen_rows(row_at(loc_ref, place_ref, k), refs[:-1], 0)
        refs[-1][k * rows : (k + 1) * rows, :] = chosen.astype(BF16)


def early(place, loc, parts, turns):
    return call(
        functools.partial(early_kernel, turns),
        "early",
        jax.ShapeDtypeStruct((turns * loc.shape[1], parts[0].shape[1]), BF16),
        2e9,
        in_specs=[SCALARS] + [NEAR] * (1 + len(parts)),
    )(place, loc, *parts)


def arrange_kernel(turns, gates, at, place_ref, loc_ref, early_ref, *refs):
    refs = refs[gates:]
    rows = loc_ref.shape[1]
    parts, (query_ref, raw_ref), blocks = refs[: -2 - turns], refs[-2 - turns : -turns], refs[-turns:]
    for k in range(turns):
        span = slice(k * rows, (k + 1) * rows)
        raw = early_ref[span, :].astype(F32) + chosen_rows(row_at(loc_ref, place_ref, k), parts, at)
        query = normalize(raw).astype(BF16)
        query_ref[span, :] = query
        blocks[k][...] = query
        if k == 0:
            raw_ref[...] = raw.astype(BF16)


def arrange(place, loc, early_rows, parts, at, turns, gates):
    rows, channels = loc.shape[1], parts[0].shape[1]
    out = call(
        functools.partial(arrange_kernel, turns, len(gates), at),
        "arrange",
        [jax.ShapeDtypeStruct((turns * rows, channels), BF16)]
        + [jax.ShapeDtypeStruct((rows, channels), BF16)] * (turns + 1),
        3e9,
        in_specs=[SCALARS] + [NEAR] * 2 + [ANYWHERE] * len(gates) + [NEAR] * len(parts),
    )(place, loc, early_rows, *gates, *parts)
    return out[0], out[1], out[2:]


def sweep(query, keys, total, pushed):
    sub = math.gcd(keys.shape[0], 1024)
    for at in range(0, keys.shape[0], sub):
        block = keys[at : at + sub, :]
        logit = lax.dot_general(query, block, NT, preferred_element_type=F32)
        terms = jnp.exp2(logit * RATE - RATE)
        if total is not None:
            for c in range(0, sub, 128):
                total = total + terms[:, c : c + 128]
        pushed = pushed + jnp.dot(terms.astype(BF16), block, preferred_element_type=F32)
    return total, pushed


def first_kernel(turns, gates, query_ref, keys_ref, *refs):
    total_ref, blocks = refs[gates], refs[gates + 1 :]
    rows = query_ref.shape[0] // turns
    for k in range(turns):
        part = slice(k * rows, (k + 1) * rows)
        total_ref[part, :], blocks[k][...] = sweep(
            query_ref[part, :], keys_ref, jnp.zeros((rows, 128), F32), jnp.zeros(blocks[k].shape, F32)
        )


def first(query, keys, turns, gates):
    rows, channels = query.shape
    out = call(
        functools.partial(first_kernel, turns, len(gates)),
        "first",
        [jax.ShapeDtypeStruct((rows, 128), F32)] + [jax.ShapeDtypeStruct((rows // turns, channels), F32)] * turns,
        8 * rows * keys.shape[0] * channels,
        room=24,
        in_specs=[pl.BlockSpec(memory_space=pltpu.VMEM)] * 2 + [ANYWHERE] * len(gates),
    )(query, keys, *gates)
    return out[0], out[1:]


def lane_sums(query, keys, total):
    sub = math.gcd(keys.shape[0], 256)
    for at in range(0, keys.shape[0], sub):
        logit = lax.dot_general(query, keys[at : at + sub, :], NT, preferred_element_type=F32)
        terms = jnp.exp2(logit * RATE - RATE)
        for c in range(0, sub, 128):
            total = total + terms[:, c : c + 128]
    return total


def far_kernel(count, turns, query_ref, total_in, *refs):
    note_ref = refs[count]
    rows = note_ref.shape[1]
    total = total_in[...]
    for ref in refs[:count]:
        total = lane_sums(query_ref[...], ref, total)
    note_ref[...] = jnp.zeros(note_ref.shape, F32)
    for t in range(turns):
        note_ref[t : t + 1, :] = in_lanes(total[t * rows : (t + 1) * rows], jnp.sum)


def far_totals(query, total, keys, turns):
    lines = -(-2 * turns // 8) * 8
    return call(
        functools.partial(far_kernel, len(keys), turns),
        "far",
        jax.ShapeDtypeStruct((lines, query.shape[0] // turns), F32),
        2 * query.shape[0] * sum(k.shape[0] for k in keys) * query.shape[1],
        room=24,
    )(query, total, *keys)


def spread_kernel(turns, place_ref, note_in, loc_ref, own_ref, side_ref, *refs):
    blocks, note_ref, outs = refs[:turns], refs[turns], refs[turns + 1 :]
    note_ref[...] = note_in[...]
    for t in range(turns):
        positive = chosen_rows(row_at(loc_ref, place_ref, t), [own_ref, side_ref], 0)
        outs[t][...] = positive.astype(BF16)
        matched = in_lanes(blocks[t][...].astype(F32) * positive, jnp.sum)
        note_ref[turns + t : turns + t + 1, :] = matched / SOFTMAX_TEMP


def spread(place, note, loc, own, side, blocks):
    turns = len(blocks)
    rows, channels = blocks[0].shape
    out = call(
        functools.partial(spread_kernel, turns),
        "spread",
        [jax.ShapeDtypeStruct(note.shape, F32)] + [jax.ShapeDtypeStruct((rows, channels), BF16)] * turns,
        1e9,
        in_specs=[SCALARS] + [NEAR] * (4 + turns),
    )(place, note, loc, own, side, *blocks)
    return out[0], out[1:]


def exponent(size):
    return jnp.ceil(jnp.log2(jnp.maximum(size, 1e-30)))


def last_kernel(query_ref, pushed_in, gate_ref, *refs):
    pushed = pushed_in[...]
    for ref in refs[:-1]:
        _, pushed = sweep(query_ref[...], ref, None, pushed)
    refs[-1][...] = pushed


def last(query, pushed, keys, gate):
    rows, channels = query.shape
    return call(
        last_kernel,
        "last",
        jax.ShapeDtypeStruct((rows, channels), F32),
        4 * rows * sum(v.shape[0] for v in keys) * channels,
        in_specs=[pl.BlockSpec(memory_space=pltpu.VMEM)] * 2 + [ANYWHERE] + [pl.BlockSpec(memory_space=pltpu.VMEM)] * len(keys),
    )(query, pushed, gate, *keys)


def step_of(k, pushed_ref, positive_ref, totals_ref):
    return pushed_ref[...] / column_of(totals_ref[k : k + 1, :]) - positive_ref[...].astype(F32)


def code_kernel(k, pushed_ref, positive_ref, totals_ref, gate_ref, sent_ref):
    step = step_of(k, pushed_ref, positive_ref, totals_ref)
    size = jnp.abs(step)
    wide = size[:, :128]
    for c in range(128, size.shape[1], 128):
        wide = jnp.maximum(wide, size[:, c : c + 128])
    rows = step.shape[0]
    scale = jnp.exp2(-exponent(jnp.max(wide, axis=1, keepdims=True))) * STEPS
    sent_ref[:rows, :] = jnp.round(step * scale).astype(jnp.int32).astype(jnp.int16)
    power = exponent(in_lanes(wide, jnp.max)).astype(jnp.int32)
    rest = sent_ref.shape[1] - rows
    if rest:
        power = jnp.concatenate([power, jnp.zeros((1, rest), jnp.int32)], axis=1)
    sent_ref[rows:, :] = jnp.broadcast_to(power, (sent_ref.shape[0] - rows, sent_ref.shape[1])).astype(jnp.int16)


def code(pushed, positive, totals, k, gate):
    rows, channels = pushed.shape
    shape = jax.ShapeDtypeStruct((rows + 16, channels), jnp.int16)
    return call(
        functools.partial(code_kernel, k),
        "code",
        shape,
        2e8,
        in_specs=[pl.BlockSpec(memory_space=pltpu.VMEM)] * 3 + [ANYWHERE],
    )(pushed, positive, totals, gate)


def settle_kernel(turns, caps, note_ref, most_ref, held_ref, *refs):
    came = refs[: turns - 1]
    loss_ref, totals_ref, word_ref = refs[turns - 1 :]
    line = jnp.zeros(loss_ref.shape, F32)
    for t in range(turns):
        total = note_ref[t : t + 1, :]
        matched = note_ref[turns + t : turns + t + 1, :]
        for k in range(1, turns):
            ref = came[k - 1]
            total = total + ref[t ^ k : (t ^ k) + 1, :]
            matched = matched + ref[turns + (t ^ k) : turns + (t ^ k) + 1, :]
        totals_ref[t : t + 1, :] = total
        loss = jnp.log(total) + INV_TEMP - matched
        if t == 0:
            loss_ref[...] = loss
        line = line + loss
    over = (jnp.max(most_ref[...]) > caps[0]) | (jnp.max(held_ref[...]) > caps[1])
    word_ref[...] = jnp.zeros(word_ref.shape, F32)
    word_ref[0:1, 0:1] = jnp.sum(line, axis=1, keepdims=True)
    word_ref[1:2, :] = jnp.full((1, word_ref.shape[1]), jnp.where(over, 1.0, 0.0))


def settle(note, most, held, came, turns, caps):
    rows = note.shape[1]
    return call(
        functools.partial(settle_kernel, turns, caps),
        "settle",
        [
            jax.ShapeDtypeStruct((1, rows), F32),
            jax.ShapeDtypeStruct((-(-turns // 8) * 8, rows), F32),
            jax.ShapeDtypeStruct((8, 128), F32),
        ],
        1e8,
    )(note, most, held, *came)


def finish_kernel(count, queries, raw_ref, positive_ref, own_ref, totals_ref, loss_in, word_ref, came_ref, *refs):
    out_ref, loss_ref, mean_ref, flag_ref, grad_ref, sems = refs[count:]
    loss_store = pltpu.make_async_copy(loss_in, loss_ref, sems.at[0])
    loss_store.start()
    word = word_ref[...] + came_ref[...]
    mean_ref[0, 0] = jnp.sum(word[0:1, :]) * (1.0 / queries)
    flag_ref[0, 0] = (jnp.max(word[1:2, :]) > 0.5).astype(jnp.int32)
    rows = raw_ref.shape[0]
    scales = [ref[rows : rows + 16, :rows].astype(jnp.int32).astype(F32)[0:1, :] for ref in refs[:count]]
    scales = [jnp.exp2(v) * (1.0 / STEPS) for v in scales]
    fill = -count % 128
    turned = jnp.concatenate(scales + [jnp.zeros((fill, rows), F32)], axis=0).T
    step = step_of(0, own_ref, positive_ref, totals_ref)
    for j in range(count):
        step = step + refs[j][:rows, :].astype(jnp.int32).astype(F32) * turned[:, j : j + 1]
    step = step * INV_TEMP
    raw = raw_ref[...].astype(F32)
    scale = lax.rsqrt(jnp.mean(raw * raw, axis=-1, keepdims=True) + EPSILON)
    inner = jnp.mean(step * raw, axis=-1, keepdims=True)
    grad_ref[...] = (step - raw * (scale * scale * inner)) * (scale / math.sqrt(raw.shape[1]))
    store = pltpu.make_async_copy(grad_ref, out_ref, sems.at[1])
    store.start()
    loss_store.wait()
    store.wait()


def finish(raw, positive, own, totals, loss, word, came, parts, queries):
    return call(
        functools.partial(finish_kernel, len(parts), queries),
        "finish",
        [
            jax.ShapeDtypeStruct(own.shape, F32),
            jax.ShapeDtypeStruct(loss.shape, F32),
            jax.ShapeDtypeStruct((1, 1), F32),
            jax.ShapeDtypeStruct((1, 1), jnp.int32),
        ],
        5e8,
        in_specs=[NEAR] * (7 + len(parts)),
        out_specs=[pl.BlockSpec(memory_space=pltpu.HBM)] * 2 + [SCALARS] * 2,
        scratch_shapes=[pltpu.VMEM(own.shape, F32), pltpu.SemaphoreType.DMA((2,))],
    )(raw, positive, own, totals, loss, word, came, *parts)


def on_device(features, patch_index, positive_index, bank):
    groups, copies = lax.axis_size("bank"), lax.axis_size("dp")
    place = lax.axis_index("bank")
    core = lax.axis_index("dp") % 2
    images, hw_dev, channels = features.shape
    queries_dp = images * patch_index.shape[1]
    owned = queries_dp // groups
    turns = groups // 2
    inner, outer = place % 2, place // 2
    bank_dev = bank.shape[0]
    across = [(b, b ^ 1) for b in range(groups)]
    swap = [(c, c ^ 1) for c in range(copies)]

    def turn(value, k):
        pairs = [(b, b ^ (2 * k)) for b in range(groups)]
        return lax.ppermute(value, "bank", pairs)

    def to_all(values):
        return [values[0]] + [turn(values[k], k) for k in [*range(2, turns), 1]]

    cap = capacity(queries_dp / groups / 2, queries_dp // 2, 4.0)
    own_set, other_set, loc, most, half = pick(features, patch_index, bank, place, core, groups, owned, cap)
    from_side = lax.ppermute(other_set, "bank", across)
    fetched = lax.ppermute(half, "bank", across)
    held_rows = jnp.concatenate([own_set, from_side])
    parts = to_all([held_rows] * turns)

    cap_pos = capacity(queries_dp / groups / 2, queries_dp // 2, 5.0)
    index = positive_index.reshape(images, -1)
    near_keys, own_keys, other_keys, key_loc, held = bring_keys(
        index, bank, place, groups, owned, cap_pos, [from_side]
    )
    side_keys = lax.ppermute(other_keys, "bank", across)

    here = place.reshape(1)
    early_rows = early(here, loc, parts[:2], turns)
    query, raw, blocks = arrange(here, loc, early_rows, parts[2:], 4 * cap, turns, [near_keys, key_loc])

    total, pushed = first(query, near_keys, turns, [])
    fetched = after(fetched, total)
    far_keys = [fetched, lax.ppermute(fetched, "dp", swap)]
    far_note = far_totals(query, total, far_keys, turns)
    note, positive = spread(here, far_note, key_loc, own_keys, side_keys, blocks)
    came = to_all([note] * turns)
    came = [came[-1], *came[1:-1]]
    loss, totals, word = settle(note, most, held, came, turns, (cap, cap_pos))
    moved = [None] * turns
    order = [*range(2, turns)]
    order.insert(1, 1)
    whole = {k: last(blocks[k], pushed[k], far_keys, note) for k in order[:3]}
    gate = totals
    for k in order:
        if k not in whole:
            whole[k] = last(blocks[k], pushed[k], far_keys, gate)
        sent = code(whole[k], positive[k], totals, k, gate)
        moved[k] = turn(sent, k)
        gate = sent
    for axis, step in [("dp", 1), ("bank", 1)] + [("dp", 1 << i) for i in range(1, copies.bit_length() - 1)]:
        pairs = [(i, i ^ step) for i in range(lax.axis_size(axis))]
        last_word, came_word = word, lax.ppermute(word, axis, pairs)
        word = last_word + came_word
        if step == 1 and axis == "dp":
            own = last(blocks[0], pushed[0], far_keys, word)
    grad, loss, mean_loss, flag = finish(
        raw, positive[0], own, totals, loss, last_word, came_word, moved[1:], queries_dp * copies
    )
    return lax.cond(
        flag.reshape(()) > 0,
        lambda *a: plain(*a[:4]),
        lambda *a: a[4:],
        features,
        patch_index,
        positive_index,
        bank,
        loss.reshape(owned),
        grad,
        mean_loss.reshape(()),
    )


def solution(mesh):
    in_specs = (P("dp", "bank", None), P("dp", None), P("dp"), P("bank", None))
    out_specs = (P(("dp", "bank")), P(("dp", "bank"), None), P())
    turns = mesh.shape["bank"] // 2
    paired = turns > 1 and turns & (turns - 1) == 0 and mesh.shape["bank"] % 2 == 0
    copies = mesh.shape["dp"]
    paired = paired and copies > 1 and copies & (copies - 1) == 0
    return jax.shard_map(
        on_device if paired else plain, mesh=mesh, in_specs=in_specs, out_specs=out_specs, check_vma=False
    )
```

time: 82 us -> 66 us (0.80)
  local copies, waits for them, and re-layouts: 5.86 us -> 0.72 us
  waiting for transfers between devices: 20.2 us -> 15.9 us
  starting transfers between devices: 25.3 us -> 23.4 us
  between operations: 2.94 us -> 1.51 us
  Pallas kernels: 25.6 us -> 24.3 us
  other arithmetic: 1.15 us -> 0.08 us
    ppermute x12 -> x9, waiting for transfers between devices: 16 us -> 7.92 us  [turn(): return lax.ppermute(value, 'bank', pairs)]
    ppermute x5 -> x4, waiting for transfers between devices: 0.01 us -> 3.96 us  [the longest x3 3.96 us: on_device(): last_word, came_word = (word, lax.ppermute(word, axis, pairs))]
    gather x1 -> x0, local copies, waits for them, and re-layouts: 3.42 us -> none  [on_device(): bank[after(listed, from_side).reshape(-1)]]
    pallas_call x9 -> x13, Pallas kernels: 9.71 us -> 12.8 us  [the longest x4 5.63 us: last(): call(last_kernel, 'last', jax.ShapeDtypeStruct((rows, channels), F32), 4...]
    pallas_call x1, Pallas kernels: 7.7 us -> 5.08 us  [first(): call(functools.partial(first_kernel, turns, len(gates)), 'first', [jax.Sh...]
    ppermute x1, waiting for transfers between devices: 2.31 us -> 0.01 us  [on_device(): fetched = lax.ppermute(half, 'bank', across)]
    ppermute x1, waiting for transfers between devices: 1.91 us -> 3.05 us  [on_device(): from_side = lax.ppermute(other_set, 'bank', across)]
    ppermute x12 -> x9, starting transfers between devices: 16.6 us -> 15.5 us  [turn(): return lax.ppermute(value, 'bank', pairs)]
  transfers between devices with their start and end apart: 20 -> 16, of which waited for: 7 -> 6; matrix products, arithmetic and copies ran while one was open for 7% -> 0% of each run, Pallas kernels for 25% -> 27%
where the time goes in v3:
time: 66 us; the launch traced here: 65.9 us
  Pallas kernels  24.3 us (37%)
  starting transfers between devices  23.4 us (35%)
  waiting for transfers between devices  15.9 us (24%)
  between operations  1.51 us (2%)
  local copies, waits for them, and re-layouts  0.72 us (1%)
    ppermute x9, starting transfers between devices, turn(): return lax.ppermute(value, 'bank', pairs)  15.5 us
    ppermute x9, waiting for transfers between devices, turn(): return lax.ppermute(value, 'bank', pairs)  7.92 us
    pallas_call x4, Pallas kernels, last(): call(last_kernel, 'last', jax.ShapeDtypeStruct((rows, channels), F32), 4...  5.63 us
    pallas_call x1, Pallas kernels, first(): call(functools.partial(first_kernel, turns, len(gates)), 'first', [jax.Sh...  5.08 us
    ppermute x3, waiting for transfers between devices, on_device(): last_word, came_word = (word, lax.ppermute(word, axis, pairs))  3.96 us
    pallas_call x1, Pallas kernels, pick(): call(functools.partial(pick_kernel, groups, owned, cap), 'pick', [jax.Sha...  3.71 us
    ppermute x1, waiting for transfers between devices, on_device(): from_side = lax.ppermute(other_set, 'bank', across)  3.05 us
    ppermute x3, starting transfers between devices, on_device(): last_word, came_word = (word, lax.ppermute(word, axis, pairs))  3.01 us
  transfers between devices with their start and end apart: 16, of which 6 were waited for; matrix products, arithmetic and copies ran while one was open for 0% of the time, Pallas kernels for 27%

profile of v3, /device:TPU:0, one launch (start us, length us, event | category | flops | bytes accessed | tf_op | source)
XLA Modules:
  0.0 65.9 jit_solution(2029517329123191601)
XLA Ops:
  0.6 0.1 pad_add_fusion.place_ref
  0.7 3.7 %pick.1 = (bf16[176,256]{1,0:T(8,128)(2,1)S(1)}, bf16[176,256]{1,0:T(8,128)(2,1)S(1)}, s32[8,256]{1,0:T(8,128)S(1)}, f32[8,128]{1,0:T(8,128)S(1)}, bf16[2048,256]{1,0:T(8,128)(2,1)S(1)}) custom-call(s32[2]{0:T(128)S(1)} %pad_add_fusion.place_ref, s32[16,128]{1,0:T(8,128)} %pos_ref.1, bf16[16,64,256]{2,1,0:T(8,128)(2,1)} %feat_ref.1, bf16[4096,256]{1,0:T(8,128)(2,1)} %bank_ref.3), custom_call_target="tpu_custom_call" | custom-call | flops 3000000000 | bytes 1048576 | tf_op jit(solution)/shard_map/pick/pallas_call | solution.py:209
  4.4 3.0 %collective-permute-start.7 = (bf16[176,256]{1,0:T(8,128)(2,1)S(1)}, bf16[176,256]{1,0:T(8,128)(2,1)S(1)}, u32[]{:S(2)}, u32[]{:S(2)}) collective-permute-start(bf16[176,256]{1,0:T(8,128)(2,1)S(1)} %get-tuple-element.316), channel_id=1, source_target_pairs={{0,1},{1,0},{2,3},{3,2},{4,5},{5,4},{6,7},{7,6},{8,9},{9,8},{10,11... | collective-permute-start | bytes 270344 | tf_op jit(solution)/shard_map/ppermute | solution.py:588
  7.4 0.1 collective-permute-start.11
  7.5 3.1 %collective-permute-done.7.refs_0_ = bf16[176,256]{1,0:T(8,128)(2,1)S(1)} collective-permute-done((bf16[176,256]{1,0:T(8,128)(2,1)S(1)}, bf16[176,256]{1,0:T(8,128)(2,1)S(1)}, u32[]{:S(2)}, u32[]{:S(2)}) %collective-permute-start.7) | collective-permute-done | bytes 90144 | tf_op jit(solution)/shard_map/ppermute | solution.py:588
  10.6 3.4 %collective-permute-start.8 = (bf16[352,256]{1,0:T(8,128)(2,1)S(1)}, bf16[352,256]{1,0:T(8,128)(2,1)S(1)}, u32[]{:S(2)}, u32[]{:S(2)}) collective-permute-start(bf16[352,256]{1,0:T(8,128)(2,1)S(1)} %constant_dynamic-update-slice_fusion.refs_0_), channel_id=1, source_target_pairs={{0,4},{1,5},{2,6},{3,7},{4,0},{5,1},{6,2},{7,3},{8,12},{9,13},{10,... | collective-permute-start | bytes 540680 | tf_op jit(solution)/shard_map/ppermute | solution.py:581
  14.0 1.4 %collective-permute-start.9 = (bf16[352,256]{1,0:T(8,128)(2,1)S(1)}, bf16[352,256]{1,0:T(8,128)(2,1)S(1)}, u32[]{:S(2)}, u32[]{:S(2)}) collective-permute-start(bf16[352,256]{1,0:T(8,128)(2,1)S(1)} %constant_dynamic-update-slice_fusion.refs_0_), channel_id=1, source_target_pairs={{0,6},{1,7},{2,4},{3,5},{4,2},{5,3},{6,0},{7,1},{8,14},{9,15},{10,... | collective-permute-start | bytes 540680 | tf_op jit(solution)/shard_map/ppermute | solution.py:581
  15.4 0.2 collective-permute-start.10
  15.6 2.0 %keys.1 = (bf16[4096,256]{1,0:T(8,128)(2,1)S(1)}, bf16[192,256]{1,0:T(8,128)(2,1)S(1)}, bf16[192,256]{1,0:T(8,128)(2,1)S(1)}, s32[8,256]{1,0:T(8,128)S(1)}, f32[8,128]{1,0:T(8,128)S(1)}) custom-call(s32[1]{0:T(128)} %bitcast.4.place_ref, s32[16,128]{1,0:T(8,128)S(1)} %bitcast.14, bf16[4096,256]{1,0:T(8,128)(2,1)S(1)} %copy-done.7, ...), custom_call_target="tpu_custom_call" | custom-call | flops 2000000000 | bytes 1048576 | tf_op jit(solution)/shard_map/keys/pallas_call | solution.py:266
  17.6 7.9 %collective-permute-done.8.refs_1_ = bf16[352,256]{1,0:T(8,128)(2,1)S(1)} collective-permute-done((bf16[352,256]{1,0:T(8,128)(2,1)S(1)}, bf16[352,256]{1,0:T(8,128)(2,1)S(1)}, u32[]{:S(2)}, u32[]{:S(2)}) %collective-permute-start.8) | collective-permute-done | bytes 180256 | tf_op jit(solution)/shard_map/ppermute | solution.py:581
  25.5 0.9 %early.1.early_ref = bf16[1024,256]{1,0:T(8,128)(2,1)S(1)} custom-call(s32[1]{0:T(128)} %bitcast.4.place_ref, s32[8,256]{1,0:T(8,128)S(1)} %get-tuple-element.314.loc_ref, bf16[352,256]{1,0:T(8,128)(2,1)S(1)} %constant_dynamic-update-slice_fusion.refs_0_, bf16[352,256]{1,0:T(8,128)(2,1)S(1)} %collective-permute-done.8.refs_1_), custom_call_target="tpu_custom_call" | custom-call | flops 2000000000 | bytes 1048576 | tf_op jit(solution)/shard_map/early/pallas_call | solution.py:306
  26.4 0.0 collective-permute-done.9.refs_2_
  26.4 0.0 collective-permute-done.10.refs_3_
  26.4 1.0 %arrange.1 = (bf16[1024,256]{1,0:T(8,128)(2,1)S(1)}, bf16[256,256]{1,0:T(8,128)(2,1)S(1)}, bf16[256,256]{1,0:T(8,128)(2,1)S(1)}, bf16[256,256]{1,0:T(8,128)(2,1)...) custom-call(s32[1]{0:T(128)} %bitcast.4.place_ref, s32[8,256]{1,0:T(8,128)S(1)} %get-tuple-element.314.loc_ref, ...), custom_call_target="tpu_custom_call" | custom-call | flops 3000000000 | bytes 1048576 | tf_op jit(solution)/shard_map/arrange/pallas_call | solution.py:331
  27.4 5.1 %first.1 = (f32[1024,128]{1,0:T(8,128)S(1)}, f32[256,256]{1,0:T(8,128)S(1)}, f32[256,256]{1,0:T(8,128)S(1)}, f32[256,256]{1,0:T(8,128)S(1)}, f32[256,256]{1,0:T(8,128)S(1)}) custom-call(bf16[1024,256]{1,0:T(8,128)(2,1)S(1)} %get-tuple-element.320.query_ref, bf16[4096,256]{1,0:T(8,128)(2,1)S(1)} %get-tuple-element.317.refs_0_.keys_ref), custom_call_target="tpu_custom_call" | custom-call | flops 8589934592 | bytes 1048576 | tf_op jit(solution)/shard_map/first/pallas_call | solution.py:367
  32.5 0.0 collective-permute-done.11.refs_0_
  32.6 0.1 collective-permute-start.12
  32.6 1.7 %collective-permute-start.13 = (bf16[192,256]{1,0:T(8,128)(2,1)S(1)}, bf16[192,256]{1,0:T(8,128)(2,1)S(1)}, u32[]{:S(2)}, u32[]{:S(2)}) collective-permute-start(bf16[192,256]{1,0:T(8,128)(2,1)S(1)} %get-tuple-element.324), channel_id=1, source_target_pairs={{0,1},{1,0},{2,3},{3,2},{4,5},{5,4},{6,7},{7,6},{8,9},{9,8},{10,11... | collective-permute-start | bytes 294920 | tf_op jit(solution)/shard_map/ppermute | solution.py:598
  34.4 0.9 %collective-permute-done.12.refs_1_ = bf16[2048,256]{1,0:T(8,128)(2,1)S(1)} collective-permute-done((bf16[2048,256]{1,0:T(8,128)(2,1)S(1)}, bf16[2048,256]{1,0:T(8,128)(2,1)S(1)}, u32[]{:S(2)}, u32[]{:S(2)}) %collective-permute-start.12) | collective-permute-done | bytes 1048608 | tf_op jit(solution)/shard_map/ppermute | solution.py:606
  35.3 2.7 %far.1.note_in = f32[8,256]{1,0:T(8,128)S(1)} custom-call(bf16[1024,256]{1,0:T(8,128)(2,1)S(1)} %get-tuple-element.320.query_ref, f32[1024,128]{1,0:T(8,128)S(1)} %get-tuple-element.321.refs_1_.total_in, bf16[2048,256]{1,0:T(8,128)(2,1)S(1)} %after.1.refs_0_, bf16[2048,256]{1,0:T(8,128)(2,1)S(1)} %collective-permute-done.12.refs_1_), custom_call_target="tpu_custom_call" | custom-call | flops 2147483648 | bytes 1048576 | tf_op jit(solution)/shard_map/far/pallas_call | solution.py:401
  38.0 0.0 collective-permute-done.13.side_ref
  38.0 1.0 %spread.1 = (f32[8,256]{1,0:T(8,128)S(1)}, bf16[256,256]{1,0:T(8,128)(2,1)S(1)}, bf16[256,256]{1,0:T(8,128)(2,1)S(1)}, bf16[256,256]{1,0:T(8,128)(2,1)S(1)}, bf16[256,256]{1,0:T(8,128)(2,1)S(1)}) custom-call(s32[1]{0:T(128)} %bitcast.4.place_ref, f32[8,256]{1,0:T(8,128)S(1)} %far.1.note_in, s32[8,256]{1,0:T(8,128)S(1)} %get-tuple-element.318.refs_1_.loc_ref, ...), custom_call_target="tpu_custom_call" | custom-call | flops 1000000000 | bytes 1048576 | tf_op jit(solution)/shard_map/spread/pallas_call | solution.py:423
  39.1 2.6 %collective-permute-start.14 = (f32[8,256]{1,0:T(8,128)S(1)}, f32[8,256]{1,0:T(8,128)S(1)}, u32[]{:S(2)}, u32[]{:S(2)}) collective-permute-start(f32[8,256]{1,0:T(8,128)S(1)} %get-tuple-element.331.note_ref.gate_ref), channel_id=1, source_target_pairs={{0,2},{1,3},{2,0},{3,1},{4,6},{5,7},{6,4},{7,5},{8,10},{9,11},{10,... | collective-permute-start | bytes 24584 | tf_op jit(solution)/shard_map/ppermute | solution.py:581
  41.7 2.0 %collective-permute-start.15 = (f32[8,256]{1,0:T(8,128)S(1)}, f32[8,256]{1,0:T(8,128)S(1)}, u32[]{:S(2)}, u32[]{:S(2)}) collective-permute-start(f32[8,256]{1,0:T(8,128)S(1)} %get-tuple-element.331.note_ref.gate_ref), channel_id=1, source_target_pairs={{0,4},{1,5},{2,6},{3,7},{4,0},{5,1},{6,2},{7,3},{8,12},{9,13},{10,... | collective-permute-start | bytes 24584 | tf_op jit(solution)/shard_map/ppermute | solution.py:581
  43.6 1.3 %collective-permute-start.16 = (f32[8,256]{1,0:T(8,128)S(1)}, f32[8,256]{1,0:T(8,128)S(1)}, u32[]{:S(2)}, u32[]{:S(2)}) collective-permute-start(f32[8,256]{1,0:T(8,128)S(1)} %get-tuple-element.331.note_ref.gate_ref), channel_id=1, source_target_pairs={{0,6},{1,7},{2,4},{3,5},{4,2},{5,3},{6,0},{7,1},{8,14},{9,15},{10,... | collective-permute-start | bytes 24584 | tf_op jit(solution)/shard_map/ppermute | solution.py:581
  45.0 1.4 %last.5.pushed_ref = f32[256,256]{1,0:T(8,128)S(1)} custom-call(bf16[256,256]{1,0:T(8,128)(2,1)S(1)} %get-tuple-element.326.refs_1_.query_ref, f32[256,256]{1,0:T(8,128)S(1)} %get-tuple-element.337.pushed_in, f32[8,256]{1,0:T(8,128)S(1)} %get-tuple-element.331.note_ref.gate_ref, bf16[2048,256]{1,0:T(8,128)(2,1)S(1)} %after.1.refs_0_, ...), custom_call_target="tpu_custom_call" | custom-call | flops 1073741824 | bytes 1048576 | tf_op jit(solution)/shard_map/last/pallas_call | solution.py:446
  46.4 1.4 %last.6.pushed_ref = f32[256,256]{1,0:T(8,128)S(1)} custom-call(bf16[256,256]{1,0:T(8,128)(2,1)S(1)} %get-tuple-element.327.refs_2_.query_ref, f32[256,256]{1,0:T(8,128)S(1)} %get-tuple-element.339.pushed_in, f32[8,256]{1,0:T(8,128)S(1)} %get-tuple-element.331.note_ref.gate_ref, bf16[2048,256]{1,0:T(8,128)(2,1)S(1)} %after.1.refs_0_, ...), custom_call_target="tpu_custom_call" | custom-call | flops 1073741824 | bytes 1048576 | tf_op jit(solution)/shard_map/last/pallas_call | solution.py:446
  47.8 1.4 %last.7.pushed_ref = f32[256,256]{1,0:T(8,128)S(1)} custom-call(bf16[256,256]{1,0:T(8,128)(2,1)S(1)} %get-tuple-element.328.refs_3_.query_ref, f32[256,256]{1,0:T(8,128)S(1)} %get-tuple-element.341.pushed_in, f32[8,256]{1,0:T(8,128)S(1)} %get-tuple-element.331.note_ref.gate_ref, bf16[2048,256]{1,0:T(8,128)(2,1)S(1)} %after.1.refs_0_, ...), custom_call_target="tpu_custom_call" | custom-call | flops 1073741824 | bytes 1048576 | tf_op jit(solution)/shard_map/last/pallas_call | solution.py:446
  49.2 0.0 collective-permute-done.14.refs_0_
  49.3 0.1 settle.1
  49.4 0.3 code.3.gate_ref
  49.7 2.1 %collective-permute-start.21 = (s16[272,256]{1,0:T(8,128)(2,1)S(1)}, s16[272,256]{1,0:T(8,128)(2,1)S(1)}, u32[]{:S(2)}, u32[]{:S(2)}) collective-permute-start(s16[272,256]{1,0:T(8,128)(2,1)S(1)} %code.3.gate_ref), channel_id=1, source_target_pairs={{0,4},{1,5},{2,6},{3,7},{4,0},{5,1},{6,2},{7,3},{8,12},{9,13},{10,... | collective-permute-start | bytes 417800 | tf_op jit(solution)/shard_map/ppermute | solution.py:581
  51.8 0.3 code.4.gate_ref
  52.2 1.1 %collective-permute-start.20 = (s16[272,256]{1,0:T(8,128)(2,1)S(1)}, s16[272,256]{1,0:T(8,128)(2,1)S(1)}, u32[]{:S(2)}, u32[]{:S(2)}) collective-permute-start(s16[272,256]{1,0:T(8,128)(2,1)S(1)} %code.4.gate_ref), channel_id=1, source_target_pairs={{0,2},{1,3},{2,0},{3,1},{4,6},{5,7},{6,4},{7,5},{8,10},{9,11},{10,... | collective-permute-start | bytes 417800 | tf_op jit(solution)/shard_map/ppermute | solution.py:581
  53.3 0.3 code.5
  53.6 1.4 %collective-permute-start.22 = (s16[272,256]{1,0:T(8,128)(2,1)S(1)}, s16[272,256]{1,0:T(8,128)(2,1)S(1)}, u32[]{:S(2)}, u32[]{:S(2)}) collective-permute-start(s16[272,256]{1,0:T(8,128)(2,1)S(1)} %code.5), channel_id=1, source_target_pairs={{0,6},{1,7},{2,4},{3,5},{4,2},{5,3},{6,0},{7,1},{8,14},{9,15},{10,... | collective-permute-start | bytes 417800 | tf_op jit(solution)/shard_map/ppermute | solution.py:581
  55.0 0.0 collective-permute-start.17
  55.0 1.2 %collective-permute-done.17 = f32[8,128]{1,0:T(8,128)S(1)} collective-permute-done((f32[8,128]{1,0:T(8,128)S(1)}, f32[8,128]{1,0:T(8,128)S(1)}, u32[]{:S(2)}, u32[]{:S(2)}) %collective-permute-start.17) | collective-permute-done | bytes 4128 | tf_op jit(solution)/shard_map/ppermute | solution.py:625
  56.2 1.5 %collective-permute-start.18 = (f32[8,128]{1,0:T(8,128)S(1)}, f32[8,128]{1,0:T(8,128)S(1)}, u32[]{:S(2)}, u32[]{:S(2)}) collective-permute-start(f32[8,128]{1,0:T(8,128)S(1)} %add.141.gate_ref), channel_id=1, source_target_pairs={{0,1},{1,0},{2,3},{3,2},{4,5},{5,4},{6,7},{7,6},{8,9},{9,8},{10,11... | collective-permute-start | bytes 12296 | tf_op jit(solution)/shard_map/ppermute | solution.py:625
  57.7 2.1 %collective-permute-done.18 = f32[8,128]{1,0:T(8,128)S(1)} collective-permute-done((f32[8,128]{1,0:T(8,128)S(1)}, f32[8,128]{1,0:T(8,128)S(1)}, u32[]{:S(2)}, u32[]{:S(2)}) %collective-permute-start.18) | collective-permute-done | bytes 4128 | tf_op jit(solution)/shard_map/ppermute | solution.py:625
  59.8 1.5 %collective-permute-start.19 = (f32[8,128]{1,0:T(8,128)S(1)}, f32[8,128]{1,0:T(8,128)S(1)}, u32[]{:S(2)}, u32[]{:S(2)}) collective-permute-start(f32[8,128]{1,0:T(8,128)S(1)} %add.142.word_ref), channel_id=1, source_target_pairs={{0,16},{8,24},{16,0},{24,8},{1,17},{9,25},{17,1},{25,9},{2,18},{10... | collective-permute-start | bytes 12296 | tf_op jit(solution)/shard_map/ppermute | solution.py:625
  61.3 1.4 %last.4.own_ref = f32[256,256]{1,0:T(8,128)S(1)} custom-call(bf16[256,256]{1,0:T(8,128)(2,1)S(1)} %get-tuple-element.325.refs_0_.query_ref, f32[256,256]{1,0:T(8,128)S(1)} %get-tuple-element.330.pushed_in, f32[8,128]{1,0:T(8,128)S(1)} %add.141.gate_ref, bf16[2048,256]{1,0:T(8,128)(2,1)S(1)} %after.1.refs_0_, ...), custom_call_target="tpu_custom_call" | custom-call | flops 1073741824 | bytes 1048576 | tf_op jit(solution)/shard_map/last/pallas_call | solution.py:446
  62.7 0.7 %collective-permute-done.19.came_ref = f32[8,128]{1,0:T(8,128)S(1)} collective-permute-done((f32[8,128]{1,0:T(8,128)S(1)}, f32[8,128]{1,0:T(8,128)S(1)}, u32[]{:S(2)}, u32[]{:S(2)}) %collective-permute-start.19) | collective-permute-done | bytes 4128 | tf_op jit(solution)/shard_map/ppermute | solution.py:625
  63.4 0.0 collective-permute-done.20.refs_0_
  63.4 1.1 %finish.1 = (f32[256,256]{1,0:T(8,128)S(1)}, f32[1,256]{1,0:T(1,128)S(1)}, f32[1,1]{1,0:T(1,128)}, s32[1,1]{1,0:T(1,128)}) custom-call(bf16[256,256]{1,0:T(8,128)(2,1)S(1)} %get-tuple-element.319.raw_ref, bf16[256,256]{1,0:T(8,128)(2,1)S(1)} %get-tuple-element.329.positive_ref, f32[256,256]{1,0:T(8,128)S(1)} %last.4.own_ref, ...), custom_call_target="tpu_custom_call" | custom-call | flops 500000000 | bytes 1048576 | tf_op jit(solution)/shard_map/finish/pallas_call | solution.py:550
  65.2 0.0 copy-start.14
  65.2 0.0 copy-start.15
  65.2 0.7 %copy-done.14 = f32[256,256]{1,0:T(8,128)} copy-done((f32[256,256]{1,0:T(8,128)}, f32[256,256]{1,0:T(8,128)S(1)}, u32[]{:S(2)}) %copy-start.14) | copy-done | bytes 262168
  (19 shorter events, 0.1 us)
Async XLA Ops:
  0.7 14.9 %copy-start.7 = (bf16[4096,256]{1,0:T(8,128)(2,1)S(1)}, bf16[4096,256]{1,0:T(8,128)(2,1)}, u32[]{:S(2)}) copy-start(bf16[4096,256]{1,0:T(8,128)(2,1)} %bank_ref.3) | copy-start | bytes 6291460
  0.7 14.9 %copy-start.12 = (s32[2048]{0:T(1024)S(1)}, s32[2048]{0:T(1024)}, u32[]{:S(2)}) copy-start(s32[2048]{0:T(1024)} %param.24) | copy-start | bytes 24580
  4.4 6.1 %collective-permute-start.7 = (bf16[176,256]{1,0:T(8,128)(2,1)S(1)}, bf16[176,256]{1,0:T(8,128)(2,1)S(1)}, u32[]{:S(2)}, u32[]{:S(2)}) collective-permute-start(bf16[176,256]{1,0:T(8,128)(2,1)S(1)} %get-tuple-element.316), channel_id=1, source_target_pairs={{0,1},{1,0},{2,3},{3,2},{4,5},{5,4},{6,7},{7,6},{8,9},{9,8},{10,11... | collective-permute-start | bytes 270344 | tf_op jit(solution)/shard_map/ppermute | solution.py:588
  7.4 25.1 %collective-permute-start.11 = (bf16[2048,256]{1,0:T(8,128)(2,1)S(1)}, bf16[2048,256]{1,0:T(8,128)(2,1)S(1)}, u32[]{:S(2)}, u32[]{:S(2)}) collective-permute-start(bf16[2048,256]{1,0:T(8,128)(2,1)S(1)} %get-tuple-element.322), channel_id=1, source_target_pairs={{0,1},{1,0},{2,3},{3,2},{4,5},{5,4},{6,7},{7,6},{8,9},{9,8},{10,11... | collective-permute-start | bytes 3145736 | tf_op jit(solution)/shard_map/ppermute | solution.py:589
  10.6 14.9 %collective-permute-start.8 = (bf16[352,256]{1,0:T(8,128)(2,1)S(1)}, bf16[352,256]{1,0:T(8,128)(2,1)S(1)}, u32[]{:S(2)}, u32[]{:S(2)}) collective-permute-start(bf16[352,256]{1,0:T(8,128)(2,1)S(1)} %constant_dynamic-update-slice_fusion.refs_0_), channel_id=1, source_target_pairs={{0,4},{1,5},{2,6},{3,7},{4,0},{5,1},{6,2},{7,3},{8,12},{9,13},{10,... | collective-permute-start | bytes 540680 | tf_op jit(solution)/shard_map/ppermute | solution.py:581
  14.0 12.4 %collective-permute-start.9 = (bf16[352,256]{1,0:T(8,128)(2,1)S(1)}, bf16[352,256]{1,0:T(8,128)(2,1)S(1)}, u32[]{:S(2)}, u32[]{:S(2)}) collective-permute-start(bf16[352,256]{1,0:T(8,128)(2,1)S(1)} %constant_dynamic-update-slice_fusion.refs_0_), channel_id=1, source_target_pairs={{0,6},{1,7},{2,4},{3,5},{4,2},{5,3},{6,0},{7,1},{8,14},{9,15},{10,... | collective-permute-start | bytes 540680 | tf_op jit(solution)/shard_map/ppermute | solution.py:581
  15.4 11.1 %collective-permute-start.10 = (bf16[352,256]{1,0:T(8,128)(2,1)S(1)}, bf16[352,256]{1,0:T(8,128)(2,1)S(1)}, u32[]{:S(2)}, u32[]{:S(2)}) collective-permute-start(bf16[352,256]{1,0:T(8,128)(2,1)S(1)} %constant_dynamic-update-slice_fusion.refs_0_), channel_id=1, source_target_pairs={{0,2},{1,3},{2,0},{3,1},{4,6},{5,7},{6,4},{7,5},{8,10},{9,11},{10,... | collective-permute-start | bytes 540680 | tf_op jit(solution)/shard_map/ppermute | solution.py:581
  32.6 2.7 %collective-permute-start.12 = (bf16[2048,256]{1,0:T(8,128)(2,1)S(1)}, bf16[2048,256]{1,0:T(8,128)(2,1)S(1)}, u32[]{:S(2)}, u32[]{:S(2)}) collective-permute-start(bf16[2048,256]{1,0:T(8,128)(2,1)S(1)} %after.1.refs_0_), channel_id=1, source_target_pairs={{0,8},{8,0},{16,24},{24,16},{1,9},{9,1},{17,25},{25,17},{2,10},{10... | collective-permute-start | bytes 3145736 | tf_op jit(solution)/shard_map/ppermute | solution.py:606
  32.6 5.4 %collective-permute-start.13 = (bf16[192,256]{1,0:T(8,128)(2,1)S(1)}, bf16[192,256]{1,0:T(8,128)(2,1)S(1)}, u32[]{:S(2)}, u32[]{:S(2)}) collective-permute-start(bf16[192,256]{1,0:T(8,128)(2,1)S(1)} %get-tuple-element.324), channel_id=1, source_target_pairs={{0,1},{1,0},{2,3},{3,2},{4,5},{5,4},{6,7},{7,6},{8,9},{9,8},{10,11... | collective-permute-start | bytes 294920 | tf_op jit(solution)/shard_map/ppermute | solution.py:598
  39.1 10.2 %collective-permute-start.14 = (f32[8,256]{1,0:T(8,128)S(1)}, f32[8,256]{1,0:T(8,128)S(1)}, u32[]{:S(2)}, u32[]{:S(2)}) collective-permute-start(f32[8,256]{1,0:T(8,128)S(1)} %get-tuple-element.331.note_ref.gate_ref), channel_id=1, source_target_pairs={{0,2},{1,3},{2,0},{3,1},{4,6},{5,7},{6,4},{7,5},{8,10},{9,11},{10,... | collective-permute-start | bytes 24584 | tf_op jit(solution)/shard_map/ppermute | solution.py:581
  41.7 7.6 %collective-permute-start.15 = (f32[8,256]{1,0:T(8,128)S(1)}, f32[8,256]{1,0:T(8,128)S(1)}, u32[]{:S(2)}, u32[]{:S(2)}) collective-permute-start(f32[8,256]{1,0:T(8,128)S(1)} %get-tuple-element.331.note_ref.gate_ref), channel_id=1, source_target_pairs={{0,4},{1,5},{2,6},{3,7},{4,0},{5,1},{6,2},{7,3},{8,12},{9,13},{10,... | collective-permute-start | bytes 24584 | tf_op jit(solution)/shard_map/ppermute | solution.py:581
  43.6 5.6 %collective-permute-start.16 = (f32[8,256]{1,0:T(8,128)S(1)}, f32[8,256]{1,0:T(8,128)S(1)}, u32[]{:S(2)}, u32[]{:S(2)}) collective-permute-start(f32[8,256]{1,0:T(8,128)S(1)} %get-tuple-element.331.note_ref.gate_ref), channel_id=1, source_target_pairs={{0,6},{1,7},{2,4},{3,5},{4,2},{5,3},{6,0},{7,1},{8,14},{9,15},{10,... | collective-permute-start | bytes 24584 | tf_op jit(solution)/shard_map/ppermute | solution.py:581
  49.7 13.7 %collective-permute-start.21 = (s16[272,256]{1,0:T(8,128)(2,1)S(1)}, s16[272,256]{1,0:T(8,128)(2,1)S(1)}, u32[]{:S(2)}, u32[]{:S(2)}) collective-permute-start(s16[272,256]{1,0:T(8,128)(2,1)S(1)} %code.3.gate_ref), channel_id=1, source_target_pairs={{0,4},{1,5},{2,6},{3,7},{4,0},{5,1},{6,2},{7,3},{8,12},{9,13},{10,... | collective-permute-start | bytes 417800 | tf_op jit(solution)/shard_map/ppermute | solution.py:581
  52.2 11.2 %collective-permute-start.20 = (s16[272,256]{1,0:T(8,128)(2,1)S(1)}, s16[272,256]{1,0:T(8,128)(2,1)S(1)}, u32[]{:S(2)}, u32[]{:S(2)}) collective-permute-start(s16[272,256]{1,0:T(8,128)(2,1)S(1)} %code.4.gate_ref), channel_id=1, source_target_pairs={{0,2},{1,3},{2,0},{3,1},{4,6},{5,7},{6,4},{7,5},{8,10},{9,11},{10,... | collective-permute-start | bytes 417800 | tf_op jit(solution)/shard_map/ppermute | solution.py:581
  53.6 9.8 %collective-permute-start.22 = (s16[272,256]{1,0:T(8,128)(2,1)S(1)}, s16[272,256]{1,0:T(8,128)(2,1)S(1)}, u32[]{:S(2)}, u32[]{:S(2)}) collective-permute-start(s16[272,256]{1,0:T(8,128)(2,1)S(1)} %code.5), channel_id=1, source_target_pairs={{0,6},{1,7},{2,4},{3,5},{4,2},{5,3},{6,0},{7,1},{8,14},{9,15},{10,... | collective-permute-start | bytes 417800 | tf_op jit(solution)/shard_map/ppermute | solution.py:581
  55.0 1.2 %collective-permute-start.17 = (f32[8,128]{1,0:T(8,128)S(1)}, f32[8,128]{1,0:T(8,128)S(1)}, u32[]{:S(2)}, u32[]{:S(2)}) collective-permute-start(f32[8,128]{1,0:T(8,128)S(1)} %get-tuple-element.334), channel_id=1, source_target_pairs={{0,8},{8,0},{16,24},{24,16},{1,9},{9,1},{17,25},{25,17},{2,10},{10... | collective-permute-start | bytes 12296 | tf_op jit(solution)/shard_map/ppermute | solution.py:625
  56.2 3.6 %collective-permute-start.18 = (f32[8,128]{1,0:T(8,128)S(1)}, f32[8,128]{1,0:T(8,128)S(1)}, u32[]{:S(2)}, u32[]{:S(2)}) collective-permute-start(f32[8,128]{1,0:T(8,128)S(1)} %add.141.gate_ref), channel_id=1, source_target_pairs={{0,1},{1,0},{2,3},{3,2},{4,5},{5,4},{6,7},{7,6},{8,9},{9,8},{10,11... | collective-permute-start | bytes 12296 | tf_op jit(solution)/shard_map/ppermute | solution.py:625
  59.8 3.6 %collective-permute-start.19 = (f32[8,128]{1,0:T(8,128)S(1)}, f32[8,128]{1,0:T(8,128)S(1)}, u32[]{:S(2)}, u32[]{:S(2)}) collective-permute-start(f32[8,128]{1,0:T(8,128)S(1)} %add.142.word_ref), channel_id=1, source_target_pairs={{0,16},{8,24},{16,0},{24,8},{1,17},{9,25},{17,1},{25,9},{2,18},{10... | collective-permute-start | bytes 12296 | tf_op jit(solution)/shard_map/ppermute | solution.py:625
  61.3 3.8 %copy-start.11 = (bf16[16,64,256]{2,1,0:T(8,128)(2,1)S(1)}, bf16[16,64,256]{2,1,0:T(8,128)(2,1)}, u32[]{:S(2)}) copy-start(bf16[16,64,256]{2,1,0:T(8,128)(2,1)} %feat_ref.1) | copy-start | bytes 1572868
  61.3 3.8 %copy-start.13 = (s32[16,128]{1,0:T(8,128)S(1)}, s32[16,128]{1,0:T(8,128)}, u32[]{:S(2)}) copy-start(s32[16,128]{1,0:T(8,128)} %pos_ref.1) | copy-start | bytes 24580
  65.2 0.7 %copy-start.14 = (f32[256,256]{1,0:T(8,128)}, f32[256,256]{1,0:T(8,128)S(1)}, u32[]{:S(2)}) copy-start(f32[256,256]{1,0:T(8,128)S(1)} %get-tuple-element.312) | copy-start | bytes 786436
  65.2 0.7 %copy-start.15 = (f32[256]{0:T(256)}, f32[256]{0:T(256)S(1)}, u32[]{:S(2)}) copy-start(f32[256]{0:T(256)S(1)} %get-tuple-element.347) | copy-start | bytes 3076

commit v4 on v3

--- a/solution.py
+++ b/solution.py
@@ -166,118 +166,155 @@
 
 
 def pick_kernel(
-    groups, owned, cap, place_ref, pos_ref, feat_ref, bank_ref, own_ref, other_ref, loc_ref, most_ref, half_ref, sem
+    owned, cap, place_ref, pos_ref, feat_ref, bank_ref, own_ref, other_ref, relay_ref, rest_ref, table, sems
 ):
-    half = half_ref.shape[0]
-    rows = pl.ds(pl.multiple_of(place_ref[1] * half, half), half)
-    fetch = pltpu.make_async_copy(bank_ref.at[rows], half_ref, sem)
-    fetch.start()
+    fetches = []
+    for i, (ref, at) in enumerate([(relay_ref, place_ref[1]), (rest_ref, place_ref[2])]):
+        span = pl.ds(pl.multiple_of(at * 16, 16), ref.shape[0])
+        fetches.append(pltpu.make_async_copy(bank_ref.at[span], ref, sems.at[i]))
+        fetches[-1].start()
     place = place_ref[0]
     images, patches = pos_ref.shape
     hw = feat_ref.shape[1]
     pos = pos_ref[...]
-    holder = pos // hw
-    parity = parity_of(pos.shape, owned)
-    ranks, most = ranks_of(holder * 2 + parity, 2 * groups)
-    most_ref[...] = jnp.broadcast_to(most, most_ref.shape)
-    inner = place % 2
-    outer = place // 2
-    away = outer ^ (holder // 2)
-    side = (holder % 2 + inner) % 2
-    stand = jnp.where(away == 1, groups // 2 - 1, jnp.maximum(away - 1, 0))
-    loc_ref[...] = by_owner((stand * 2 + side) * cap + ranks, owned)
-    local = pos - place * hw
-    mine = holder == place
-    slot = ranks + jnp.where(parity == inner, 0, cap)
+    mine = pos // hw == place
+    parity = (parity_of(pos.shape, owned) + place) % 2
+    code = jnp.where(mine, parity, 2)
+    ranks, _ = ranks_of(code, 2)
+    slot = ranks + parity * cap
     slot = jnp.where(mine & (ranks < cap), slot, -1)
-    total = jnp.zeros((2 * cap, feat_ref.shape[2]), F32)
-    where_slot = lax.broadcasted_iota(jnp.int32, (2 * cap, patches), 0)
-    where_pos = lax.broadcasted_iota(jnp.int32, (hw, patches), 0)
-    for i in range(images):
-        chosen = (where_slot == slot[i : i + 1, :]).astype(F32).astype(BF16)
-        spots = (where_pos == local[i : i + 1, :]).astype(F32).astype(BF16)
-        table = lax.dot_general(chosen, spots, NT, preferred_element_type=F32)
-        total = total + jnp.dot(table.astype(BF16), feat_ref[i], preferred_element_type=F32)
+    local = jnp.where(mine, pos - place * hw, -1)
+    batch = math.gcd(images, max(1, 256 // patches))
+    where_slot = lax.broadcasted_iota(jnp.int32, (2 * cap, batch * patches), 0)
+    where_pos = lax.broadcasted_iota(jnp.int32, (batch * hw, batch * patches), 0)
+    for i in range(0, images, batch):
+        slots = jnp.concatenate([slot[i + b : i + b + 1, :] for b in range(batch)], axis=1)
+        locals_ = jnp.concatenate(
+            [jnp.where(local[i + b : i + b + 1, :] < 0, -1, local[i + b : i + b + 1, :] + b * hw) for b in range(batch)],
+            axis=1,
+        )
+        chosen = (where_slot == slots).astype(F32).astype(BF16)
+        spots = (where_pos == locals_).astype(F32).astype(BF16)
+        part = lax.dot_general(chosen, spots, NT, preferred_element_type=F32)
+        table[:, i * hw : (i + batch) * hw] = part.astype(BF16)
+    rows = feat_ref[...].reshape(images * hw, feat_ref.shape[2])
+    total = jnp.dot(table[...], rows, preferred_element_type=F32)
     own_ref[...] = total[:cap].astype(BF16)
     other_ref[...] = total[cap:].astype(BF16)
-    fetch.wait()
-
-
-def pick(features, patch_index, bank, place, core, groups, owned, cap):
-    images, patches = patch_index.shape
-    channels = features.shape[2]
-    return call(
-        functools.partial(pick_kernel, groups, owned, cap),
+    for fetch in fetches:
+        fetch.wait()
+
+
+def pick(features, patch_index, bank, numbers, relay, rest, owned, cap):
+    images, hw, channels = features.shape
+    return call(
+        functools.partial(pick_kernel, owned, cap),
         "pick",
         [
             jax.ShapeDtypeStruct((cap, channels), BF16),
             jax.ShapeDtypeStruct((cap, channels), BF16),
-            jax.ShapeDtypeStruct((groups, owned), jnp.int32),
-            jax.ShapeDtypeStruct((8, patches), F32),
-            jax.ShapeDtypeStruct((bank.shape[0] // 2, channels), BF16),
+            jax.ShapeDtypeStruct((relay, channels), BF16),
+            jax.ShapeDtypeStruct((rest, channels), BF16),
         ],
         3e9,
-        in_specs=[
-            pl.BlockSpec(memory_space=pltpu.SMEM),
-            pl.BlockSpec(memory_space=pltpu.VMEM),
-            pl.BlockSpec(memory_space=pltpu.VMEM),
-            pl.BlockSpec(memory_space=pl.ANY),
+        in_specs=[SCALARS, NEAR, NEAR, ANYWHERE],
+        scratch_shapes=[pltpu.VMEM((2 * cap, images * hw), BF16), pltpu.SemaphoreType.DMA((2,))],
+    )(numbers, patch_index, features, bank)
+
+
+def locate_kernel(groups, owned, cap, hw, gates, place_ref, pos_ref, *refs):
+    loc_ref, most_ref = refs[gates:]
+    place = place_ref[0]
+    pos = pos_ref[...]
+    holder = pos // hw
+    ranks, most = ranks_of(holder * 2 + parity_of(pos.shape, owned), 2 * groups)
+    most_ref[...] = jnp.broadcast_to(most, most_ref.shape)
+    away = (place // 2) ^ (holder // 2)
+    side = (holder % 2 + place) % 2
+    stand = jnp.where(away == 1, groups // 2 - 1, jnp.maximum(away - 1, 0))
+    loc_ref[...] = by_owner((stand * 2 + side) * cap + ranks, owned)
+
+
+def locate(patch_index, place, groups, owned, cap, hw, gates):
+    return call(
+        functools.partial(locate_kernel, groups, owned, cap, hw, len(gates)),
+        "locate",
+        [
+            jax.ShapeDtypeStruct((groups, owned), jnp.int32),
+            jax.ShapeDtypeStruct((8, patch_index.shape[1]), F32),
         ],
-        scratch_shapes=[pltpu.SemaphoreType.DMA],
-    )(jnp.stack([place, core]), patch_index, features, bank)
-
-
-def keys_kernel(groups, owned, cap, gates, place_ref, index_ref, bank_ref, *refs):
-    near_ref, own_ref, other_ref, loc_ref, most_ref, sem = refs[gates:]
+        1e9,
+        in_specs=[SCALARS, NEAR] + [ANYWHERE] * len(gates),
+    )(place.reshape(1), patch_index, *gates)
+
+
+def keys_kernel(groups, owned, cap, relay, gates, place_ref, index_ref, bank_ref, *refs):
+    near_ref, own_ref, list_ref, loc_ref, most_ref, sem = refs[gates:]
     fetch = pltpu.make_async_copy(bank_ref, near_ref, sem)
     fetch.start()
-    place = place_ref[0]
-    inner = place % 2
+    place, core, line = place_ref[0], place_ref[1], place_ref[2]
     index = index_ref[...]
     keys = near_ref.shape[0]
     holder = index // keys
     parity = parity_of(index.shape, owned)
     ranks, most = ranks_of(holder * 2 + parity, 2 * groups)
     most_ref[...] = jnp.broadcast_to(most, most_ref.shape)
-    mine = holder == place
-    loc_ref[...] = by_owner(jnp.where(mine, ranks, jnp.where(holder == (place ^ 1), ranks + cap, -1)), owned)
-    slot = ranks + jnp.where(parity == inner, 0, cap)
-    slot = jnp.where(mine & (ranks < cap), slot, -1)
-    local = (index - place * keys + 1).astype(F32)
+    mine, theirs = holder == place, holder == (place ^ 1)
+    loc_ref[...] = by_owner(jnp.where(mine, ranks, jnp.where(theirs, ranks + cap, -1)), owned)
+    slot = jnp.where(theirs, ranks + cap, ranks)
+    slot = jnp.where((mine | theirs) & (ranks < cap) & (parity == place % 2), slot, -1)
+    half = keys // 2
+    rest = half - 2 * relay
+    far = index - (place ^ 1) * keys
+    other = jnp.where(far // half == core, 0, 1)
+    offset = far % half
+    strip = jnp.where(offset // relay == line, 0, 1)
+    far = jnp.where(
+        offset < 2 * relay,
+        (strip * 2 + other) * relay + offset % relay,
+        4 * relay + other * rest + offset - 2 * relay,
+    )
+    local = (jnp.where(mine, index - place * keys, far) + 1).astype(F32)
     rows, lanes = index.shape
     where_slot = lax.broadcasted_iota(jnp.int32, (2 * cap, lanes), 0)
     listed = jnp.zeros((2 * cap, lanes), F32)
     for i in range(rows):
         listed = listed + jnp.where(where_slot == slot[i : i + 1, :], local[i : i + 1, :], 0.0)
     listed = jnp.sum(listed, axis=1, keepdims=True).astype(jnp.int32) - 1
+    list_ref[...] = listed[cap:]
     fetch.wait()
-    sub = math.gcd(keys, 256)
-    lane = lax.broadcasted_iota(jnp.int32, (2 * cap, sub), 1)
-    total = jnp.zeros((2 * cap, near_ref.shape[1]), F32)
-    for at in range(0, keys, sub):
-        table = (lane + at == listed).astype(F32).astype(BF16)
-        total = total + jnp.dot(table, near_ref[at : at + sub, :], preferred_element_type=F32)
-    own_ref[...] = total[:cap].astype(BF16)
-    other_ref[...] = total[cap:].astype(BF16)
-
-
-def bring_keys(index, bank, place, groups, owned, cap, gates):
+    own_ref[...] = listed_rows(listed[:cap], [near_ref]).astype(BF16)
+
+
+def listed_rows(listed, parts):
+    total = jnp.zeros((listed.shape[0], parts[0].shape[1]), F32)
+    start = 0
+    for ref in parts:
+        sub = math.gcd(ref.shape[0], 256)
+        lane = lax.broadcasted_iota(jnp.int32, (listed.shape[0], sub), 1)
+        for at in range(0, ref.shape[0], sub):
+            table = (lane + (start + at) == listed).astype(F32).astype(BF16)
+            total = total + jnp.dot(table, ref[at : at + sub, :], preferred_element_type=F32)
+        start += ref.shape[0]
+    return total
+
+
+def bring_keys(index, bank, numbers, groups, owned, cap, relay, gates):
     channels = bank.shape[1]
     return call(
-        functools.partial(keys_kernel, groups, owned, cap, len(gates)),
+        functools.partial(keys_kernel, groups, owned, cap, relay, len(gates)),
         "keys",
         [
             jax.ShapeDtypeStruct(bank.shape, BF16),
             jax.ShapeDtypeStruct((cap, channels), BF16),
-            jax.ShapeDtypeStruct((cap, channels), BF16),
+            jax.ShapeDtypeStruct((cap, 1), jnp.int32),
             jax.ShapeDtypeStruct((groups, owned), jnp.int32),
             jax.ShapeDtypeStruct((8, index.shape[1]), F32),
         ],
         2e9,
-        in_specs=[pl.BlockSpec(memory_space=pltpu.SMEM), pl.BlockSpec(memory_space=pltpu.VMEM)]
-        + [ANYWHERE] * (1 + len(gates)),
+        in_specs=[SCALARS, NEAR] + [ANYWHERE] * (1 + len(gates)),
         scratch_shapes=[pltpu.SemaphoreType.DMA],
-    )(place.reshape(1), index, bank, *gates)
+    )(numbers, index, bank, *gates)
 
 
 def column_of(row):
@@ -295,21 +332,22 @@
     return total
 
 
-def early_kernel(turns, place_ref, loc_ref, *refs):
+def early_kernel(turns, gates, place_ref, loc_ref, *refs):
+    refs = refs[gates:]
     rows = loc_ref.shape[1]
     for k in range(turns):
         chosen = chosen_rows(row_at(loc_ref, place_ref, k), refs[:-1], 0)
         refs[-1][k * rows : (k + 1) * rows, :] = chosen.astype(BF16)
 
 
-def early(place, loc, parts, turns):
-    return call(
-        functools.partial(early_kernel, turns),
+def early(place, loc, parts, turns, gates):
+    return call(
+        functools.partial(early_kernel, turns, len(gates)),
         "early",
         jax.ShapeDtypeStruct((turns * loc.shape[1], parts[0].shape[1]), BF16),
         2e9,
-        in_specs=[SCALARS] + [NEAR] * (1 + len(parts)),
-    )(place, loc, *parts)
+        in_specs=[SCALARS, NEAR] + [ANYWHERE] * len(gates) + [NEAR] * len(parts),
+    )(place, loc, *gates, *parts)
 
 
 def arrange_kernel(turns, gates, at, place_ref, loc_ref, early_ref, *refs):
@@ -385,48 +423,35 @@
     return total
 
 
-def far_kernel(count, turns, query_ref, total_in, *refs):
-    note_ref = refs[count]
+def far_kernel(count, turns, place_ref, loc_ref, query_ref, total_in, own_ref, list_ref, *refs):
+    keys, note_ref, outs, side_ref = refs[:count], refs[count], refs[count + 1 : -1], refs[-1]
     rows = note_ref.shape[1]
+    side_ref[...] = listed_rows(list_ref[...], keys).astype(BF16)
     total = total_in[...]
-    for ref in refs[:count]:
+    for ref in keys:
         total = lane_sums(query_ref[...], ref, total)
     note_ref[...] = jnp.zeros(note_ref.shape, F32)
     for t in range(turns):
-        note_ref[t : t + 1, :] = in_lanes(total[t * rows : (t + 1) * rows], jnp.sum)
-
-
-def far_totals(query, total, keys, turns):
+        part = slice(t * rows, (t + 1) * rows)
+        note_ref[t : t + 1, :] = in_lanes(total[part], jnp.sum)
+        positive = chosen_rows(row_at(loc_ref, place_ref, t), [own_ref, side_ref], 0)
+        outs[t][...] = positive.astype(BF16)
+        matched = in_lanes(query_ref[part, :].astype(F32) * positive, jnp.sum)
+        note_ref[turns + t : turns + t + 1, :] = matched / SOFTMAX_TEMP
+
+
+def far_totals(place, loc, query, total, own, listed, keys, turns):
     lines = -(-2 * turns // 8) * 8
-    return call(
+    rows, channels = query.shape[0] // turns, query.shape[1]
+    out = call(
         functools.partial(far_kernel, len(keys), turns),
         "far",
-        jax.ShapeDtypeStruct((lines, query.shape[0] // turns), F32),
-        2 * query.shape[0] * sum(k.shape[0] for k in keys) * query.shape[1],
+        [jax.ShapeDtypeStruct((lines, rows), F32)] + [jax.ShapeDtypeStruct((rows, channels), BF16)] * turns,
+        2 * query.shape[0] * sum(k.shape[0] for k in keys) * channels,
         room=24,
-    )(query, total, *keys)
-
-
-def spread_kernel(turns, place_ref, note_in, loc_ref, own_ref, side_ref, *refs):
-    blocks, note_ref, outs = refs[:turns], refs[turns], refs[turns + 1 :]
-    note_ref[...] = note_in[...]
-    for t in range(turns):
-        positive = chosen_rows(row_at(loc_ref, place_ref, t), [own_ref, side_ref], 0)
-        outs[t][...] = positive.astype(BF16)
-        matched = in_lanes(blocks[t][...].astype(F32) * positive, jnp.sum)
-        note_ref[turns + t : turns + t + 1, :] = matched / SOFTMAX_TEMP
-
-
-def spread(place, note, loc, own, side, blocks):
-    turns = len(blocks)
-    rows, channels = blocks[0].shape
-    out = call(
-        functools.partial(spread_kernel, turns),
-        "spread",
-        [jax.ShapeDtypeStruct(note.shape, F32)] + [jax.ShapeDtypeStruct((rows, channels), BF16)] * turns,
-        1e9,
-        in_specs=[SCALARS] + [NEAR] * (4 + turns),
-    )(place, note, loc, own, side, *blocks)
+        in_specs=[SCALARS] + [NEAR] * (5 + len(keys)),
+        scratch_shapes=[pltpu.VMEM(own.shape, BF16)],
+    )(place, loc, query, total, own, listed, *keys)
     return out[0], out[1:]
 
 
@@ -456,7 +481,8 @@
     return pushed_ref[...] / column_of(totals_ref[k : k + 1, :]) - positive_ref[...].astype(F32)
 
 
-def code_kernel(k, pushed_ref, positive_ref, totals_ref, gate_ref, sent_ref):
+def code_kernel(k, pushed_ref, positive_ref, totals_ref, *refs):
+    sent_ref = refs[-1]
     step = step_of(k, pushed_ref, positive_ref, totals_ref)
     size = jnp.abs(step)
     wide = size[:, :128]
@@ -472,7 +498,7 @@
     sent_ref[rows:, :] = jnp.broadcast_to(power, (sent_ref.shape[0] - rows, sent_ref.shape[1])).astype(jnp.int16)
 
 
-def code(pushed, positive, totals, k, gate):
+def code(pushed, positive, totals, k, gates):
     rows, channels = pushed.shape
     shape = jax.ShapeDtypeStruct((rows + 16, channels), jnp.int16)
     return call(
@@ -480,8 +506,8 @@
         "code",
         shape,
         2e8,
-        in_specs=[pl.BlockSpec(memory_space=pltpu.VMEM)] * 3 + [ANYWHERE],
-    )(pushed, positive, totals, gate)
+        in_specs=[NEAR] * 3 + [ANYWHERE] * len(gates),
+    )(pushed, positive, totals, *gates)
 
 
 def settle_kernel(turns, caps, note_ref, most_ref, held_ref, *refs):
@@ -520,13 +546,26 @@
     )(note, most, held, *came)
 
 
-def finish_kernel(count, queries, raw_ref, positive_ref, own_ref, totals_ref, loss_in, word_ref, came_ref, *refs):
-    out_ref, loss_ref, mean_ref, flag_ref, grad_ref, sems = refs[count:]
-    loss_store = pltpu.make_async_copy(loss_in, loss_ref, sems.at[0])
-    loss_store.start()
+def mean_kernel(queries, word_ref, came_ref, mean_ref, flag_ref):
     word = word_ref[...] + came_ref[...]
     mean_ref[0, 0] = jnp.sum(word[0:1, :]) * (1.0 / queries)
     flag_ref[0, 0] = (jnp.max(word[1:2, :]) > 0.5).astype(jnp.int32)
+
+
+def mean(word, came, queries):
+    return call(
+        functools.partial(mean_kernel, queries),
+        "mean",
+        [jax.ShapeDtypeStruct((1, 1), F32), jax.ShapeDtypeStruct((1, 1), jnp.int32)],
+        1e8,
+        in_specs=[NEAR] * 2,
+        out_specs=[SCALARS] * 2,
+    )(word, came)
+
+
+def finish_kernel(count, loss_in, raw_ref, positive_ref, own_ref, totals_ref, *refs):
+    grad_ref, loss_ref = refs[count:]
+    loss_ref[...] = loss_in[...]
     rows = raw_ref.shape[0]
     scales = [ref[rows : rows + 16, :rows].astype(jnp.int32).astype(F32)[0:1, :] for ref in refs[:count]]
     scales = [jnp.exp2(v) * (1.0 / STEPS) for v in scales]
@@ -540,27 +579,16 @@
     scale = lax.rsqrt(jnp.mean(raw * raw, axis=-1, keepdims=True) + EPSILON)
     inner = jnp.mean(step * raw, axis=-1, keepdims=True)
     grad_ref[...] = (step - raw * (scale * scale * inner)) * (scale / math.sqrt(raw.shape[1]))
-    store = pltpu.make_async_copy(grad_ref, out_ref, sems.at[1])
-    store.start()
-    loss_store.wait()
-    store.wait()
-
-
-def finish(raw, positive, own, totals, loss, word, came, parts, queries):
-    return call(
-        functools.partial(finish_kernel, len(parts), queries),
+
+
+def finish(loss, raw, positive, own, totals, parts):
+    return call(
+        functools.partial(finish_kernel, len(parts)),
         "finish",
-        [
-            jax.ShapeDtypeStruct(own.shape, F32),
-            jax.ShapeDtypeStruct(loss.shape, F32),
-            jax.ShapeDtypeStruct((1, 1), F32),
-            jax.ShapeDtypeStruct((1, 1), jnp.int32),
-        ],
+        [jax.ShapeDtypeStruct(own.shape, F32), jax.ShapeDtypeStruct(loss.shape, F32)],
         5e8,
-        in_specs=[NEAR] * (7 + len(parts)),
-        out_specs=[pl.BlockSpec(memory_space=pltpu.HBM)] * 2 + [SCALARS] * 2,
-        scratch_shapes=[pltpu.VMEM(own.shape, F32), pltpu.SemaphoreType.DMA((2,))],
-    )(raw, positive, own, totals, loss, word, came, *parts)
+        in_specs=[NEAR] * (5 + len(parts)),
+    )(loss, raw, positive, own, totals, *parts)
 
 
 def on_device(features, patch_index, positive_index, bank):
@@ -584,28 +612,40 @@
         return [values[0]] + [turn(values[k], k) for k in [*range(2, turns), 1]]
 
     cap = capacity(queries_dp / groups / 2, queries_dp // 2, 4.0)
-    own_set, other_set, loc, most, half = pick(features, patch_index, bank, place, core, groups, owned, cap)
+    half = bank_dev // 2
+    relay = half * 2 // 8 // 16 * 16
+    rest = half - 2 * relay
+    row = (lax.axis_index("dp") // 2) % 2
+    start = core * half // 16
+    numbers = jnp.stack([place, start + row * (relay // 16), start + relay // 8])
+    own_set, other_set, relay_out, rest_out = pick(features, patch_index, bank, numbers, relay, rest, owned, cap)
     from_side = lax.ppermute(other_set, "bank", across)
-    fetched = lax.ppermute(half, "bank", across)
+    relayed = lax.ppermute(relay_out, "bank", across)
+    rest_in = lax.ppermute(rest_out, "bank", across)
     held_rows = jnp.concatenate([own_set, from_side])
     parts = to_all([held_rows] * turns)
 
+    loc, most = locate(patch_index, place, groups, owned, cap, hw_dev, [from_side])
+    over = [(c, c ^ 2) for c in range(copies)]
+    from_row = lax.ppermute(after(relayed, loc), "dp", over)
+
     cap_pos = capacity(queries_dp / groups / 2, queries_dp // 2, 5.0)
     index = positive_index.reshape(images, -1)
-    near_keys, own_keys, other_keys, key_loc, held = bring_keys(
-        index, bank, place, groups, owned, cap_pos, [from_side]
+    numbers = jnp.stack([place, core, row])
+    near_keys, own_keys, listed, key_loc, held = bring_keys(
+        index, bank, numbers, groups, owned, cap_pos, relay, [from_side]
     )
-    side_keys = lax.ppermute(other_keys, "bank", across)
 
     here = place.reshape(1)
-    early_rows = early(here, loc, parts[:2], turns)
+    early_rows = early(here, loc, parts[:2], turns, [])
     query, raw, blocks = arrange(here, loc, early_rows, parts[2:], 4 * cap, turns, [near_keys, key_loc])
 
-    total, pushed = first(query, near_keys, turns, [])
-    fetched = after(fetched, total)
-    far_keys = [fetched, lax.ppermute(fetched, "dp", swap)]
-    far_note = far_totals(query, total, far_keys, turns)
-    note, positive = spread(here, far_note, key_loc, own_keys, side_keys, blocks)
+    far_keys = []
+    for part in (relayed, from_row, rest_in):
+        part = after(part, query)
+        far_keys += [part, lax.ppermute(part, "dp", swap)]
+    total, pushed = first(query, near_keys, turns, [far_keys[0], far_keys[2], far_keys[4]])
+    note, positive = far_totals(here, key_loc, query, total, own_keys, listed, far_keys, turns)
     came = to_all([note] * turns)
     came = [came[-1], *came[1:-1]]
     loss, totals, word = settle(note, most, held, came, turns, (cap, cap_pos))
@@ -613,32 +653,32 @@
     order = [*range(2, turns)]
     order.insert(1, 1)
     whole = {k: last(blocks[k], pushed[k], far_keys, note) for k in order[:3]}
-    gate = totals
+    words = [word]
+    for axis, step in [("dp", 1), ("bank", 1)] + [("dp", 1 << i) for i in range(1, copies.bit_length() - 1)]:
+        pairs = [(i, i ^ step) for i in range(lax.axis_size(axis))]
+        came_word = lax.ppermute(words[-1], axis, pairs)
+        words.append(words[-1] + came_word)
+    gates = [totals]
     for k in order:
         if k not in whole:
-            whole[k] = last(blocks[k], pushed[k], far_keys, gate)
-        sent = code(whole[k], positive[k], totals, k, gate)
+            whole[k] = last(blocks[k], pushed[k], far_keys, gates[0])
+        sent = code(whole[k], positive[k], totals, k, gates)
         moved[k] = turn(sent, k)
-        gate = sent
-    for axis, step in [("dp", 1), ("bank", 1)] + [("dp", 1 << i) for i in range(1, copies.bit_length() - 1)]:
-        pairs = [(i, i ^ step) for i in range(lax.axis_size(axis))]
-        last_word, came_word = word, lax.ppermute(word, axis, pairs)
-        word = last_word + came_word
-        if step == 1 and axis == "dp":
-            own = last(blocks[0], pushed[0], far_keys, word)
-    grad, loss, mean_loss, flag = finish(
-        raw, positive[0], own, totals, loss, last_word, came_word, moved[1:], queries_dp * copies
-    )
+        gates = [sent, words[1]]
+    own = last(blocks[0], pushed[0], far_keys, words[-2])
+    mean_loss, flag = mean(words[-2], came_word, queries_dp * copies)
+    ready = [loss, raw, positive[0], own, totals, *moved[1:]]
+
+    def usual(given, ready, mean_loss):
+        grad, loss = finish(*ready[:5], ready[5:])
+        return (loss.reshape(owned), grad, mean_loss)
+
     return lax.cond(
         flag.reshape(()) > 0,
-        lambda *a: plain(*a[:4]),
-        lambda *a: a[4:],
-        features,
-        patch_index,
-        positive_index,
-        bank,
-        loss.reshape(owned),
-        grad,
+        lambda given, ready, mean_loss: plain(*given),
+        usual,
+        [features, patch_index, positive_index, bank],
+        ready,
         mean_loss.reshape(()),
     )
 
@@ -649,7 +689,7 @@
     turns = mesh.shape["bank"] // 2
     paired = turns > 1 and turns & (turns - 1) == 0 and mesh.shape["bank"] % 2 == 0
     copies = mesh.shape["dp"]
-    paired = paired and copies > 1 and copies & (copies - 1) == 0
+    paired = paired and copies > 2 and copies & (copies - 1) == 0
     return jax.shard_map(
         on_device if paired else plain, mesh=mesh, in_specs=in_specs, out_specs=out_specs, check_vma=False
     )

time: 66 us -> 61.8 us (0.936)
  waiting for transfers between devices: 15.9 us -> 9.87 us
  starting transfers between devices: 23.4 us -> 25.8 us
  Pallas kernels: 24.3 us -> 23.4 us
    ppermute x6 -> x9, starting transfers between devices: 4.88 us -> 7.35 us  [the longest x3 3.09 us: on_device(): came_word = lax.ppermute(words[-1], axis, pairs)]
    ppermute x6 -> x9, waiting for transfers between devices: 4.89 us -> 2.77 us  [the longest x3 2.76 us: on_device(): came_word = lax.ppermute(words[-1], axis, pairs)]
    ppermute x1, waiting for transfers between devices: 3.05 us -> 1.03 us  [on_device(): from_side = lax.ppermute(other_set, 'bank', across)]
    ppermute x9, waiting for transfers between devices: 7.92 us -> 6.06 us  [turn(): return lax.ppermute(value, 'bank', pairs)]
    pallas_call x6 -> x7, Pallas kernels: 11.5 us -> 10.5 us  [the longest x1 3.52 us: far_totals(): call(functools.partial(far_kernel, len(keys), turns), 'far', [jax.ShapeDt...]
  transfers between devices with their start and end apart: 16 -> 19, of which waited for: 6 -> 5; matrix products, arithmetic and copies ran while one was open for 0% -> 0% of each run, Pallas kernels for 27% -> 27%
where the time goes in v4:
time: 61.8 us; the launch traced here: 61.6 us
  starting transfers between devices  25.8 us (42%)
  Pallas kernels  23.4 us (38%)
  waiting for transfers between devices  9.87 us (16%)
  between operations  1.62 us (3%)
  local copies, waits for them, and re-layouts  0.74 us (1%)
    ppermute x9, starting transfers between devices, turn(): return lax.ppermute(value, 'bank', pairs)  15.5 us
    ppermute x9, waiting for transfers between devices, turn(): return lax.ppermute(value, 'bank', pairs)  6.06 us
    pallas_call x4, Pallas kernels, last(): call(last_kernel, 'last', jax.ShapeDtypeStruct((rows, channels), F32), 4...  5.72 us
    pallas_call x1, Pallas kernels, first(): call(functools.partial(first_kernel, turns, len(gates)), 'first', [jax.Sh...  5.07 us
    pallas_call x1, Pallas kernels, far_totals(): call(functools.partial(far_kernel, len(keys), turns), 'far', [jax.ShapeDt...  3.52 us
    ppermute x3, starting transfers between devices, on_device(): came_word = lax.ppermute(words[-1], axis, pairs)  3.09 us
    ppermute x1, starting transfers between devices, on_device(): from_side = lax.ppermute(other_set, 'bank', across)  3 us
    ppermute x3, waiting for transfers between devices, on_device(): came_word = lax.ppermute(words[-1], axis, pairs)  2.76 us
  transfers between devices with their start and end apart: 19, of which 5 were waited for; matrix products, arithmetic and copies ran while one was open for 0% of the time, Pallas kernels for 27%

profile of v4, /device:TPU:0, one launch (start us, length us, event | category | flops | bytes accessed | tf_op | source)
XLA Modules:
  0.0 61.6 jit_solution(4688998781309035509)
XLA Ops:
  0.7 0.1 pad_add_fusion.1.place_ref
  0.8 2.4 %pick.1 = (bf16[176,256]{1,0:T(8,128)(2,1)S(1)}, bf16[176,256]{1,0:T(8,128)(2,1)S(1)}, bf16[512,256]{1,0:T(8,128)(2,1)S(1)}, bf16[1024,256]{1,0:T(8,128)(2,1)S(1)}) custom-call(s32[3]{0:T(128)S(1)} %pad_add_fusion.1.place_ref, s32[16,128]{1,0:T(8,128)} %pos_ref.3, bf16[16,64,256]{2,1,0:T(8,128)(2,1)} %feat_ref.1, bf16[4096,256]{1,0:T(8,128)(2,1)} %bank_ref.3), custom_call_target="tpu_custom_call" | custom-call | flops 3000000000 | bytes 1048576 | tf_op jit(solution)/shard_map/pick/pallas_call | solution.py:210
  3.1 3.0 %collective-permute-start.7 = (bf16[176,256]{1,0:T(8,128)(2,1)S(1)}, bf16[176,256]{1,0:T(8,128)(2,1)S(1)}, u32[]{:S(2)}, u32[]{:S(2)}) collective-permute-start(bf16[176,256]{1,0:T(8,128)(2,1)S(1)} %get-tuple-element.329), channel_id=1, source_target_pairs={{0,1},{1,0},{2,3},{3,2},{4,5},{5,4},{6,7},{7,6},{8,9},{9,8},{10,11... | collective-permute-start | bytes 270344 | tf_op jit(solution)/shard_map/ppermute | solution.py:622
  6.1 0.1 collective-permute-start.11
  6.2 1.9 %collective-permute-start.13 = (bf16[1024,256]{1,0:T(8,128)(2,1)S(1)}, bf16[1024,256]{1,0:T(8,128)(2,1)S(1)}, u32[]{:S(2)}, u32[]{:S(2)}) collective-permute-start(bf16[1024,256]{1,0:T(8,128)(2,1)S(1)} %get-tuple-element.336), channel_id=1, source_target_pairs={{0,1},{1,0},{2,3},{3,2},{4,5},{5,4},{6,7},{7,6},{8,9},{9,8},{10,11... | collective-permute-start | bytes 1572872 | tf_op jit(solution)/shard_map/ppermute | solution.py:624
  8.2 0.1 pad_add_fusion.place_ref
  8.3 1.0 %collective-permute-done.7.refs_0_ = bf16[176,256]{1,0:T(8,128)(2,1)S(1)} collective-permute-done((bf16[176,256]{1,0:T(8,128)(2,1)S(1)}, bf16[176,256]{1,0:T(8,128)(2,1)S(1)}, u32[]{:S(2)}, u32[]{:S(2)}) %collective-permute-start.7) | collective-permute-done | bytes 90144 | tf_op jit(solution)/shard_map/ppermute | solution.py:622
  9.3 3.4 %collective-permute-start.8 = (bf16[352,256]{1,0:T(8,128)(2,1)S(1)}, bf16[352,256]{1,0:T(8,128)(2,1)S(1)}, u32[]{:S(2)}, u32[]{:S(2)}) collective-permute-start(bf16[352,256]{1,0:T(8,128)(2,1)S(1)} %constant_dynamic-update-slice_fusion.refs_0_), channel_id=1, source_target_pairs={{0,4},{1,5},{2,6},{3,7},{4,0},{5,1},{6,2},{7,3},{8,12},{9,13},{10,... | collective-permute-start | bytes 540680 | tf_op jit(solution)/shard_map/ppermute | solution.py:609
  12.7 1.3 %collective-permute-start.9 = (bf16[352,256]{1,0:T(8,128)(2,1)S(1)}, bf16[352,256]{1,0:T(8,128)(2,1)S(1)}, u32[]{:S(2)}, u32[]{:S(2)}) collective-permute-start(bf16[352,256]{1,0:T(8,128)(2,1)S(1)} %constant_dynamic-update-slice_fusion.refs_0_), channel_id=1, source_target_pairs={{0,6},{1,7},{2,4},{3,5},{4,2},{5,3},{6,0},{7,1},{8,14},{9,15},{10,... | collective-permute-start | bytes 540680 | tf_op jit(solution)/shard_map/ppermute | solution.py:609
  14.1 0.2 collective-permute-start.10
  14.3 2.2 %keys.1 = (bf16[4096,256]{1,0:T(8,128)(2,1)S(1)}, bf16[192,256]{1,0:T(8,128)(2,1)S(1)}, s32[192,1]{1,0:T(8,128)S(1)}, s32[8,256]{1,0:T(8,128)S(1)}, f32[8,128]{1,0:T(8,128)S(1)}) custom-call(s32[3]{0:T(128)S(1)} %pad_add_fusion.place_ref, s32[16,128]{1,0:T(8,128)S(1)} %bitcast.17, bf16[4096,256]{1,0:T(8,128)(2,1)S(1)} %copy-done.7, ...), custom_call_target="tpu_custom_call" | custom-call | flops 2000000000 | bytes 1048576 | tf_op jit(solution)/shard_map/keys/pallas_call | solution.py:304
  16.5 0.4 locate.1
  16.9 0.0 collective-permute-done.11.refs_0_
  17.0 1.6 %collective-permute-start.12 = (bf16[512,256]{1,0:T(8,128)(2,1)S(1)}, bf16[512,256]{1,0:T(8,128)(2,1)S(1)}, u32[]{:S(2)}, u32[]{:S(2)}) collective-permute-start(bf16[512,256]{1,0:T(8,128)(2,1)S(1)} %after.5), channel_id=1, source_target_pairs={{0,16},{8,24},{16,0},{24,8},{1,17},{9,25},{17,1},{25,9},{2,18},{10... | collective-permute-start | bytes 786440 | tf_op jit(solution)/shard_map/ppermute | solution.py:630
  18.5 5.7 %collective-permute-done.8.refs_1_ = bf16[352,256]{1,0:T(8,128)(2,1)S(1)} collective-permute-done((bf16[352,256]{1,0:T(8,128)(2,1)S(1)}, bf16[352,256]{1,0:T(8,128)(2,1)S(1)}, u32[]{:S(2)}, u32[]{:S(2)}) %collective-permute-start.8) | collective-permute-done | bytes 180256 | tf_op jit(solution)/shard_map/ppermute | solution.py:609
  24.2 0.9 %early.1.early_ref = bf16[1024,256]{1,0:T(8,128)(2,1)S(1)} custom-call(s32[1]{0:T(128)} %bitcast.4.place_ref, s32[8,256]{1,0:T(8,128)S(1)} %get-tuple-element.331.loc_ref.refs_1_, bf16[352,256]{1,0:T(8,128)(2,1)S(1)} %constant_dynamic-update-slice_fusion.refs_0_, bf16[352,256]{1,0:T(8,128)(2,1)S(1)} %collective-permute-done.8.refs_1_), custom_call_target="tpu_custom_call" | custom-call | flops 2000000000 | bytes 1048576 | tf_op jit(solution)/shard_map/early/pallas_call | solution.py:344
  25.1 1.0 %arrange.1 = (bf16[1024,256]{1,0:T(8,128)(2,1)S(1)}, bf16[256,256]{1,0:T(8,128)(2,1)S(1)}, bf16[256,256]{1,0:T(8,128)(2,1)S(1)}, bf16[256,256]{1,0:T(8,128)(2,1)...) custom-call(s32[1]{0:T(128)} %bitcast.4.place_ref, s32[8,256]{1,0:T(8,128)S(1)} %get-tuple-element.331.loc_ref.refs_1_, ...), custom_call_target="tpu_custom_call" | custom-call | flops 3000000000 | bytes 1048576 | tf_op jit(solution)/shard_map/arrange/pallas_call | solution.py:369
  26.1 0.1 collective-permute-start.14
  26.2 0.5 collective-permute-start.15
  26.7 0.1 collective-permute-start.16
  26.8 5.1 %first.1 = (f32[1024,128]{1,0:T(8,128)S(1)}, f32[256,256]{1,0:T(8,128)S(1)}, f32[256,256]{1,0:T(8,128)S(1)}, f32[256,256]{1,0:T(8,128)S(1)}, f32[256,256]{1,0:T(8,128)S(1)}) custom-call(bf16[1024,256]{1,0:T(8,128)(2,1)S(1)} %get-tuple-element.334.refs_1_.query_ref, bf16[4096,256]{1,0:T(8,128)(2,1)S(1)} %get-tuple-element.333.refs_0_.keys_ref, ...), custom_call_target="tpu_custom_call" | custom-call | flops 8589934592 | bytes 1048576 | tf_op jit(solution)/shard_map/first/pallas_call | solution.py:405
  31.9 3.5 %far.1 = (f32[8,256]{1,0:T(8,128)S(1)}, bf16[256,256]{1,0:T(8,128)(2,1)S(1)}, bf16[256,256]{1,0:T(8,128)(2,1)S(1)}, bf16[256,256]{1,0:T(8,128)(2,1)S(1)}, bf16[256,256]{1,0:T(8,128)(2,1)S(1)}) custom-call(s32[1]{0:T(128)} %bitcast.4.place_ref, s32[8,256]{1,0:T(8,128)S(1)} %get-tuple-element.330.refs_1_.loc_ref, ...), custom_call_target="tpu_custom_call" | custom-call | flops 2147483648 | bytes 1048576 | tf_op jit(solution)/shard_map/far/pallas_call | solution.py:446
  35.5 2.6 %collective-permute-start.17 = (f32[8,256]{1,0:T(8,128)S(1)}, f32[8,256]{1,0:T(8,128)S(1)}, u32[]{:S(2)}, u32[]{:S(2)}) collective-permute-start(f32[8,256]{1,0:T(8,128)S(1)} %get-tuple-element.340.note_ref.gate_ref), channel_id=1, source_target_pairs={{0,2},{1,3},{2,0},{3,1},{4,6},{5,7},{6,4},{7,5},{8,10},{9,11},{10,... | collective-permute-start | bytes 24584 | tf_op jit(solution)/shard_map/ppermute | solution.py:609
  38.1 2.1 %collective-permute-start.18 = (f32[8,256]{1,0:T(8,128)S(1)}, f32[8,256]{1,0:T(8,128)S(1)}, u32[]{:S(2)}, u32[]{:S(2)}) collective-permute-start(f32[8,256]{1,0:T(8,128)S(1)} %get-tuple-element.340.note_ref.gate_ref), channel_id=1, source_target_pairs={{0,4},{1,5},{2,6},{3,7},{4,0},{5,1},{6,2},{7,3},{8,12},{9,13},{10,... | collective-permute-start | bytes 24584 | tf_op jit(solution)/shard_map/ppermute | solution.py:609
  40.2 1.2 %collective-permute-start.19 = (f32[8,256]{1,0:T(8,128)S(1)}, f32[8,256]{1,0:T(8,128)S(1)}, u32[]{:S(2)}, u32[]{:S(2)}) collective-permute-start(f32[8,256]{1,0:T(8,128)S(1)} %get-tuple-element.340.note_ref.gate_ref), channel_id=1, source_target_pairs={{0,6},{1,7},{2,4},{3,5},{4,2},{5,3},{6,0},{7,1},{8,14},{9,15},{10,... | collective-permute-start | bytes 24584 | tf_op jit(solution)/shard_map/ppermute | solution.py:609
  41.4 1.4 %last.5.pushed_ref = f32[256,256]{1,0:T(8,128)S(1)} custom-call(bf16[256,256]{1,0:T(8,128)(2,1)S(1)} %get-tuple-element.351.query_ref, f32[256,256]{1,0:T(8,128)S(1)} %get-tuple-element.352.pushed_in, f32[8,256]{1,0:T(8,128)S(1)} %get-tuple-element.340.note_ref.gate_ref, bf16[512,256]{1,0:T(8,128)(2,1)S(1)} %after.4.refs_0_, ...), custom_call_target="tpu_custom_call" | custom-call | flops 1073741824 | bytes 1048576 | tf_op jit(solution)/shard_map/last/pallas_call | solution.py:471
  42.8 1.4 %last.6.pushed_ref = f32[256,256]{1,0:T(8,128)S(1)} custom-call(bf16[256,256]{1,0:T(8,128)(2,1)S(1)} %get-tuple-element.354.query_ref, f32[256,256]{1,0:T(8,128)S(1)} %get-tuple-element.355.pushed_in, f32[8,256]{1,0:T(8,128)S(1)} %get-tuple-element.340.note_ref.gate_ref, bf16[512,256]{1,0:T(8,128)(2,1)S(1)} %after.4.refs_0_, ...), custom_call_target="tpu_custom_call" | custom-call | flops 1073741824 | bytes 1048576 | tf_op jit(solution)/shard_map/last/pallas_call | solution.py:471
  44.2 1.4 %last.7.pushed_ref = f32[256,256]{1,0:T(8,128)S(1)} custom-call(bf16[256,256]{1,0:T(8,128)(2,1)S(1)} %get-tuple-element.357.query_ref, f32[256,256]{1,0:T(8,128)S(1)} %get-tuple-element.358.pushed_in, f32[8,256]{1,0:T(8,128)S(1)} %get-tuple-element.340.note_ref.gate_ref, bf16[512,256]{1,0:T(8,128)(2,1)S(1)} %after.4.refs_0_, ...), custom_call_target="tpu_custom_call" | custom-call | flops 1073741824 | bytes 1048576 | tf_op jit(solution)/shard_map/last/pallas_call | solution.py:471
  45.7 0.1 settle.1
  45.8 0.1 collective-permute-start.20
  45.9 0.3 code.3.refs_0_
  46.3 2.1 %collective-permute-start.24 = (s16[272,256]{1,0:T(8,128)(2,1)S(1)}, s16[272,256]{1,0:T(8,128)(2,1)S(1)}, u32[]{:S(2)}, u32[]{:S(2)}) collective-permute-start(s16[272,256]{1,0:T(8,128)(2,1)S(1)} %code.3.refs_0_), channel_id=1, source_target_pairs={{0,4},{1,5},{2,6},{3,7},{4,0},{5,1},{6,2},{7,3},{8,12},{9,13},{10,... | collective-permute-start | bytes 417800 | tf_op jit(solution)/shard_map/ppermute | solution.py:609
  48.4 0.3 code.4.refs_0_
  48.7 1.2 %collective-permute-start.23 = (s16[272,256]{1,0:T(8,128)(2,1)S(1)}, s16[272,256]{1,0:T(8,128)(2,1)S(1)}, u32[]{:S(2)}, u32[]{:S(2)}) collective-permute-start(s16[272,256]{1,0:T(8,128)(2,1)S(1)} %code.4.refs_0_), channel_id=1, source_target_pairs={{0,2},{1,3},{2,0},{3,1},{4,6},{5,7},{6,4},{7,5},{8,10},{9,11},{10,... | collective-permute-start | bytes 417800 | tf_op jit(solution)/shard_map/ppermute | solution.py:609
  49.9 0.3 code.5
  50.3 1.3 %collective-permute-start.25 = (s16[272,256]{1,0:T(8,128)(2,1)S(1)}, s16[272,256]{1,0:T(8,128)(2,1)S(1)}, u32[]{:S(2)}, u32[]{:S(2)}) collective-permute-start(s16[272,256]{1,0:T(8,128)(2,1)S(1)} %code.5), channel_id=1, source_target_pairs={{0,6},{1,7},{2,4},{3,5},{4,2},{5,3},{6,0},{7,1},{8,14},{9,15},{10,... | collective-permute-start | bytes 417800 | tf_op jit(solution)/shard_map/ppermute | solution.py:609
  51.5 1.5 %collective-permute-start.21 = (f32[8,128]{1,0:T(8,128)S(1)}, f32[8,128]{1,0:T(8,128)S(1)}, u32[]{:S(2)}, u32[]{:S(2)}) collective-permute-start(f32[8,128]{1,0:T(8,128)S(1)} %add.155.refs_1_), channel_id=1, source_target_pairs={{0,1},{1,0},{2,3},{3,2},{4,5},{5,4},{6,7},{7,6},{8,9},{9,8},{10,11... | collective-permute-start | bytes 12296 | tf_op jit(solution)/shard_map/ppermute | solution.py:659
  53.0 2.1 %collective-permute-done.21 = f32[8,128]{1,0:T(8,128)S(1)} collective-permute-done((f32[8,128]{1,0:T(8,128)S(1)}, f32[8,128]{1,0:T(8,128)S(1)}, u32[]{:S(2)}, u32[]{:S(2)}) %collective-permute-start.21) | collective-permute-done | bytes 4128 | tf_op jit(solution)/shard_map/ppermute | solution.py:659
  55.1 1.5 %collective-permute-start.22 = (f32[8,128]{1,0:T(8,128)S(1)}, f32[8,128]{1,0:T(8,128)S(1)}, u32[]{:S(2)}, u32[]{:S(2)}) collective-permute-start(f32[8,128]{1,0:T(8,128)S(1)} %add.156.word_ref.gate_ref), channel_id=1, source_target_pairs={{0,16},{8,24},{16,0},{24,8},{1,17},{9,25},{17,1},{25,9},{2,18},{10... | collective-permute-start | bytes 12296 | tf_op jit(solution)/shard_map/ppermute | solution.py:659
  56.7 1.4 %last.4 = f32[256,256]{1,0:T(8,128)S(1)} custom-call(bf16[256,256]{1,0:T(8,128)(2,1)S(1)} %get-tuple-element.348.query_ref, f32[256,256]{1,0:T(8,128)S(1)} %get-tuple-element.349.pushed_in, f32[8,128]{1,0:T(8,128)S(1)} %add.156.word_ref.gate_ref, bf16[512,256]{1,0:T(8,128)(2,1)S(1)} %after.4.refs_0_, bf16[512,256]{1,0:T(8,128)(2,1)S(1)} %collective-permute-done.14.refs_1_, ...), custom_call_target="tpu_custom_call" | custom-call | flops 1073741824 | bytes 1048576 | tf_op jit(solution)/shard_map/last/pallas_call | solution.py:471
  58.1 0.6 %collective-permute-done.22.came_ref = f32[8,128]{1,0:T(8,128)S(1)} collective-permute-done((f32[8,128]{1,0:T(8,128)S(1)}, f32[8,128]{1,0:T(8,128)S(1)}, u32[]{:S(2)}, u32[]{:S(2)}) %collective-permute-start.22) | collective-permute-done | bytes 4128 | tf_op jit(solution)/shard_map/ppermute | solution.py:659
  58.8 0.6 %mean.1 = (f32[1,1]{1,0:T(1,128)}, s32[1,1]{1,0:T(1,128)}) custom-call(f32[8,128]{1,0:T(8,128)S(1)} %add.156.word_ref.gate_ref, f32[8,128]{1,0:T(8,128)S(1)} %collective-permute-done.22.came_ref), custom_call_target="tpu_custom_call" | custom-call | flops 100000000 | bytes 1048576 | tf_op jit(solution)/shard_map/mean/pallas_call | solution.py:556
  60.1 0.4 collective-permute-done.23
  60.4 0.5 conditional.1
  60.4 0.5 finish.1
  60.9 0.0 copy-start.14
  60.9 0.0 copy-start.15
  60.9 0.7 %copy-done.14 = f32[256,256]{1,0:T(8,128)} copy-done((f32[256,256]{1,0:T(8,128)}, f32[256,256]{1,0:T(8,128)S(1)}, u32[]{:S(2)}) %copy-start.14) | copy-done | bytes 262168
  (31 shorter events, 0.1 us)
Async XLA Ops:
  0.8 13.5 %copy-start.7 = (bf16[4096,256]{1,0:T(8,128)(2,1)S(1)}, bf16[4096,256]{1,0:T(8,128)(2,1)}, u32[]{:S(2)}) copy-start(bf16[4096,256]{1,0:T(8,128)(2,1)} %bank_ref.3) | copy-start | bytes 6291460
  0.8 13.5 %copy-start.12 = (s32[2048]{0:T(1024)S(1)}, s32[2048]{0:T(1024)}, u32[]{:S(2)}) copy-start(s32[2048]{0:T(1024)} %param.24) | copy-start | bytes 24580
  3.1 6.1 %collective-permute-start.7 = (bf16[176,256]{1,0:T(8,128)(2,1)S(1)}, bf16[176,256]{1,0:T(8,128)(2,1)S(1)}, u32[]{:S(2)}, u32[]{:S(2)}) collective-permute-start(bf16[176,256]{1,0:T(8,128)(2,1)S(1)} %get-tuple-element.329), channel_id=1, source_target_pairs={{0,1},{1,0},{2,3},{3,2},{4,5},{5,4},{6,7},{7,6},{8,9},{9,8},{10,11... | collective-permute-start | bytes 270344 | tf_op jit(solution)/shard_map/ppermute | solution.py:622
  6.1 10.8 %collective-permute-start.11 = (bf16[512,256]{1,0:T(8,128)(2,1)S(1)}, bf16[512,256]{1,0:T(8,128)(2,1)S(1)}, u32[]{:S(2)}, u32[]{:S(2)}) collective-permute-start(bf16[512,256]{1,0:T(8,128)(2,1)S(1)} %get-tuple-element.335), channel_id=1, source_target_pairs={{0,1},{1,0},{2,3},{3,2},{4,5},{5,4},{6,7},{7,6},{8,9},{9,8},{10,11... | collective-permute-start | bytes 786440 | tf_op jit(solution)/shard_map/ppermute | solution.py:623
  6.2 20.5 %collective-permute-start.13 = (bf16[1024,256]{1,0:T(8,128)(2,1)S(1)}, bf16[1024,256]{1,0:T(8,128)(2,1)S(1)}, u32[]{:S(2)}, u32[]{:S(2)}) collective-permute-start(bf16[1024,256]{1,0:T(8,128)(2,1)S(1)} %get-tuple-element.336), channel_id=1, source_target_pairs={{0,1},{1,0},{2,3},{3,2},{4,5},{5,4},{6,7},{7,6},{8,9},{9,8},{10,11... | collective-permute-start | bytes 1572872 | tf_op jit(solution)/shard_map/ppermute | solution.py:624
  9.3 14.9 %collective-permute-start.8 = (bf16[352,256]{1,0:T(8,128)(2,1)S(1)}, bf16[352,256]{1,0:T(8,128)(2,1)S(1)}, u32[]{:S(2)}, u32[]{:S(2)}) collective-permute-start(bf16[352,256]{1,0:T(8,128)(2,1)S(1)} %constant_dynamic-update-slice_fusion.refs_0_), channel_id=1, source_target_pairs={{0,4},{1,5},{2,6},{3,7},{4,0},{5,1},{6,2},{7,3},{8,12},{9,13},{10,... | collective-permute-start | bytes 540680 | tf_op jit(solution)/shard_map/ppermute | solution.py:609
  12.7 12.4 %collective-permute-start.9 = (bf16[352,256]{1,0:T(8,128)(2,1)S(1)}, bf16[352,256]{1,0:T(8,128)(2,1)S(1)}, u32[]{:S(2)}, u32[]{:S(2)}) collective-permute-start(bf16[352,256]{1,0:T(8,128)(2,1)S(1)} %constant_dynamic-update-slice_fusion.refs_0_), channel_id=1, source_target_pairs={{0,6},{1,7},{2,4},{3,5},{4,2},{5,3},{6,0},{7,1},{8,14},{9,15},{10,... | collective-permute-start | bytes 540680 | tf_op jit(solution)/shard_map/ppermute | solution.py:609
  14.1 11.1 %collective-permute-start.10 = (bf16[352,256]{1,0:T(8,128)(2,1)S(1)}, bf16[352,256]{1,0:T(8,128)(2,1)S(1)}, u32[]{:S(2)}, u32[]{:S(2)}) collective-permute-start(bf16[352,256]{1,0:T(8,128)(2,1)S(1)} %constant_dynamic-update-slice_fusion.refs_0_), channel_id=1, source_target_pairs={{0,2},{1,3},{2,0},{3,1},{4,6},{5,7},{6,4},{7,5},{8,10},{9,11},{10,... | collective-permute-start | bytes 540680 | tf_op jit(solution)/shard_map/ppermute | solution.py:609
  14.3 2.2 %copy-start.13 = (s32[16,128]{1,0:T(8,128)S(1)}, s32[16,128]{1,0:T(8,128)}, u32[]{:S(2)}) copy-start(s32[16,128]{1,0:T(8,128)} %pos_ref.3) | copy-start | bytes 24580
  17.0 9.3 %collective-permute-start.12 = (bf16[512,256]{1,0:T(8,128)(2,1)S(1)}, bf16[512,256]{1,0:T(8,128)(2,1)S(1)}, u32[]{:S(2)}, u32[]{:S(2)}) collective-permute-start(bf16[512,256]{1,0:T(8,128)(2,1)S(1)} %after.5), channel_id=1, source_target_pairs={{0,16},{8,24},{16,0},{24,8},{1,17},{9,25},{17,1},{25,9},{2,18},{10... | collective-permute-start | bytes 786440 | tf_op jit(solution)/shard_map/ppermute | solution.py:630
  26.1 5.8 %collective-permute-start.14 = (bf16[512,256]{1,0:T(8,128)(2,1)S(1)}, bf16[512,256]{1,0:T(8,128)(2,1)S(1)}, u32[]{:S(2)}, u32[]{:S(2)}) collective-permute-start(bf16[512,256]{1,0:T(8,128)(2,1)S(1)} %after.4.refs_0_), channel_id=1, source_target_pairs={{0,8},{8,0},{16,24},{24,16},{1,9},{9,1},{17,25},{25,17},{2,10},{10... | collective-permute-start | bytes 786440 | tf_op jit(solution)/shard_map/ppermute | solution.py:646
  26.2 5.7 %collective-permute-start.15 = (bf16[512,256]{1,0:T(8,128)(2,1)S(1)}, bf16[512,256]{1,0:T(8,128)(2,1)S(1)}, u32[]{:S(2)}, u32[]{:S(2)}) collective-permute-start(bf16[512,256]{1,0:T(8,128)(2,1)S(1)} %after.6.refs_1_.refs_2_), channel_id=1, source_target_pairs={{0,8},{8,0},{16,24},{24,16},{1,9},{9,1},{17,25},{25,17},{2,10},{10... | collective-permute-start | bytes 786440 | tf_op jit(solution)/shard_map/ppermute | solution.py:646
  26.7 5.2 %collective-permute-start.16 = (bf16[1024,256]{1,0:T(8,128)(2,1)S(1)}, bf16[1024,256]{1,0:T(8,128)(2,1)S(1)}, u32[]{:S(2)}, u32[]{:S(2)}) collective-permute-start(bf16[1024,256]{1,0:T(8,128)(2,1)S(1)} %after.7.refs_2_.refs_4_), channel_id=1, source_target_pairs={{0,8},{8,0},{16,24},{24,16},{1,9},{9,1},{17,25},{25,17},{2,10},{10... | collective-permute-start | bytes 1572872 | tf_op jit(solution)/shard_map/ppermute | solution.py:646
  35.5 10.2 %collective-permute-start.17 = (f32[8,256]{1,0:T(8,128)S(1)}, f32[8,256]{1,0:T(8,128)S(1)}, u32[]{:S(2)}, u32[]{:S(2)}) collective-permute-start(f32[8,256]{1,0:T(8,128)S(1)} %get-tuple-element.340.note_ref.gate_ref), channel_id=1, source_target_pairs={{0,2},{1,3},{2,0},{3,1},{4,6},{5,7},{6,4},{7,5},{8,10},{9,11},{10,... | collective-permute-start | bytes 24584 | tf_op jit(solution)/shard_map/ppermute | solution.py:609
  38.1 7.6 %collective-permute-start.18 = (f32[8,256]{1,0:T(8,128)S(1)}, f32[8,256]{1,0:T(8,128)S(1)}, u32[]{:S(2)}, u32[]{:S(2)}) collective-permute-start(f32[8,256]{1,0:T(8,128)S(1)} %get-tuple-element.340.note_ref.gate_ref), channel_id=1, source_target_pairs={{0,4},{1,5},{2,6},{3,7},{4,0},{5,1},{6,2},{7,3},{8,12},{9,13},{10,... | collective-permute-start | bytes 24584 | tf_op jit(solution)/shard_map/ppermute | solution.py:609
  40.2 5.5 %collective-permute-start.19 = (f32[8,256]{1,0:T(8,128)S(1)}, f32[8,256]{1,0:T(8,128)S(1)}, u32[]{:S(2)}, u32[]{:S(2)}) collective-permute-start(f32[8,256]{1,0:T(8,128)S(1)} %get-tuple-element.340.note_ref.gate_ref), channel_id=1, source_target_pairs={{0,6},{1,7},{2,4},{3,5},{4,2},{5,3},{6,0},{7,1},{8,14},{9,15},{10,... | collective-permute-start | bytes 24584 | tf_op jit(solution)/shard_map/ppermute | solution.py:609
  45.8 2.5 %collective-permute-start.20 = (f32[8,128]{1,0:T(8,128)S(1)}, f32[8,128]{1,0:T(8,128)S(1)}, u32[]{:S(2)}, u32[]{:S(2)}) collective-permute-start(f32[8,128]{1,0:T(8,128)S(1)} %get-tuple-element.343), channel_id=1, source_target_pairs={{0,8},{8,0},{16,24},{24,16},{1,9},{9,1},{17,25},{25,17},{2,10},{10... | collective-permute-start | bytes 12296 | tf_op jit(solution)/shard_map/ppermute | solution.py:659
  46.3 13.8 %collective-permute-start.24 = (s16[272,256]{1,0:T(8,128)(2,1)S(1)}, s16[272,256]{1,0:T(8,128)(2,1)S(1)}, u32[]{:S(2)}, u32[]{:S(2)}) collective-permute-start(s16[272,256]{1,0:T(8,128)(2,1)S(1)} %code.3.refs_0_), channel_id=1, source_target_pairs={{0,4},{1,5},{2,6},{3,7},{4,0},{5,1},{6,2},{7,3},{8,12},{9,13},{10,... | collective-permute-start | bytes 417800 | tf_op jit(solution)/shard_map/ppermute | solution.py:609
  48.7 11.7 %collective-permute-start.23 = (s16[272,256]{1,0:T(8,128)(2,1)S(1)}, s16[272,256]{1,0:T(8,128)(2,1)S(1)}, u32[]{:S(2)}, u32[]{:S(2)}) collective-permute-start(s16[272,256]{1,0:T(8,128)(2,1)S(1)} %code.4.refs_0_), channel_id=1, source_target_pairs={{0,2},{1,3},{2,0},{3,1},{4,6},{5,7},{6,4},{7,5},{8,10},{9,11},{10,... | collective-permute-start | bytes 417800 | tf_op jit(solution)/shard_map/ppermute | solution.py:609
  50.3 10.2 %collective-permute-start.25 = (s16[272,256]{1,0:T(8,128)(2,1)S(1)}, s16[272,256]{1,0:T(8,128)(2,1)S(1)}, u32[]{:S(2)}, u32[]{:S(2)}) collective-permute-start(s16[272,256]{1,0:T(8,128)(2,1)S(1)} %code.5), channel_id=1, source_target_pairs={{0,6},{1,7},{2,4},{3,5},{4,2},{5,3},{6,0},{7,1},{8,14},{9,15},{10,... | collective-permute-start | bytes 417800 | tf_op jit(solution)/shard_map/ppermute | solution.py:609
  51.5 3.6 %collective-permute-start.21 = (f32[8,128]{1,0:T(8,128)S(1)}, f32[8,128]{1,0:T(8,128)S(1)}, u32[]{:S(2)}, u32[]{:S(2)}) collective-permute-start(f32[8,128]{1,0:T(8,128)S(1)} %add.155.refs_1_), channel_id=1, source_target_pairs={{0,1},{1,0},{2,3},{3,2},{4,5},{5,4},{6,7},{7,6},{8,9},{9,8},{10,11... | collective-permute-start | bytes 12296 | tf_op jit(solution)/shard_map/ppermute | solution.py:659
  55.1 3.6 %collective-permute-start.22 = (f32[8,128]{1,0:T(8,128)S(1)}, f32[8,128]{1,0:T(8,128)S(1)}, u32[]{:S(2)}, u32[]{:S(2)}) collective-permute-start(f32[8,128]{1,0:T(8,128)S(1)} %add.156.word_ref.gate_ref), channel_id=1, source_target_pairs={{0,16},{8,24},{16,0},{24,8},{1,17},{9,25},{17,1},{25,9},{2,18},{10... | collective-permute-start | bytes 12296 | tf_op jit(solution)/shard_map/ppermute | solution.py:659
  56.7 3.8 %copy-start.11 = (bf16[16,64,256]{2,1,0:T(8,128)(2,1)S(1)}, bf16[16,64,256]{2,1,0:T(8,128)(2,1)}, u32[]{:S(2)}) copy-start(bf16[16,64,256]{2,1,0:T(8,128)(2,1)} %feat_ref.1) | copy-start | bytes 1572868
  60.9 0.7 %copy-start.14 = (f32[256,256]{1,0:T(8,128)}, f32[256,256]{1,0:T(8,128)S(1)}, u32[]{:S(2)}) copy-start(f32[256,256]{1,0:T(8,128)S(1)} %get-tuple-element.327) | copy-start | bytes 786436
  60.9 0.7 %copy-start.15 = (f32[256]{0:T(256)}, f32[256]{0:T(256)S(1)}, u32[]{:S(2)}) copy-start(f32[256]{0:T(256)S(1)} %get-tuple-element.361) | copy-start | bytes 3076

commit v5 on v4

--- a/solution.py
+++ b/solution.py
@@ -231,7 +231,7 @@
     most_ref[...] = jnp.broadcast_to(most, most_ref.shape)
     away = (place // 2) ^ (holder // 2)
     side = (holder % 2 + place) % 2
-    stand = jnp.where(away == 1, groups // 2 - 1, jnp.maximum(away - 1, 0))
+    stand = away // 2 + (away % 2) * (groups // 4)
     loc_ref[...] = by_owner((stand * 2 + side) * cap + ranks, owned)
 
 
@@ -321,11 +321,16 @@
     return jnp.broadcast_to(row, (128, row.shape[1])).T[:, 0:1]
 
 
-def chosen_rows(loc, parts, at):
-    column = column_of(loc.astype(F32)).astype(jnp.int32)
-    total = jnp.zeros((loc.shape[1], parts[0].shape[1]), F32)
+def columns_of(ref, place_ref, turns):
+    rows = jnp.concatenate([row_at(ref, place_ref, k) for k in range(turns)], axis=0).astype(F32)
+    rows = jnp.concatenate([rows, jnp.zeros((-turns % 128, rows.shape[1]), F32)], axis=0)
+    return rows.T.astype(jnp.int32)
+
+
+def chosen_rows(column, parts, at):
+    total = jnp.zeros((column.shape[0], parts[0].shape[1]), F32)
     for ref in parts:
-        lane = lax.broadcasted_iota(jnp.int32, (loc.shape[1], ref.shape[0]), 1)
+        lane = lax.broadcasted_iota(jnp.int32, (column.shape[0], ref.shape[0]), 1)
         table = (lane + at == column).astype(F32).astype(BF16)
         total = total + jnp.dot(table, ref[...], preferred_element_type=F32)
         at += ref.shape[0]
@@ -335,8 +340,9 @@
 def early_kernel(turns, gates, place_ref, loc_ref, *refs):
     refs = refs[gates:]
     rows = loc_ref.shape[1]
+    columns = columns_of(loc_ref, place_ref, turns)
     for k in range(turns):
-        chosen = chosen_rows(row_at(loc_ref, place_ref, k), refs[:-1], 0)
+        chosen = chosen_rows(columns[:, k : k + 1], refs[:-1], 0)
         refs[-1][k * rows : (k + 1) * rows, :] = chosen.astype(BF16)
 
 
@@ -354,9 +360,10 @@
     refs = refs[gates:]
     rows = loc_ref.shape[1]
     parts, (query_ref, raw_ref), blocks = refs[: -2 - turns], refs[-2 - turns : -turns], refs[-turns:]
+    columns = columns_of(loc_ref, place_ref, turns)
     for k in range(turns):
         span = slice(k * rows, (k + 1) * rows)
-        raw = early_ref[span, :].astype(F32) + chosen_rows(row_at(loc_ref, place_ref, k), parts, at)
+        raw = early_ref[span, :].astype(F32) + chosen_rows(columns[:, k : k + 1], parts, at)
         query = normalize(raw).astype(BF16)
         query_ref[span, :] = query
         blocks[k][...] = query
@@ -431,12 +438,14 @@
     for ref in keys:
         total = lane_sums(query_ref[...], ref, total)
     note_ref[...] = jnp.zeros(note_ref.shape, F32)
+    columns = columns_of(loc_ref, place_ref, turns)
     for t in range(turns):
         part = slice(t * rows, (t + 1) * rows)
         note_ref[t : t + 1, :] = in_lanes(total[part], jnp.sum)
-        positive = chosen_rows(row_at(loc_ref, place_ref, t), [own_ref, side_ref], 0)
+        positive = chosen_rows(columns[:, t : t + 1], [own_ref, side_ref], 0)
         outs[t][...] = positive.astype(BF16)
-        matched = in_lanes(query_ref[part, :].astype(F32) * positive, jnp.sum)
+        product = query_ref[part, :].astype(F32) * positive
+        matched = in_lanes(sum(product[:, c : c + 128] for c in range(0, product.shape[1], 128)), jnp.sum)
         note_ref[turns + t : turns + t + 1, :] = matched / SOFTMAX_TEMP
 
 
@@ -623,7 +632,10 @@
     relayed = lax.ppermute(relay_out, "bank", across)
     rest_in = lax.ppermute(rest_out, "bank", across)
     held_rows = jnp.concatenate([own_set, from_side])
-    parts = to_all([held_rows] * turns)
+    parts = [held_rows]
+    for k in range(1, turns):
+        parts.append(turn(parts[k & (k - 1)], k & -k))
+    parts = parts[::2] + parts[1::2]
 
     loc, most = locate(patch_index, place, groups, owned, cap, hw_dev, [from_side])
     over = [(c, c ^ 2) for c in range(copies)]
@@ -687,7 +699,7 @@
     in_specs = (P("dp", "bank", None), P("dp", None), P("dp"), P("bank", None))
     out_specs = (P(("dp", "bank")), P(("dp", "bank"), None), P())
     turns = mesh.shape["bank"] // 2
-    paired = turns > 1 and turns & (turns - 1) == 0 and mesh.shape["bank"] % 2 == 0
+    paired = turns > 2 and turns & (turns - 1) == 0 and mesh.shape["bank"] % 2 == 0
     copies = mesh.shape["dp"]
     paired = paired and copies > 2 and copies & (copies - 1) == 0
     return jax.shard_map(

time: 61.8 us -> 60.3 us (0.976)
  starting transfers between devices: 25.8 us -> 24.7 us
    ppermute x9, starting transfers between devices: 15.5 us -> 14.3 us  [turn(): return lax.ppermute(value, 'bank', pairs)]
  transfers between devices with their start and end apart: 19 -> 19, of which waited for: 5 -> 7; matrix products, arithmetic and copies ran while one was open for 0% -> 0% of each run, Pallas kernels for 27% -> 28%
where the time goes in v5:
time: 60.3 us; the launch traced here: 60.2 us
  starting transfers between devices  24.7 us (41%)
  Pallas kernels  23.4 us (39%)
  waiting for transfers between devices  9.5 us (16%)
  between operations  1.62 us (3%)
  local copies, waits for them, and re-layouts  0.74 us (1%)
    ppermute x9, starting transfers between devices, turn(): return lax.ppermute(value, 'bank', pairs)  14.3 us
    pallas_call x4, Pallas kernels, last(): call(last_kernel, 'last', jax.ShapeDtypeStruct((rows, channels), F32), 4...  5.74 us
    ppermute x9, waiting for transfers between devices, turn(): return lax.ppermute(value, 'bank', pairs)  5.64 us
    pallas_call x1, Pallas kernels, first(): call(functools.partial(first_kernel, turns, len(gates)), 'first', [jax.Sh...  5.07 us
    pallas_call x1, Pallas kernels, far_totals(): call(functools.partial(far_kernel, len(keys), turns), 'far', [jax.ShapeDt...  3.57 us
    ppermute x3, starting transfers between devices, on_device(): came_word = lax.ppermute(words[-1], axis, pairs)  3.08 us
    ppermute x1, starting transfers between devices, on_device(): from_side = lax.ppermute(other_set, 'bank', across)  3 us
    ppermute x3, waiting for transfers between devices, on_device(): came_word = lax.ppermute(words[-1], axis, pairs)  2.82 us
  transfers between devices with their start and end apart: 19, of which 7 were waited for; matrix products, arithmetic and copies ran while one was open for 0% of the time, Pallas kernels for 28%

profile of v5, /device:TPU:0, one launch (start us, length us, event | category | flops | bytes accessed | tf_op | source)
XLA Modules:
  0.0 60.2 jit_solution(13528049337882900024)
XLA Ops:
  0.7 0.1 pad_add_fusion.1.place_ref
  0.8 2.4 %pick.1 = (bf16[176,256]{1,0:T(8,128)(2,1)S(1)}, bf16[176,256]{1,0:T(8,128)(2,1)S(1)}, bf16[512,256]{1,0:T(8,128)(2,1)S(1)}, bf16[1024,256]{1,0:T(8,128)(2,1)S(1)}) custom-call(s32[3]{0:T(128)S(1)} %pad_add_fusion.1.place_ref, s32[16,128]{1,0:T(8,128)} %pos_ref.3, bf16[16,64,256]{2,1,0:T(8,128)(2,1)} %feat_ref.1, bf16[4096,256]{1,0:T(8,128)(2,1)} %bank_ref.3), custom_call_target="tpu_custom_call" | custom-call | flops 3000000000 | bytes 1048576 | tf_op jit(solution)/shard_map/pick/pallas_call | solution.py:210
  3.1 3.0 %collective-permute-start.7 = (bf16[176,256]{1,0:T(8,128)(2,1)S(1)}, bf16[176,256]{1,0:T(8,128)(2,1)S(1)}, u32[]{:S(2)}, u32[]{:S(2)}) collective-permute-start(bf16[176,256]{1,0:T(8,128)(2,1)S(1)} %get-tuple-element.329), channel_id=1, source_target_pairs={{0,1},{1,0},{2,3},{3,2},{4,5},{5,4},{6,7},{7,6},{8,9},{9,8},{10,11... | collective-permute-start | bytes 270344 | tf_op jit(solution)/shard_map/ppermute | solution.py:631
  6.1 0.1 collective-permute-start.11
  6.2 1.9 %collective-permute-start.13 = (bf16[1024,256]{1,0:T(8,128)(2,1)S(1)}, bf16[1024,256]{1,0:T(8,128)(2,1)S(1)}, u32[]{:S(2)}, u32[]{:S(2)}) collective-permute-start(bf16[1024,256]{1,0:T(8,128)(2,1)S(1)} %get-tuple-element.336), channel_id=1, source_target_pairs={{0,1},{1,0},{2,3},{3,2},{4,5},{5,4},{6,7},{7,6},{8,9},{9,8},{10,11... | collective-permute-start | bytes 1572872 | tf_op jit(solution)/shard_map/ppermute | solution.py:633
  8.2 0.1 pad_add_fusion.place_ref
  8.3 1.0 %collective-permute-done.7.refs_0_ = bf16[176,256]{1,0:T(8,128)(2,1)S(1)} collective-permute-done((bf16[176,256]{1,0:T(8,128)(2,1)S(1)}, bf16[176,256]{1,0:T(8,128)(2,1)S(1)}, u32[]{:S(2)}, u32[]{:S(2)}) %collective-permute-start.7) | collective-permute-done | bytes 90144 | tf_op jit(solution)/shard_map/ppermute | solution.py:631
  9.3 3.4 %collective-permute-start.8 = (bf16[352,256]{1,0:T(8,128)(2,1)S(1)}, bf16[352,256]{1,0:T(8,128)(2,1)S(1)}, u32[]{:S(2)}, u32[]{:S(2)}) collective-permute-start(bf16[352,256]{1,0:T(8,128)(2,1)S(1)} %constant_dynamic-update-slice_fusion.refs_0_), channel_id=1, source_target_pairs={{0,4},{1,5},{2,6},{3,7},{4,0},{5,1},{6,2},{7,3},{8,12},{9,13},{10,... | collective-permute-start | bytes 540680 | tf_op jit(solution)/shard_map/ppermute | solution.py:618
  12.7 1.6 %collective-permute-start.9 = (bf16[352,256]{1,0:T(8,128)(2,1)S(1)}, bf16[352,256]{1,0:T(8,128)(2,1)S(1)}, u32[]{:S(2)}, u32[]{:S(2)}) collective-permute-start(bf16[352,256]{1,0:T(8,128)(2,1)S(1)} %constant_dynamic-update-slice_fusion.refs_0_), channel_id=1, source_target_pairs={{0,2},{1,3},{2,0},{3,1},{4,6},{5,7},{6,4},{7,5},{8,10},{9,11},{10,... | collective-permute-start | bytes 540680 | tf_op jit(solution)/shard_map/ppermute | solution.py:618
  14.3 2.2 %keys.1 = (bf16[4096,256]{1,0:T(8,128)(2,1)S(1)}, bf16[192,256]{1,0:T(8,128)(2,1)S(1)}, s32[192,1]{1,0:T(8,128)S(1)}, s32[8,256]{1,0:T(8,128)S(1)}, f32[8,128]{1,0:T(8,128)S(1)}) custom-call(s32[3]{0:T(128)S(1)} %pad_add_fusion.place_ref, s32[16,128]{1,0:T(8,128)S(1)} %bitcast.17, bf16[4096,256]{1,0:T(8,128)(2,1)S(1)} %copy-done.7, ...), custom_call_target="tpu_custom_call" | custom-call | flops 2000000000 | bytes 1048576 | tf_op jit(solution)/shard_map/keys/pallas_call | solution.py:304
  16.5 0.4 locate.1
  17.0 1.6 %collective-permute-start.12 = (bf16[512,256]{1,0:T(8,128)(2,1)S(1)}, bf16[512,256]{1,0:T(8,128)(2,1)S(1)}, u32[]{:S(2)}, u32[]{:S(2)}) collective-permute-start(bf16[512,256]{1,0:T(8,128)(2,1)S(1)} %after.5), channel_id=1, source_target_pairs={{0,16},{8,24},{16,0},{24,8},{1,17},{9,25},{17,1},{25,9},{2,18},{10... | collective-permute-start | bytes 786440 | tf_op jit(solution)/shard_map/ppermute | solution.py:642
  18.5 0.9 %collective-permute-done.8.refs_1_ = bf16[352,256]{1,0:T(8,128)(2,1)S(1)} collective-permute-done((bf16[352,256]{1,0:T(8,128)(2,1)S(1)}, bf16[352,256]{1,0:T(8,128)(2,1)S(1)}, u32[]{:S(2)}, u32[]{:S(2)}) %collective-permute-start.8) | collective-permute-done | bytes 180256 | tf_op jit(solution)/shard_map/ppermute | solution.py:618
  19.5 0.3 collective-permute-start.10
  19.8 0.9 %early.1.early_ref = bf16[1024,256]{1,0:T(8,128)(2,1)S(1)} custom-call(s32[1]{0:T(128)} %bitcast.4.place_ref, s32[8,256]{1,0:T(8,128)S(1)} %get-tuple-element.331.loc_ref.refs_1_, bf16[352,256]{1,0:T(8,128)(2,1)S(1)} %constant_dynamic-update-slice_fusion.refs_0_, bf16[352,256]{1,0:T(8,128)(2,1)S(1)} %collective-permute-done.8.refs_1_), custom_call_target="tpu_custom_call" | custom-call | flops 2000000000 | bytes 1048576 | tf_op jit(solution)/shard_map/early/pallas_call | solution.py:350
  20.7 4.3 %collective-permute-done.10.refs_3_ = bf16[352,256]{1,0:T(8,128)(2,1)S(1)} collective-permute-done((bf16[352,256]{1,0:T(8,128)(2,1)S(1)}, bf16[352,256]{1,0:T(8,128)(2,1)S(1)}, u32[]{:S(2)}, u32[]{:S(2)}) %collective-permute-start.10) | collective-permute-done | bytes 180256 | tf_op jit(solution)/shard_map/ppermute | solution.py:618
  25.0 1.0 %arrange.1 = (bf16[1024,256]{1,0:T(8,128)(2,1)S(1)}, bf16[256,256]{1,0:T(8,128)(2,1)S(1)}, bf16[256,256]{1,0:T(8,128)(2,1)S(1)}, bf16[256,256]{1,0:T(8,128)(2,1)...) custom-call(s32[1]{0:T(128)} %bitcast.4.place_ref, s32[8,256]{1,0:T(8,128)S(1)} %get-tuple-element.331.loc_ref.refs_1_, ...), custom_call_target="tpu_custom_call" | custom-call | flops 3000000000 | bytes 1048576 | tf_op jit(solution)/shard_map/arrange/pallas_call | solution.py:376
  26.0 0.1 collective-permute-start.14
  26.1 0.5 collective-permute-start.15
  26.6 0.1 collective-permute-start.16
  26.6 5.1 %first.1 = (f32[1024,128]{1,0:T(8,128)S(1)}, f32[256,256]{1,0:T(8,128)S(1)}, f32[256,256]{1,0:T(8,128)S(1)}, f32[256,256]{1,0:T(8,128)S(1)}, f32[256,256]{1,0:T(8,128)S(1)}) custom-call(bf16[1024,256]{1,0:T(8,128)(2,1)S(1)} %get-tuple-element.334.refs_1_.query_ref, bf16[4096,256]{1,0:T(8,128)(2,1)S(1)} %get-tuple-element.333.refs_0_.keys_ref, ...), custom_call_target="tpu_custom_call" | custom-call | flops 8589934592 | bytes 1048576 | tf_op jit(solution)/shard_map/first/pallas_call | solution.py:412
  31.8 3.6 %far.1 = (f32[8,256]{1,0:T(8,128)S(1)}, bf16[256,256]{1,0:T(8,128)(2,1)S(1)}, bf16[256,256]{1,0:T(8,128)(2,1)S(1)}, bf16[256,256]{1,0:T(8,128)(2,1)S(1)}, bf16[256,256]{1,0:T(8,128)(2,1)S(1)}) custom-call(s32[1]{0:T(128)} %bitcast.4.place_ref, s32[8,256]{1,0:T(8,128)S(1)} %get-tuple-element.330.refs_1_.loc_ref, ...), custom_call_target="tpu_custom_call" | custom-call | flops 2147483648 | bytes 1048576 | tf_op jit(solution)/shard_map/far/pallas_call | solution.py:455
  35.3 1.0 %collective-permute-start.17 = (f32[8,256]{1,0:T(8,128)S(1)}, f32[8,256]{1,0:T(8,128)S(1)}, u32[]{:S(2)}, u32[]{:S(2)}) collective-permute-start(f32[8,256]{1,0:T(8,128)S(1)} %get-tuple-element.340.note_ref.gate_ref), channel_id=1, source_target_pairs={{0,2},{1,3},{2,0},{3,1},{4,6},{5,7},{6,4},{7,5},{8,10},{9,11},{10,... | collective-permute-start | bytes 24584 | tf_op jit(solution)/shard_map/ppermute | solution.py:618
  36.4 2.8 %collective-permute-start.18 = (f32[8,256]{1,0:T(8,128)S(1)}, f32[8,256]{1,0:T(8,128)S(1)}, u32[]{:S(2)}, u32[]{:S(2)}) collective-permute-start(f32[8,256]{1,0:T(8,128)S(1)} %get-tuple-element.340.note_ref.gate_ref), channel_id=1, source_target_pairs={{0,4},{1,5},{2,6},{3,7},{4,0},{5,1},{6,2},{7,3},{8,12},{9,13},{10,... | collective-permute-start | bytes 24584 | tf_op jit(solution)/shard_map/ppermute | solution.py:618
  39.1 0.7 %collective-permute-start.19 = (f32[8,256]{1,0:T(8,128)S(1)}, f32[8,256]{1,0:T(8,128)S(1)}, u32[]{:S(2)}, u32[]{:S(2)}) collective-permute-start(f32[8,256]{1,0:T(8,128)S(1)} %get-tuple-element.340.note_ref.gate_ref), channel_id=1, source_target_pairs={{0,6},{1,7},{2,4},{3,5},{4,2},{5,3},{6,0},{7,1},{8,14},{9,15},{10,... | collective-permute-start | bytes 24584 | tf_op jit(solution)/shard_map/ppermute | solution.py:618
  39.8 1.4 %last.5.pushed_ref = f32[256,256]{1,0:T(8,128)S(1)} custom-call(bf16[256,256]{1,0:T(8,128)(2,1)S(1)} %get-tuple-element.351.query_ref, f32[256,256]{1,0:T(8,128)S(1)} %get-tuple-element.352.pushed_in, f32[8,256]{1,0:T(8,128)S(1)} %get-tuple-element.340.note_ref.gate_ref, bf16[512,256]{1,0:T(8,128)(2,1)S(1)} %after.4.refs_0_, ...), custom_call_target="tpu_custom_call" | custom-call | flops 1073741824 | bytes 1048576 | tf_op jit(solution)/shard_map/last/pallas_call | solution.py:480
  41.2 1.4 %last.6.pushed_ref = f32[256,256]{1,0:T(8,128)S(1)} custom-call(bf16[256,256]{1,0:T(8,128)(2,1)S(1)} %get-tuple-element.354.query_ref, f32[256,256]{1,0:T(8,128)S(1)} %get-tuple-element.355.pushed_in, f32[8,256]{1,0:T(8,128)S(1)} %get-tuple-element.340.note_ref.gate_ref, bf16[512,256]{1,0:T(8,128)(2,1)S(1)} %after.4.refs_0_, ...), custom_call_target="tpu_custom_call" | custom-call | flops 1073741824 | bytes 1048576 | tf_op jit(solution)/shard_map/last/pallas_call | solution.py:480
  42.7 1.4 %last.7.pushed_ref = f32[256,256]{1,0:T(8,128)S(1)} custom-call(bf16[256,256]{1,0:T(8,128)(2,1)S(1)} %get-tuple-element.357.query_ref, f32[256,256]{1,0:T(8,128)S(1)} %get-tuple-element.358.pushed_in, f32[8,256]{1,0:T(8,128)S(1)} %get-tuple-element.340.note_ref.gate_ref, bf16[512,256]{1,0:T(8,128)(2,1)S(1)} %after.4.refs_0_, ...), custom_call_target="tpu_custom_call" | custom-call | flops 1073741824 | bytes 1048576 | tf_op jit(solution)/shard_map/last/pallas_call | solution.py:480
  44.1 0.4 collective-permute-done.19.refs_2_
  44.6 0.1 settle.1
  44.7 0.1 collective-permute-start.20
  44.8 0.3 code.3.refs_0_
  45.1 0.8 %collective-permute-start.24 = (s16[272,256]{1,0:T(8,128)(2,1)S(1)}, s16[272,256]{1,0:T(8,128)(2,1)S(1)}, u32[]{:S(2)}, u32[]{:S(2)}) collective-permute-start(s16[272,256]{1,0:T(8,128)(2,1)S(1)} %code.3.refs_0_), channel_id=1, source_target_pairs={{0,4},{1,5},{2,6},{3,7},{4,0},{5,1},{6,2},{7,3},{8,12},{9,13},{10,... | collective-permute-start | bytes 417800 | tf_op jit(solution)/shard_map/ppermute | solution.py:618
  45.9 0.1 collective-permute-done.20
  45.9 0.3 code.4.refs_0_
  46.3 2.6 %collective-permute-start.23 = (s16[272,256]{1,0:T(8,128)(2,1)S(1)}, s16[272,256]{1,0:T(8,128)(2,1)S(1)}, u32[]{:S(2)}, u32[]{:S(2)}) collective-permute-start(s16[272,256]{1,0:T(8,128)(2,1)S(1)} %code.4.refs_0_), channel_id=1, source_target_pairs={{0,2},{1,3},{2,0},{3,1},{4,6},{5,7},{6,4},{7,5},{8,10},{9,11},{10,... | collective-permute-start | bytes 417800 | tf_op jit(solution)/shard_map/ppermute | solution.py:618
  48.9 0.3 code.5
  49.2 1.2 %collective-permute-start.25 = (s16[272,256]{1,0:T(8,128)(2,1)S(1)}, s16[272,256]{1,0:T(8,128)(2,1)S(1)}, u32[]{:S(2)}, u32[]{:S(2)}) collective-permute-start(s16[272,256]{1,0:T(8,128)(2,1)S(1)} %code.5), channel_id=1, source_target_pairs={{0,6},{1,7},{2,4},{3,5},{4,2},{5,3},{6,0},{7,1},{8,14},{9,15},{10,... | collective-permute-start | bytes 417800 | tf_op jit(solution)/shard_map/ppermute | solution.py:618
  50.4 1.5 %collective-permute-start.21 = (f32[8,128]{1,0:T(8,128)S(1)}, f32[8,128]{1,0:T(8,128)S(1)}, u32[]{:S(2)}, u32[]{:S(2)}) collective-permute-start(f32[8,128]{1,0:T(8,128)S(1)} %add.155.refs_1_), channel_id=1, source_target_pairs={{0,1},{1,0},{2,3},{3,2},{4,5},{5,4},{6,7},{7,6},{8,9},{9,8},{10,11... | collective-permute-start | bytes 12296 | tf_op jit(solution)/shard_map/ppermute | solution.py:671
  51.9 2.1 %collective-permute-done.21 = f32[8,128]{1,0:T(8,128)S(1)} collective-permute-done((f32[8,128]{1,0:T(8,128)S(1)}, f32[8,128]{1,0:T(8,128)S(1)}, u32[]{:S(2)}, u32[]{:S(2)}) %collective-permute-start.21) | collective-permute-done | bytes 4128 | tf_op jit(solution)/shard_map/ppermute | solution.py:671
  54.0 1.5 %collective-permute-start.22 = (f32[8,128]{1,0:T(8,128)S(1)}, f32[8,128]{1,0:T(8,128)S(1)}, u32[]{:S(2)}, u32[]{:S(2)}) collective-permute-start(f32[8,128]{1,0:T(8,128)S(1)} %add.156.word_ref.gate_ref), channel_id=1, source_target_pairs={{0,16},{8,24},{16,0},{24,8},{1,17},{9,25},{17,1},{25,9},{2,18},{10... | collective-permute-start | bytes 12296 | tf_op jit(solution)/shard_map/ppermute | solution.py:671
  55.5 1.4 %last.4 = f32[256,256]{1,0:T(8,128)S(1)} custom-call(bf16[256,256]{1,0:T(8,128)(2,1)S(1)} %get-tuple-element.348.query_ref, f32[256,256]{1,0:T(8,128)S(1)} %get-tuple-element.349.pushed_in, f32[8,128]{1,0:T(8,128)S(1)} %add.156.word_ref.gate_ref, bf16[512,256]{1,0:T(8,128)(2,1)S(1)} %after.4.refs_0_, bf16[512,256]{1,0:T(8,128)(2,1)S(1)} %collective-permute-done.14.refs_1_, ...), custom_call_target="tpu_custom_call" | custom-call | flops 1073741824 | bytes 1048576 | tf_op jit(solution)/shard_map/last/pallas_call | solution.py:480
  57.0 0.6 %collective-permute-done.22.came_ref = f32[8,128]{1,0:T(8,128)S(1)} collective-permute-done((f32[8,128]{1,0:T(8,128)S(1)}, f32[8,128]{1,0:T(8,128)S(1)}, u32[]{:S(2)}, u32[]{:S(2)}) %collective-permute-start.22) | collective-permute-done | bytes 4128 | tf_op jit(solution)/shard_map/ppermute | solution.py:671
  57.6 0.6 %mean.1 = (f32[1,1]{1,0:T(1,128)}, s32[1,1]{1,0:T(1,128)}) custom-call(f32[8,128]{1,0:T(8,128)S(1)} %add.156.word_ref.gate_ref, f32[8,128]{1,0:T(8,128)S(1)} %collective-permute-done.22.came_ref), custom_call_target="tpu_custom_call" | custom-call | flops 100000000 | bytes 1048576 | tf_op jit(solution)/shard_map/mean/pallas_call | solution.py:565
  59.0 0.5 conditional.1
  59.0 0.5 finish.1
  59.5 0.0 copy-start.15
  59.5 0.7 %copy-done.14 = f32[256,256]{1,0:T(8,128)} copy-done((f32[256,256]{1,0:T(8,128)}, f32[256,256]{1,0:T(8,128)S(1)}, u32[]{:S(2)}) %copy-start.14) | copy-done | bytes 262168
  (31 shorter events, 0.1 us)
Async XLA Ops:
  0.8 13.5 %copy-start.7 = (bf16[4096,256]{1,0:T(8,128)(2,1)S(1)}, bf16[4096,256]{1,0:T(8,128)(2,1)}, u32[]{:S(2)}) copy-start(bf16[4096,256]{1,0:T(8,128)(2,1)} %bank_ref.3) | copy-start | bytes 6291460
  0.8 13.5 %copy-start.12 = (s32[2048]{0:T(1024)S(1)}, s32[2048]{0:T(1024)}, u32[]{:S(2)}) copy-start(s32[2048]{0:T(1024)} %param.24) | copy-start | bytes 24580
  3.1 6.1 %collective-permute-start.7 = (bf16[176,256]{1,0:T(8,128)(2,1)S(1)}, bf16[176,256]{1,0:T(8,128)(2,1)S(1)}, u32[]{:S(2)}, u32[]{:S(2)}) collective-permute-start(bf16[176,256]{1,0:T(8,128)(2,1)S(1)} %get-tuple-element.329), channel_id=1, source_target_pairs={{0,1},{1,0},{2,3},{3,2},{4,5},{5,4},{6,7},{7,6},{8,9},{9,8},{10,11... | collective-permute-start | bytes 270344 | tf_op jit(solution)/shard_map/ppermute | solution.py:631
  6.1 10.8 %collective-permute-start.11 = (bf16[512,256]{1,0:T(8,128)(2,1)S(1)}, bf16[512,256]{1,0:T(8,128)(2,1)S(1)}, u32[]{:S(2)}, u32[]{:S(2)}) collective-permute-start(bf16[512,256]{1,0:T(8,128)(2,1)S(1)} %get-tuple-element.335), channel_id=1, source_target_pairs={{0,1},{1,0},{2,3},{3,2},{4,5},{5,4},{6,7},{7,6},{8,9},{9,8},{10,11... | collective-permute-start | bytes 786440 | tf_op jit(solution)/shard_map/ppermute | solution.py:632
  6.2 20.3 %collective-permute-start.13 = (bf16[1024,256]{1,0:T(8,128)(2,1)S(1)}, bf16[1024,256]{1,0:T(8,128)(2,1)S(1)}, u32[]{:S(2)}, u32[]{:S(2)}) collective-permute-start(bf16[1024,256]{1,0:T(8,128)(2,1)S(1)} %get-tuple-element.336), channel_id=1, source_target_pairs={{0,1},{1,0},{2,3},{3,2},{4,5},{5,4},{6,7},{7,6},{8,9},{9,8},{10,11... | collective-permute-start | bytes 1572872 | tf_op jit(solution)/shard_map/ppermute | solution.py:633
  9.3 10.2 %collective-permute-start.8 = (bf16[352,256]{1,0:T(8,128)(2,1)S(1)}, bf16[352,256]{1,0:T(8,128)(2,1)S(1)}, u32[]{:S(2)}, u32[]{:S(2)}) collective-permute-start(bf16[352,256]{1,0:T(8,128)(2,1)S(1)} %constant_dynamic-update-slice_fusion.refs_0_), channel_id=1, source_target_pairs={{0,4},{1,5},{2,6},{3,7},{4,0},{5,1},{6,2},{7,3},{8,12},{9,13},{10,... | collective-permute-start | bytes 540680 | tf_op jit(solution)/shard_map/ppermute | solution.py:618
  12.7 8.0 %collective-permute-start.9 = (bf16[352,256]{1,0:T(8,128)(2,1)S(1)}, bf16[352,256]{1,0:T(8,128)(2,1)S(1)}, u32[]{:S(2)}, u32[]{:S(2)}) collective-permute-start(bf16[352,256]{1,0:T(8,128)(2,1)S(1)} %constant_dynamic-update-slice_fusion.refs_0_), channel_id=1, source_target_pairs={{0,2},{1,3},{2,0},{3,1},{4,6},{5,7},{6,4},{7,5},{8,10},{9,11},{10,... | collective-permute-start | bytes 540680 | tf_op jit(solution)/shard_map/ppermute | solution.py:618
  14.3 2.2 %copy-start.13 = (s32[16,128]{1,0:T(8,128)S(1)}, s32[16,128]{1,0:T(8,128)}, u32[]{:S(2)}) copy-start(s32[16,128]{1,0:T(8,128)} %pos_ref.3) | copy-start | bytes 24580
  17.0 9.1 %collective-permute-start.12 = (bf16[512,256]{1,0:T(8,128)(2,1)S(1)}, bf16[512,256]{1,0:T(8,128)(2,1)S(1)}, u32[]{:S(2)}, u32[]{:S(2)}) collective-permute-start(bf16[512,256]{1,0:T(8,128)(2,1)S(1)} %after.5), channel_id=1, source_target_pairs={{0,16},{8,24},{16,0},{24,8},{1,17},{9,25},{17,1},{25,9},{2,18},{10... | collective-permute-start | bytes 786440 | tf_op jit(solution)/shard_map/ppermute | solution.py:642
  19.5 5.5 %collective-permute-start.10 = (bf16[352,256]{1,0:T(8,128)(2,1)S(1)}, bf16[352,256]{1,0:T(8,128)(2,1)S(1)}, u32[]{:S(2)}, u32[]{:S(2)}) collective-permute-start(bf16[352,256]{1,0:T(8,128)(2,1)S(1)} %collective-permute-done.8.refs_1_), channel_id=1, source_target_pairs={{0,2},{1,3},{2,0},{3,1},{4,6},{5,7},{6,4},{7,5},{8,10},{9,11},{10,... | collective-permute-start | bytes 540680 | tf_op jit(solution)/shard_map/ppermute | solution.py:618
  26.0 5.8 %collective-permute-start.14 = (bf16[512,256]{1,0:T(8,128)(2,1)S(1)}, bf16[512,256]{1,0:T(8,128)(2,1)S(1)}, u32[]{:S(2)}, u32[]{:S(2)}) collective-permute-start(bf16[512,256]{1,0:T(8,128)(2,1)S(1)} %after.4.refs_0_), channel_id=1, source_target_pairs={{0,8},{8,0},{16,24},{24,16},{1,9},{9,1},{17,25},{25,17},{2,10},{10... | collective-permute-start | bytes 786440 | tf_op jit(solution)/shard_map/ppermute | solution.py:658
  26.1 5.7 %collective-permute-start.15 = (bf16[512,256]{1,0:T(8,128)(2,1)S(1)}, bf16[512,256]{1,0:T(8,128)(2,1)S(1)}, u32[]{:S(2)}, u32[]{:S(2)}) collective-permute-start(bf16[512,256]{1,0:T(8,128)(2,1)S(1)} %after.6.refs_1_.refs_2_), channel_id=1, source_target_pairs={{0,8},{8,0},{16,24},{24,16},{1,9},{9,1},{17,25},{25,17},{2,10},{10... | collective-permute-start | bytes 786440 | tf_op jit(solution)/shard_map/ppermute | solution.py:658
  26.6 5.2 %collective-permute-start.16 = (bf16[1024,256]{1,0:T(8,128)(2,1)S(1)}, bf16[1024,256]{1,0:T(8,128)(2,1)S(1)}, u32[]{:S(2)}, u32[]{:S(2)}) collective-permute-start(bf16[1024,256]{1,0:T(8,128)(2,1)S(1)} %after.7.refs_2_.refs_4_), channel_id=1, source_target_pairs={{0,8},{8,0},{16,24},{24,16},{1,9},{9,1},{17,25},{25,17},{2,10},{10... | collective-permute-start | bytes 1572872 | tf_op jit(solution)/shard_map/ppermute | solution.py:658
  35.3 8.8 %collective-permute-start.17 = (f32[8,256]{1,0:T(8,128)S(1)}, f32[8,256]{1,0:T(8,128)S(1)}, u32[]{:S(2)}, u32[]{:S(2)}) collective-permute-start(f32[8,256]{1,0:T(8,128)S(1)} %get-tuple-element.340.note_ref.gate_ref), channel_id=1, source_target_pairs={{0,2},{1,3},{2,0},{3,1},{4,6},{5,7},{6,4},{7,5},{8,10},{9,11},{10,... | collective-permute-start | bytes 24584 | tf_op jit(solution)/shard_map/ppermute | solution.py:618
  36.4 7.8 %collective-permute-start.18 = (f32[8,256]{1,0:T(8,128)S(1)}, f32[8,256]{1,0:T(8,128)S(1)}, u32[]{:S(2)}, u32[]{:S(2)}) collective-permute-start(f32[8,256]{1,0:T(8,128)S(1)} %get-tuple-element.340.note_ref.gate_ref), channel_id=1, source_target_pairs={{0,4},{1,5},{2,6},{3,7},{4,0},{5,1},{6,2},{7,3},{8,12},{9,13},{10,... | collective-permute-start | bytes 24584 | tf_op jit(solution)/shard_map/ppermute | solution.py:618
  39.1 5.4 %collective-permute-start.19 = (f32[8,256]{1,0:T(8,128)S(1)}, f32[8,256]{1,0:T(8,128)S(1)}, u32[]{:S(2)}, u32[]{:S(2)}) collective-permute-start(f32[8,256]{1,0:T(8,128)S(1)} %get-tuple-element.340.note_ref.gate_ref), channel_id=1, source_target_pairs={{0,6},{1,7},{2,4},{3,5},{4,2},{5,3},{6,0},{7,1},{8,14},{9,15},{10,... | collective-permute-start | bytes 24584 | tf_op jit(solution)/shard_map/ppermute | solution.py:618
  44.7 1.2 %collective-permute-start.20 = (f32[8,128]{1,0:T(8,128)S(1)}, f32[8,128]{1,0:T(8,128)S(1)}, u32[]{:S(2)}, u32[]{:S(2)}) collective-permute-start(f32[8,128]{1,0:T(8,128)S(1)} %get-tuple-element.343), channel_id=1, source_target_pairs={{0,8},{8,0},{16,24},{24,16},{1,9},{9,1},{17,25},{25,17},{2,10},{10... | collective-permute-start | bytes 12296 | tf_op jit(solution)/shard_map/ppermute | solution.py:671
  45.1 13.8 %collective-permute-start.24 = (s16[272,256]{1,0:T(8,128)(2,1)S(1)}, s16[272,256]{1,0:T(8,128)(2,1)S(1)}, u32[]{:S(2)}, u32[]{:S(2)}) collective-permute-start(s16[272,256]{1,0:T(8,128)(2,1)S(1)} %code.3.refs_0_), channel_id=1, source_target_pairs={{0,4},{1,5},{2,6},{3,7},{4,0},{5,1},{6,2},{7,3},{8,12},{9,13},{10,... | collective-permute-start | bytes 417800 | tf_op jit(solution)/shard_map/ppermute | solution.py:618
  46.3 12.7 %collective-permute-start.23 = (s16[272,256]{1,0:T(8,128)(2,1)S(1)}, s16[272,256]{1,0:T(8,128)(2,1)S(1)}, u32[]{:S(2)}, u32[]{:S(2)}) collective-permute-start(s16[272,256]{1,0:T(8,128)(2,1)S(1)} %code.4.refs_0_), channel_id=1, source_target_pairs={{0,2},{1,3},{2,0},{3,1},{4,6},{5,7},{6,4},{7,5},{8,10},{9,11},{10,... | collective-permute-start | bytes 417800 | tf_op jit(solution)/shard_map/ppermute | solution.py:618
  49.2 9.7 %collective-permute-start.25 = (s16[272,256]{1,0:T(8,128)(2,1)S(1)}, s16[272,256]{1,0:T(8,128)(2,1)S(1)}, u32[]{:S(2)}, u32[]{:S(2)}) collective-permute-start(s16[272,256]{1,0:T(8,128)(2,1)S(1)} %code.5), channel_id=1, source_target_pairs={{0,6},{1,7},{2,4},{3,5},{4,2},{5,3},{6,0},{7,1},{8,14},{9,15},{10,... | collective-permute-start | bytes 417800 | tf_op jit(solution)/shard_map/ppermute | solution.py:618
  50.4 3.6 %collective-permute-start.21 = (f32[8,128]{1,0:T(8,128)S(1)}, f32[8,128]{1,0:T(8,128)S(1)}, u32[]{:S(2)}, u32[]{:S(2)}) collective-permute-start(f32[8,128]{1,0:T(8,128)S(1)} %add.155.refs_1_), channel_id=1, source_target_pairs={{0,1},{1,0},{2,3},{3,2},{4,5},{5,4},{6,7},{7,6},{8,9},{9,8},{10,11... | collective-permute-start | bytes 12296 | tf_op jit(solution)/shard_map/ppermute | solution.py:671
  54.0 3.6 %collective-permute-start.22 = (f32[8,128]{1,0:T(8,128)S(1)}, f32[8,128]{1,0:T(8,128)S(1)}, u32[]{:S(2)}, u32[]{:S(2)}) collective-permute-start(f32[8,128]{1,0:T(8,128)S(1)} %add.156.word_ref.gate_ref), channel_id=1, source_target_pairs={{0,16},{8,24},{16,0},{24,8},{1,17},{9,25},{17,1},{25,9},{2,18},{10... | collective-permute-start | bytes 12296 | tf_op jit(solution)/shard_map/ppermute | solution.py:671
  55.5 3.4 %copy-start.11 = (bf16[16,64,256]{2,1,0:T(8,128)(2,1)S(1)}, bf16[16,64,256]{2,1,0:T(8,128)(2,1)}, u32[]{:S(2)}) copy-start(bf16[16,64,256]{2,1,0:T(8,128)(2,1)} %feat_ref.1) | copy-start | bytes 1572868
  59.4 0.7 %copy-start.14 = (f32[256,256]{1,0:T(8,128)}, f32[256,256]{1,0:T(8,128)S(1)}, u32[]{:S(2)}) copy-start(f32[256,256]{1,0:T(8,128)S(1)} %get-tuple-element.327) | copy-start | bytes 786436
  59.5 0.7 %copy-start.15 = (f32[256]{0:T(256)}, f32[256]{0:T(256)S(1)}, u32[]{:S(2)}) copy-start(f32[256]{0:T(256)S(1)} %get-tuple-element.361) | copy-start | bytes 3076

commit v6 on v5

--- a/solution.py
+++ b/solution.py
@@ -433,7 +433,9 @@
 def far_kernel(count, turns, place_ref, loc_ref, query_ref, total_in, own_ref, list_ref, *refs):
     keys, note_ref, outs, side_ref = refs[:count], refs[count], refs[count + 1 : -1], refs[-1]
     rows = note_ref.shape[1]
-    side_ref[...] = listed_rows(list_ref[...], keys).astype(BF16)
+    cap = own_ref.shape[0]
+    side_ref[:cap, :] = own_ref[...]
+    side_ref[cap:, :] = listed_rows(list_ref[...], keys).astype(BF16)
     total = total_in[...]
     for ref in keys:
         total = lane_sums(query_ref[...], ref, total)
@@ -442,7 +444,7 @@
     for t in range(turns):
         part = slice(t * rows, (t + 1) * rows)
         note_ref[t : t + 1, :] = in_lanes(total[part], jnp.sum)
-        positive = chosen_rows(columns[:, t : t + 1], [own_ref, side_ref], 0)
+        positive = chosen_rows(columns[:, t : t + 1], [side_ref], 0)
         outs[t][...] = positive.astype(BF16)
         product = query_ref[part, :].astype(F32) * positive
         matched = in_lanes(sum(product[:, c : c + 128] for c in range(0, product.shape[1], 128)), jnp.sum)
@@ -459,7 +461,7 @@
         2 * query.shape[0] * sum(k.shape[0] for k in keys) * channels,
         room=24,
         in_specs=[SCALARS] + [NEAR] * (5 + len(keys)),
-        scratch_shapes=[pltpu.VMEM(own.shape, BF16)],
+        scratch_shapes=[pltpu.VMEM((2 * own.shape[0], channels), BF16)],
     )(place, loc, query, total, own, listed, *keys)
     return out[0], out[1:]
 

time: 60.3 us -> 60.2 us (level)
  no operation moved by 1% of the time
where the time goes in v6:
time: 60.2 us; the launch traced here: 60.1 us
  starting transfers between devices  24.6 us (41%)
  Pallas kernels  23.4 us (39%)
  waiting for transfers between devices  9.52 us (16%)
  between operations  1.62 us (3%)
  local copies, waits for them, and re-layouts  0.74 us (1%)
    ppermute x9, starting transfers between devices, turn(): return lax.ppermute(value, 'bank', pairs)  14.3 us
    pallas_call x4, Pallas kernels, last(): call(last_kernel, 'last', jax.ShapeDtypeStruct((rows, channels), F32), 4...  5.74 us
    ppermute x9, waiting for transfers between devices, turn(): return lax.ppermute(value, 'bank', pairs)  5.64 us
    pallas_call x1, Pallas kernels, first(): call(functools.partial(first_kernel, turns, len(gates)), 'first', [jax.Sh...  5.07 us
    pallas_call x1, Pallas kernels, far_totals(): call(functools.partial(far_kernel, len(keys), turns), 'far', [jax.ShapeDt...  3.48 us
    ppermute x3, starting transfers between devices, on_device(): came_word = lax.ppermute(words[-1], axis, pairs)  3.08 us
    ppermute x1, starting transfers between devices, on_device(): from_side = lax.ppermute(other_set, 'bank', across)  3 us
    ppermute x3, waiting for transfers between devices, on_device(): came_word = lax.ppermute(words[-1], axis, pairs)  2.84 us
  transfers between devices with their start and end apart: 19, of which 7 were waited for; matrix products, arithmetic and copies ran while one was open for 0% of the time, Pallas kernels for 28%

profile of v6, /device:TPU:0, one launch (start us, length us, event | category | flops | bytes accessed | tf_op | source)
XLA Modules:
  0.0 60.1 jit_solution(3518845542346389991)
XLA Ops:
  0.7 0.1 pad_add_fusion.1.place_ref
  0.8 2.4 %pick.1 = (bf16[176,256]{1,0:T(8,128)(2,1)S(1)}, bf16[176,256]{1,0:T(8,128)(2,1)S(1)}, bf16[512,256]{1,0:T(8,128)(2,1)S(1)}, bf16[1024,256]{1,0:T(8,128)(2,1)S(1)}) custom-call(s32[3]{0:T(128)S(1)} %pad_add_fusion.1.place_ref, s32[16,128]{1,0:T(8,128)} %pos_ref.3, bf16[16,64,256]{2,1,0:T(8,128)(2,1)} %feat_ref.1, bf16[4096,256]{1,0:T(8,128)(2,1)} %bank_ref.3), custom_call_target="tpu_custom_call" | custom-call | flops 3000000000 | bytes 1048576 | tf_op jit(solution)/shard_map/pick/pallas_call | solution.py:210
  3.1 3.0 %collective-permute-start.7 = (bf16[176,256]{1,0:T(8,128)(2,1)S(1)}, bf16[176,256]{1,0:T(8,128)(2,1)S(1)}, u32[]{:S(2)}, u32[]{:S(2)}) collective-permute-start(bf16[176,256]{1,0:T(8,128)(2,1)S(1)} %get-tuple-element.329), channel_id=1, source_target_pairs={{0,1},{1,0},{2,3},{3,2},{4,5},{5,4},{6,7},{7,6},{8,9},{9,8},{10,11... | collective-permute-start | bytes 270344 | tf_op jit(solution)/shard_map/ppermute | solution.py:633
  6.1 0.1 collective-permute-start.11
  6.2 1.9 %collective-permute-start.13 = (bf16[1024,256]{1,0:T(8,128)(2,1)S(1)}, bf16[1024,256]{1,0:T(8,128)(2,1)S(1)}, u32[]{:S(2)}, u32[]{:S(2)}) collective-permute-start(bf16[1024,256]{1,0:T(8,128)(2,1)S(1)} %get-tuple-element.336), channel_id=1, source_target_pairs={{0,1},{1,0},{2,3},{3,2},{4,5},{5,4},{6,7},{7,6},{8,9},{9,8},{10,11... | collective-permute-start | bytes 1572872 | tf_op jit(solution)/shard_map/ppermute | solution.py:635
  8.2 0.1 pad_add_fusion.place_ref
  8.3 1.0 %collective-permute-done.7.refs_0_ = bf16[176,256]{1,0:T(8,128)(2,1)S(1)} collective-permute-done((bf16[176,256]{1,0:T(8,128)(2,1)S(1)}, bf16[176,256]{1,0:T(8,128)(2,1)S(1)}, u32[]{:S(2)}, u32[]{:S(2)}) %collective-permute-start.7) | collective-permute-done | bytes 90144 | tf_op jit(solution)/shard_map/ppermute | solution.py:633
  9.3 3.4 %collective-permute-start.8 = (bf16[352,256]{1,0:T(8,128)(2,1)S(1)}, bf16[352,256]{1,0:T(8,128)(2,1)S(1)}, u32[]{:S(2)}, u32[]{:S(2)}) collective-permute-start(bf16[352,256]{1,0:T(8,128)(2,1)S(1)} %constant_dynamic-update-slice_fusion.refs_0_), channel_id=1, source_target_pairs={{0,4},{1,5},{2,6},{3,7},{4,0},{5,1},{6,2},{7,3},{8,12},{9,13},{10,... | collective-permute-start | bytes 540680 | tf_op jit(solution)/shard_map/ppermute | solution.py:620
  12.7 1.6 %collective-permute-start.9 = (bf16[352,256]{1,0:T(8,128)(2,1)S(1)}, bf16[352,256]{1,0:T(8,128)(2,1)S(1)}, u32[]{:S(2)}, u32[]{:S(2)}) collective-permute-start(bf16[352,256]{1,0:T(8,128)(2,1)S(1)} %constant_dynamic-update-slice_fusion.refs_0_), channel_id=1, source_target_pairs={{0,2},{1,3},{2,0},{3,1},{4,6},{5,7},{6,4},{7,5},{8,10},{9,11},{10,... | collective-permute-start | bytes 540680 | tf_op jit(solution)/shard_map/ppermute | solution.py:620
  14.3 2.2 %keys.1 = (bf16[4096,256]{1,0:T(8,128)(2,1)S(1)}, bf16[192,256]{1,0:T(8,128)(2,1)S(1)}, s32[192,1]{1,0:T(8,128)S(1)}, s32[8,256]{1,0:T(8,128)S(1)}, f32[8,128]{1,0:T(8,128)S(1)}) custom-call(s32[3]{0:T(128)S(1)} %pad_add_fusion.place_ref, s32[16,128]{1,0:T(8,128)S(1)} %bitcast.17, bf16[4096,256]{1,0:T(8,128)(2,1)S(1)} %copy-done.7, ...), custom_call_target="tpu_custom_call" | custom-call | flops 2000000000 | bytes 1048576 | tf_op jit(solution)/shard_map/keys/pallas_call | solution.py:304
  16.5 0.4 locate.1
  17.0 1.6 %collective-permute-start.12 = (bf16[512,256]{1,0:T(8,128)(2,1)S(1)}, bf16[512,256]{1,0:T(8,128)(2,1)S(1)}, u32[]{:S(2)}, u32[]{:S(2)}) collective-permute-start(bf16[512,256]{1,0:T(8,128)(2,1)S(1)} %after.5), channel_id=1, source_target_pairs={{0,16},{8,24},{16,0},{24,8},{1,17},{9,25},{17,1},{25,9},{2,18},{10... | collective-permute-start | bytes 786440 | tf_op jit(solution)/shard_map/ppermute | solution.py:644
  18.5 0.9 %collective-permute-done.8.refs_1_ = bf16[352,256]{1,0:T(8,128)(2,1)S(1)} collective-permute-done((bf16[352,256]{1,0:T(8,128)(2,1)S(1)}, bf16[352,256]{1,0:T(8,128)(2,1)S(1)}, u32[]{:S(2)}, u32[]{:S(2)}) %collective-permute-start.8) | collective-permute-done | bytes 180256 | tf_op jit(solution)/shard_map/ppermute | solution.py:620
  19.5 0.3 collective-permute-start.10
  19.8 0.9 %early.1.early_ref = bf16[1024,256]{1,0:T(8,128)(2,1)S(1)} custom-call(s32[1]{0:T(128)} %bitcast.4.place_ref, s32[8,256]{1,0:T(8,128)S(1)} %get-tuple-element.331.loc_ref.refs_1_, bf16[352,256]{1,0:T(8,128)(2,1)S(1)} %constant_dynamic-update-slice_fusion.refs_0_, bf16[352,256]{1,0:T(8,128)(2,1)S(1)} %collective-permute-done.8.refs_1_), custom_call_target="tpu_custom_call" | custom-call | flops 2000000000 | bytes 1048576 | tf_op jit(solution)/shard_map/early/pallas_call | solution.py:350
  20.7 4.3 %collective-permute-done.10.refs_3_ = bf16[352,256]{1,0:T(8,128)(2,1)S(1)} collective-permute-done((bf16[352,256]{1,0:T(8,128)(2,1)S(1)}, bf16[352,256]{1,0:T(8,128)(2,1)S(1)}, u32[]{:S(2)}, u32[]{:S(2)}) %collective-permute-start.10) | collective-permute-done | bytes 180256 | tf_op jit(solution)/shard_map/ppermute | solution.py:620
  25.0 1.0 %arrange.1 = (bf16[1024,256]{1,0:T(8,128)(2,1)S(1)}, bf16[256,256]{1,0:T(8,128)(2,1)S(1)}, bf16[256,256]{1,0:T(8,128)(2,1)S(1)}, bf16[256,256]{1,0:T(8,128)(2,1)...) custom-call(s32[1]{0:T(128)} %bitcast.4.place_ref, s32[8,256]{1,0:T(8,128)S(1)} %get-tuple-element.331.loc_ref.refs_1_, ...), custom_call_target="tpu_custom_call" | custom-call | flops 3000000000 | bytes 1048576 | tf_op jit(solution)/shard_map/arrange/pallas_call | solution.py:376
  26.0 0.1 collective-permute-start.14
  26.1 0.5 collective-permute-start.15
  26.6 0.1 collective-permute-start.16
  26.6 5.1 %first.1 = (f32[1024,128]{1,0:T(8,128)S(1)}, f32[256,256]{1,0:T(8,128)S(1)}, f32[256,256]{1,0:T(8,128)S(1)}, f32[256,256]{1,0:T(8,128)S(1)}, f32[256,256]{1,0:T(8,128)S(1)}) custom-call(bf16[1024,256]{1,0:T(8,128)(2,1)S(1)} %get-tuple-element.334.refs_1_.query_ref, bf16[4096,256]{1,0:T(8,128)(2,1)S(1)} %get-tuple-element.333.refs_0_.keys_ref, ...), custom_call_target="tpu_custom_call" | custom-call | flops 8589934592 | bytes 1048576 | tf_op jit(solution)/shard_map/first/pallas_call | solution.py:412
  31.8 3.5 %far.1 = (f32[8,256]{1,0:T(8,128)S(1)}, bf16[256,256]{1,0:T(8,128)(2,1)S(1)}, bf16[256,256]{1,0:T(8,128)(2,1)S(1)}, bf16[256,256]{1,0:T(8,128)(2,1)S(1)}, bf16[256,256]{1,0:T(8,128)(2,1)S(1)}) custom-call(s32[1]{0:T(128)} %bitcast.4.place_ref, s32[8,256]{1,0:T(8,128)S(1)} %get-tuple-element.330.refs_1_.loc_ref, ...), custom_call_target="tpu_custom_call" | custom-call | flops 2147483648 | bytes 1048576 | tf_op jit(solution)/shard_map/far/pallas_call | solution.py:457
  35.2 1.0 %collective-permute-start.17 = (f32[8,256]{1,0:T(8,128)S(1)}, f32[8,256]{1,0:T(8,128)S(1)}, u32[]{:S(2)}, u32[]{:S(2)}) collective-permute-start(f32[8,256]{1,0:T(8,128)S(1)} %get-tuple-element.340.note_ref.gate_ref), channel_id=1, source_target_pairs={{0,2},{1,3},{2,0},{3,1},{4,6},{5,7},{6,4},{7,5},{8,10},{9,11},{10,... | collective-permute-start | bytes 24584 | tf_op jit(solution)/shard_map/ppermute | solution.py:620
  36.3 2.7 %collective-permute-start.18 = (f32[8,256]{1,0:T(8,128)S(1)}, f32[8,256]{1,0:T(8,128)S(1)}, u32[]{:S(2)}, u32[]{:S(2)}) collective-permute-start(f32[8,256]{1,0:T(8,128)S(1)} %get-tuple-element.340.note_ref.gate_ref), channel_id=1, source_target_pairs={{0,4},{1,5},{2,6},{3,7},{4,0},{5,1},{6,2},{7,3},{8,12},{9,13},{10,... | collective-permute-start | bytes 24584 | tf_op jit(solution)/shard_map/ppermute | solution.py:620
  39.0 0.7 %collective-permute-start.19 = (f32[8,256]{1,0:T(8,128)S(1)}, f32[8,256]{1,0:T(8,128)S(1)}, u32[]{:S(2)}, u32[]{:S(2)}) collective-permute-start(f32[8,256]{1,0:T(8,128)S(1)} %get-tuple-element.340.note_ref.gate_ref), channel_id=1, source_target_pairs={{0,6},{1,7},{2,4},{3,5},{4,2},{5,3},{6,0},{7,1},{8,14},{9,15},{10,... | collective-permute-start | bytes 24584 | tf_op jit(solution)/shard_map/ppermute | solution.py:620
  39.7 1.4 %last.5.pushed_ref = f32[256,256]{1,0:T(8,128)S(1)} custom-call(bf16[256,256]{1,0:T(8,128)(2,1)S(1)} %get-tuple-element.351.query_ref, f32[256,256]{1,0:T(8,128)S(1)} %get-tuple-element.352.pushed_in, f32[8,256]{1,0:T(8,128)S(1)} %get-tuple-element.340.note_ref.gate_ref, bf16[512,256]{1,0:T(8,128)(2,1)S(1)} %after.4.refs_0_, ...), custom_call_target="tpu_custom_call" | custom-call | flops 1073741824 | bytes 1048576 | tf_op jit(solution)/shard_map/last/pallas_call | solution.py:482
  41.1 1.4 %last.6.pushed_ref = f32[256,256]{1,0:T(8,128)S(1)} custom-call(bf16[256,256]{1,0:T(8,128)(2,1)S(1)} %get-tuple-element.354.query_ref, f32[256,256]{1,0:T(8,128)S(1)} %get-tuple-element.355.pushed_in, f32[8,256]{1,0:T(8,128)S(1)} %get-tuple-element.340.note_ref.gate_ref, bf16[512,256]{1,0:T(8,128)(2,1)S(1)} %after.4.refs_0_, ...), custom_call_target="tpu_custom_call" | custom-call | flops 1073741824 | bytes 1048576 | tf_op jit(solution)/shard_map/last/pallas_call | solution.py:482
  42.6 1.4 %last.7.pushed_ref = f32[256,256]{1,0:T(8,128)S(1)} custom-call(bf16[256,256]{1,0:T(8,128)(2,1)S(1)} %get-tuple-element.357.query_ref, f32[256,256]{1,0:T(8,128)S(1)} %get-tuple-element.358.pushed_in, f32[8,256]{1,0:T(8,128)S(1)} %get-tuple-element.340.note_ref.gate_ref, bf16[512,256]{1,0:T(8,128)(2,1)S(1)} %after.4.refs_0_, ...), custom_call_target="tpu_custom_call" | custom-call | flops 1073741824 | bytes 1048576 | tf_op jit(solution)/shard_map/last/pallas_call | solution.py:482
  44.0 0.4 collective-permute-done.19.refs_2_
  44.5 0.1 settle.1
  44.6 0.1 collective-permute-start.20
  44.7 0.3 code.3.refs_0_
  45.0 0.7 %collective-permute-start.24 = (s16[272,256]{1,0:T(8,128)(2,1)S(1)}, s16[272,256]{1,0:T(8,128)(2,1)S(1)}, u32[]{:S(2)}, u32[]{:S(2)}) collective-permute-start(s16[272,256]{1,0:T(8,128)(2,1)S(1)} %code.3.refs_0_), channel_id=1, source_target_pairs={{0,4},{1,5},{2,6},{3,7},{4,0},{5,1},{6,2},{7,3},{8,12},{9,13},{10,... | collective-permute-start | bytes 417800 | tf_op jit(solution)/shard_map/ppermute | solution.py:620
  45.8 0.1 collective-permute-done.20
  45.8 0.3 code.4.refs_0_
  46.2 2.6 %collective-permute-start.23 = (s16[272,256]{1,0:T(8,128)(2,1)S(1)}, s16[272,256]{1,0:T(8,128)(2,1)S(1)}, u32[]{:S(2)}, u32[]{:S(2)}) collective-permute-start(s16[272,256]{1,0:T(8,128)(2,1)S(1)} %code.4.refs_0_), channel_id=1, source_target_pairs={{0,2},{1,3},{2,0},{3,1},{4,6},{5,7},{6,4},{7,5},{8,10},{9,11},{10,... | collective-permute-start | bytes 417800 | tf_op jit(solution)/shard_map/ppermute | solution.py:620
  48.8 0.3 code.5
  49.1 1.2 %collective-permute-start.25 = (s16[272,256]{1,0:T(8,128)(2,1)S(1)}, s16[272,256]{1,0:T(8,128)(2,1)S(1)}, u32[]{:S(2)}, u32[]{:S(2)}) collective-permute-start(s16[272,256]{1,0:T(8,128)(2,1)S(1)} %code.5), channel_id=1, source_target_pairs={{0,6},{1,7},{2,4},{3,5},{4,2},{5,3},{6,0},{7,1},{8,14},{9,15},{10,... | collective-permute-start | bytes 417800 | tf_op jit(solution)/shard_map/ppermute | solution.py:620
  50.3 1.5 %collective-permute-start.21 = (f32[8,128]{1,0:T(8,128)S(1)}, f32[8,128]{1,0:T(8,128)S(1)}, u32[]{:S(2)}, u32[]{:S(2)}) collective-permute-start(f32[8,128]{1,0:T(8,128)S(1)} %add.155.refs_1_), channel_id=1, source_target_pairs={{0,1},{1,0},{2,3},{3,2},{4,5},{5,4},{6,7},{7,6},{8,9},{9,8},{10,11... | collective-permute-start | bytes 12296 | tf_op jit(solution)/shard_map/ppermute | solution.py:673
  51.8 2.1 %collective-permute-done.21 = f32[8,128]{1,0:T(8,128)S(1)} collective-permute-done((f32[8,128]{1,0:T(8,128)S(1)}, f32[8,128]{1,0:T(8,128)S(1)}, u32[]{:S(2)}, u32[]{:S(2)}) %collective-permute-start.21) | collective-permute-done | bytes 4128 | tf_op jit(solution)/shard_map/ppermute | solution.py:673
  53.9 1.5 %collective-permute-start.22 = (f32[8,128]{1,0:T(8,128)S(1)}, f32[8,128]{1,0:T(8,128)S(1)}, u32[]{:S(2)}, u32[]{:S(2)}) collective-permute-start(f32[8,128]{1,0:T(8,128)S(1)} %add.156.word_ref.gate_ref), channel_id=1, source_target_pairs={{0,16},{8,24},{16,0},{24,8},{1,17},{9,25},{17,1},{25,9},{2,18},{10... | collective-permute-start | bytes 12296 | tf_op jit(solution)/shard_map/ppermute | solution.py:673
  55.4 1.4 %last.4 = f32[256,256]{1,0:T(8,128)S(1)} custom-call(bf16[256,256]{1,0:T(8,128)(2,1)S(1)} %get-tuple-element.348.query_ref, f32[256,256]{1,0:T(8,128)S(1)} %get-tuple-element.349.pushed_in, f32[8,128]{1,0:T(8,128)S(1)} %add.156.word_ref.gate_ref, bf16[512,256]{1,0:T(8,128)(2,1)S(1)} %after.4.refs_0_, bf16[512,256]{1,0:T(8,128)(2,1)S(1)} %collective-permute-done.14.refs_1_, ...), custom_call_target="tpu_custom_call" | custom-call | flops 1073741824 | bytes 1048576 | tf_op jit(solution)/shard_map/last/pallas_call | solution.py:482
  56.9 0.6 %collective-permute-done.22.came_ref = f32[8,128]{1,0:T(8,128)S(1)} collective-permute-done((f32[8,128]{1,0:T(8,128)S(1)}, f32[8,128]{1,0:T(8,128)S(1)}, u32[]{:S(2)}, u32[]{:S(2)}) %collective-permute-start.22) | collective-permute-done | bytes 4128 | tf_op jit(solution)/shard_map/ppermute | solution.py:673
  57.5 0.6 %mean.1 = (f32[1,1]{1,0:T(1,128)}, s32[1,1]{1,0:T(1,128)}) custom-call(f32[8,128]{1,0:T(8,128)S(1)} %add.156.word_ref.gate_ref, f32[8,128]{1,0:T(8,128)S(1)} %collective-permute-done.22.came_ref), custom_call_target="tpu_custom_call" | custom-call | flops 100000000 | bytes 1048576 | tf_op jit(solution)/shard_map/mean/pallas_call | solution.py:567
  58.9 0.5 conditional.1
  58.9 0.5 finish.1
  59.4 0.0 copy-start.14
  59.4 0.7 %copy-done.14 = f32[256,256]{1,0:T(8,128)} copy-done((f32[256,256]{1,0:T(8,128)}, f32[256,256]{1,0:T(8,128)S(1)}, u32[]{:S(2)}) %copy-start.14) | copy-done | bytes 262168
  (31 shorter events, 0.1 us)
Async XLA Ops:
  0.8 13.5 %copy-start.7 = (bf16[4096,256]{1,0:T(8,128)(2,1)S(1)}, bf16[4096,256]{1,0:T(8,128)(2,1)}, u32[]{:S(2)}) copy-start(bf16[4096,256]{1,0:T(8,128)(2,1)} %bank_ref.3) | copy-start | bytes 6291460
  0.8 13.5 %copy-start.12 = (s32[2048]{0:T(1024)S(1)}, s32[2048]{0:T(1024)}, u32[]{:S(2)}) copy-start(s32[2048]{0:T(1024)} %param.24) | copy-start | bytes 24580
  3.1 6.1 %collective-permute-start.7 = (bf16[176,256]{1,0:T(8,128)(2,1)S(1)}, bf16[176,256]{1,0:T(8,128)(2,1)S(1)}, u32[]{:S(2)}, u32[]{:S(2)}) collective-permute-start(bf16[176,256]{1,0:T(8,128)(2,1)S(1)} %get-tuple-element.329), channel_id=1, source_target_pairs={{0,1},{1,0},{2,3},{3,2},{4,5},{5,4},{6,7},{7,6},{8,9},{9,8},{10,11... | collective-permute-start | bytes 270344 | tf_op jit(solution)/shard_map/ppermute | solution.py:633
  6.1 10.8 %collective-permute-start.11 = (bf16[512,256]{1,0:T(8,128)(2,1)S(1)}, bf16[512,256]{1,0:T(8,128)(2,1)S(1)}, u32[]{:S(2)}, u32[]{:S(2)}) collective-permute-start(bf16[512,256]{1,0:T(8,128)(2,1)S(1)} %get-tuple-element.335), channel_id=1, source_target_pairs={{0,1},{1,0},{2,3},{3,2},{4,5},{5,4},{6,7},{7,6},{8,9},{9,8},{10,11... | collective-permute-start | bytes 786440 | tf_op jit(solution)/shard_map/ppermute | solution.py:634
  6.2 20.3 %collective-permute-start.13 = (bf16[1024,256]{1,0:T(8,128)(2,1)S(1)}, bf16[1024,256]{1,0:T(8,128)(2,1)S(1)}, u32[]{:S(2)}, u32[]{:S(2)}) collective-permute-start(bf16[1024,256]{1,0:T(8,128)(2,1)S(1)} %get-tuple-element.336), channel_id=1, source_target_pairs={{0,1},{1,0},{2,3},{3,2},{4,5},{5,4},{6,7},{7,6},{8,9},{9,8},{10,11... | collective-permute-start | bytes 1572872 | tf_op jit(solution)/shard_map/ppermute | solution.py:635
  9.3 10.2 %collective-permute-start.8 = (bf16[352,256]{1,0:T(8,128)(2,1)S(1)}, bf16[352,256]{1,0:T(8,128)(2,1)S(1)}, u32[]{:S(2)}, u32[]{:S(2)}) collective-permute-start(bf16[352,256]{1,0:T(8,128)(2,1)S(1)} %constant_dynamic-update-slice_fusion.refs_0_), channel_id=1, source_target_pairs={{0,4},{1,5},{2,6},{3,7},{4,0},{5,1},{6,2},{7,3},{8,12},{9,13},{10,... | collective-permute-start | bytes 540680 | tf_op jit(solution)/shard_map/ppermute | solution.py:620
  12.7 8.0 %collective-permute-start.9 = (bf16[352,256]{1,0:T(8,128)(2,1)S(1)}, bf16[352,256]{1,0:T(8,128)(2,1)S(1)}, u32[]{:S(2)}, u32[]{:S(2)}) collective-permute-start(bf16[352,256]{1,0:T(8,128)(2,1)S(1)} %constant_dynamic-update-slice_fusion.refs_0_), channel_id=1, source_target_pairs={{0,2},{1,3},{2,0},{3,1},{4,6},{5,7},{6,4},{7,5},{8,10},{9,11},{10,... | collective-permute-start | bytes 540680 | tf_op jit(solution)/shard_map/ppermute | solution.py:620
  14.3 2.2 %copy-start.13 = (s32[16,128]{1,0:T(8,128)S(1)}, s32[16,128]{1,0:T(8,128)}, u32[]{:S(2)}) copy-start(s32[16,128]{1,0:T(8,128)} %pos_ref.3) | copy-start | bytes 24580
  17.0 9.1 %collective-permute-start.12 = (bf16[512,256]{1,0:T(8,128)(2,1)S(1)}, bf16[512,256]{1,0:T(8,128)(2,1)S(1)}, u32[]{:S(2)}, u32[]{:S(2)}) collective-permute-start(bf16[512,256]{1,0:T(8,128)(2,1)S(1)} %after.5), channel_id=1, source_target_pairs={{0,16},{8,24},{16,0},{24,8},{1,17},{9,25},{17,1},{25,9},{2,18},{10... | collective-permute-start | bytes 786440 | tf_op jit(solution)/shard_map/ppermute | solution.py:644
  19.5 5.5 %collective-permute-start.10 = (bf16[352,256]{1,0:T(8,128)(2,1)S(1)}, bf16[352,256]{1,0:T(8,128)(2,1)S(1)}, u32[]{:S(2)}, u32[]{:S(2)}) collective-permute-start(bf16[352,256]{1,0:T(8,128)(2,1)S(1)} %collective-permute-done.8.refs_1_), channel_id=1, source_target_pairs={{0,2},{1,3},{2,0},{3,1},{4,6},{5,7},{6,4},{7,5},{8,10},{9,11},{10,... | collective-permute-start | bytes 540680 | tf_op jit(solution)/shard_map/ppermute | solution.py:620
  26.0 5.8 %collective-permute-start.14 = (bf16[512,256]{1,0:T(8,128)(2,1)S(1)}, bf16[512,256]{1,0:T(8,128)(2,1)S(1)}, u32[]{:S(2)}, u32[]{:S(2)}) collective-permute-start(bf16[512,256]{1,0:T(8,128)(2,1)S(1)} %after.4.refs_0_), channel_id=1, source_target_pairs={{0,8},{8,0},{16,24},{24,16},{1,9},{9,1},{17,25},{25,17},{2,10},{10... | collective-permute-start | bytes 786440 | tf_op jit(solution)/shard_map/ppermute | solution.py:660
  26.1 5.7 %collective-permute-start.15 = (bf16[512,256]{1,0:T(8,128)(2,1)S(1)}, bf16[512,256]{1,0:T(8,128)(2,1)S(1)}, u32[]{:S(2)}, u32[]{:S(2)}) collective-permute-start(bf16[512,256]{1,0:T(8,128)(2,1)S(1)} %after.6.refs_1_.refs_2_), channel_id=1, source_target_pairs={{0,8},{8,0},{16,24},{24,16},{1,9},{9,1},{17,25},{25,17},{2,10},{10... | collective-permute-start | bytes 786440 | tf_op jit(solution)/shard_map/ppermute | solution.py:660
  26.6 5.2 %collective-permute-start.16 = (bf16[1024,256]{1,0:T(8,128)(2,1)S(1)}, bf16[1024,256]{1,0:T(8,128)(2,1)S(1)}, u32[]{:S(2)}, u32[]{:S(2)}) collective-permute-start(bf16[1024,256]{1,0:T(8,128)(2,1)S(1)} %after.7.refs_2_.refs_4_), channel_id=1, source_target_pairs={{0,8},{8,0},{16,24},{24,16},{1,9},{9,1},{17,25},{25,17},{2,10},{10... | collective-permute-start | bytes 1572872 | tf_op jit(solution)/shard_map/ppermute | solution.py:660
  35.2 8.8 %collective-permute-start.17 = (f32[8,256]{1,0:T(8,128)S(1)}, f32[8,256]{1,0:T(8,128)S(1)}, u32[]{:S(2)}, u32[]{:S(2)}) collective-permute-start(f32[8,256]{1,0:T(8,128)S(1)} %get-tuple-element.340.note_ref.gate_ref), channel_id=1, source_target_pairs={{0,2},{1,3},{2,0},{3,1},{4,6},{5,7},{6,4},{7,5},{8,10},{9,11},{10,... | collective-permute-start | bytes 24584 | tf_op jit(solution)/shard_map/ppermute | solution.py:620
  36.3 7.8 %collective-permute-start.18 = (f32[8,256]{1,0:T(8,128)S(1)}, f32[8,256]{1,0:T(8,128)S(1)}, u32[]{:S(2)}, u32[]{:S(2)}) collective-permute-start(f32[8,256]{1,0:T(8,128)S(1)} %get-tuple-element.340.note_ref.gate_ref), channel_id=1, source_target_pairs={{0,4},{1,5},{2,6},{3,7},{4,0},{5,1},{6,2},{7,3},{8,12},{9,13},{10,... | collective-permute-start | bytes 24584 | tf_op jit(solution)/shard_map/ppermute | solution.py:620
  39.0 5.4 %collective-permute-start.19 = (f32[8,256]{1,0:T(8,128)S(1)}, f32[8,256]{1,0:T(8,128)S(1)}, u32[]{:S(2)}, u32[]{:S(2)}) collective-permute-start(f32[8,256]{1,0:T(8,128)S(1)} %get-tuple-element.340.note_ref.gate_ref), channel_id=1, source_target_pairs={{0,6},{1,7},{2,4},{3,5},{4,2},{5,3},{6,0},{7,1},{8,14},{9,15},{10,... | collective-permute-start | bytes 24584 | tf_op jit(solution)/shard_map/ppermute | solution.py:620
  44.6 1.2 %collective-permute-start.20 = (f32[8,128]{1,0:T(8,128)S(1)}, f32[8,128]{1,0:T(8,128)S(1)}, u32[]{:S(2)}, u32[]{:S(2)}) collective-permute-start(f32[8,128]{1,0:T(8,128)S(1)} %get-tuple-element.343), channel_id=1, source_target_pairs={{0,8},{8,0},{16,24},{24,16},{1,9},{9,1},{17,25},{25,17},{2,10},{10... | collective-permute-start | bytes 12296 | tf_op jit(solution)/shard_map/ppermute | solution.py:673
  45.0 13.8 %collective-permute-start.24 = (s16[272,256]{1,0:T(8,128)(2,1)S(1)}, s16[272,256]{1,0:T(8,128)(2,1)S(1)}, u32[]{:S(2)}, u32[]{:S(2)}) collective-permute-start(s16[272,256]{1,0:T(8,128)(2,1)S(1)} %code.3.refs_0_), channel_id=1, source_target_pairs={{0,4},{1,5},{2,6},{3,7},{4,0},{5,1},{6,2},{7,3},{8,12},{9,13},{10,... | collective-permute-start | bytes 417800 | tf_op jit(solution)/shard_map/ppermute | solution.py:620
  46.2 12.7 %collective-permute-start.23 = (s16[272,256]{1,0:T(8,128)(2,1)S(1)}, s16[272,256]{1,0:T(8,128)(2,1)S(1)}, u32[]{:S(2)}, u32[]{:S(2)}) collective-permute-start(s16[272,256]{1,0:T(8,128)(2,1)S(1)} %code.4.refs_0_), channel_id=1, source_target_pairs={{0,2},{1,3},{2,0},{3,1},{4,6},{5,7},{6,4},{7,5},{8,10},{9,11},{10,... | collective-permute-start | bytes 417800 | tf_op jit(solution)/shard_map/ppermute | solution.py:620
  49.1 9.7 %collective-permute-start.25 = (s16[272,256]{1,0:T(8,128)(2,1)S(1)}, s16[272,256]{1,0:T(8,128)(2,1)S(1)}, u32[]{:S(2)}, u32[]{:S(2)}) collective-permute-start(s16[272,256]{1,0:T(8,128)(2,1)S(1)} %code.5), channel_id=1, source_target_pairs={{0,6},{1,7},{2,4},{3,5},{4,2},{5,3},{6,0},{7,1},{8,14},{9,15},{10,... | collective-permute-start | bytes 417800 | tf_op jit(solution)/shard_map/ppermute | solution.py:620
  50.3 3.6 %collective-permute-start.21 = (f32[8,128]{1,0:T(8,128)S(1)}, f32[8,128]{1,0:T(8,128)S(1)}, u32[]{:S(2)}, u32[]{:S(2)}) collective-permute-start(f32[8,128]{1,0:T(8,128)S(1)} %add.155.refs_1_), channel_id=1, source_target_pairs={{0,1},{1,0},{2,3},{3,2},{4,5},{5,4},{6,7},{7,6},{8,9},{9,8},{10,11... | collective-permute-start | bytes 12296 | tf_op jit(solution)/shard_map/ppermute | solution.py:673
  53.9 3.6 %collective-permute-start.22 = (f32[8,128]{1,0:T(8,128)S(1)}, f32[8,128]{1,0:T(8,128)S(1)}, u32[]{:S(2)}, u32[]{:S(2)}) collective-permute-start(f32[8,128]{1,0:T(8,128)S(1)} %add.156.word_ref.gate_ref), channel_id=1, source_target_pairs={{0,16},{8,24},{16,0},{24,8},{1,17},{9,25},{17,1},{25,9},{2,18},{10... | collective-permute-start | bytes 12296 | tf_op jit(solution)/shard_map/ppermute | solution.py:673
  55.4 3.4 %copy-start.11 = (bf16[16,64,256]{2,1,0:T(8,128)(2,1)S(1)}, bf16[16,64,256]{2,1,0:T(8,128)(2,1)}, u32[]{:S(2)}) copy-start(bf16[16,64,256]{2,1,0:T(8,128)(2,1)} %feat_ref.1) | copy-start | bytes 1572868
  59.4 0.7 %copy-start.14 = (f32[256,256]{1,0:T(8,128)}, f32[256,256]{1,0:T(8,128)S(1)}, u32[]{:S(2)}) copy-start(f32[256,256]{1,0:T(8,128)S(1)} %get-tuple-element.327) | copy-start | bytes 786436
  59.4 0.7 %copy-start.15 = (f32[256]{0:T(256)}, f32[256]{0:T(256)S(1)}, u32[]{:S(2)}) copy-start(f32[256]{0:T(256)S(1)} %get-tuple-element.361) | copy-start | bytes 3076
